TPU v7x, 32 devices: a whole 2x2x4 slice. The times are simulated.
32 devices in a mesh: item: 16 (over z, y, x), pipe: 2 (over core).
Axes of the slice: x: 2, y: 2, z: 4, core: 2. Of those that a mesh axis runs over, the one named last changes fastest.
Arguments:
- waveform: bfloat16 [512, 4096], P('item'), may hold values from -6 to 6
- lengths: int32 [512], P('item'), may hold values from 512 to 4096, as said below
- code_ids: int32 [512, 2048], P('item'), may hold values from 0 to 2047
- conv_w: float32 [2, 64, 192], P('pipe'), may hold values from -0.4375 to 0.4375
- point_w: float32 [2, 2, 64, 64], P('pipe'), may hold values from -0.75 to 0.75
- edge_w: float32 [2, 64, 4], P('pipe')
- codebook: float32 [2048, 64], P('pipe'), may hold values from -6 to 6
- conv_mom: float32 [2, 64, 192], P('pipe'), may hold values from -0.01953125 to 0.01953125
- point_mom: float32 [2, 2, 64, 64], P('pipe'), may hold values from -0.01953125 to 0.01953125
- edge_mom: float32 [2, 64, 4], P('pipe'), may hold values from -0.0390625 to 0.0390625
- code_mom: float32 [2048, 64], P('pipe'), may hold values from -1.5258789e-05 to 1.5258789e-05
- conv_avg: float32 [2, 64, 192], P('pipe'), may hold values from -0.4375 to 0.4375
- point_avg: float32 [2, 2, 64, 64], P('pipe'), may hold values from -0.75 to 0.75
- edge_avg: float32 [2, 64, 4], P('pipe')
- code_avg: float32 [2048, 64], P('pipe'), may hold values from -6 to 6
- rate_net: float32 [1], replicated, may hold values from 72.40774 to 144.81548
- rate_code: float32 [1], replicated, may hold values from 185363.8 to 370727.6
Outputs:
- loss_value: float32 [], replicated
- conv_new: float32 [2, 64, 192], P('pipe')
- conv_mom_new: float32 [2, 64, 192], P('pipe')
- conv_avg_new: float32 [2, 64, 192], P('pipe')
- conv_copy: bfloat16 [2, 64, 192], P('pipe')
- point_new: float32 [2, 2, 64, 64], P('pipe')
- point_mom_new: float32 [2, 2, 64, 64], P('pipe')
- point_avg_new: float32 [2, 2, 64, 64], P('pipe')
- point_copy: bfloat16 [2, 2, 64, 64], P('pipe')
- edge_new: float32 [2, 64, 4], P('pipe')
- edge_mom_new: float32 [2, 64, 4], P('pipe')
- edge_avg_new: float32 [2, 64, 4], P('pipe')
- edge_copy: bfloat16 [2, 64, 4], P('pipe')
- code_new: float32 [2048, 64], P('pipe')
- code_mom_new: float32 [2048, 64], P('pipe')
- code_avg_new: float32 [2048, 64], P('pipe')
- code_copy: bfloat16 [2048, 64], P('pipe')
Inputs may be any that keep to these rules, and one draw needn't show every extreme that they name: `lengths`: valid frames of a clip, counted from its first frame. `code_ids`: a code number for every latent frame, padded ones too.
All inputs are finite; a program needn't handle non-finite values.
Results may differ from a plain program's by a relative error of at most 0.0087.
Values may be sent and summed in bfloat16 or wider, within the bound.
A program may use at most 512 MiB of HBM per device.

v0:
```python
import jax
import jax.numpy as jnp
from jax import lax
from jax.sharding import PartitionSpec as P

DILATION_SIZE = 3
MICRO = 2


COMMIT = 0.02
MOMENTUM = 0.9
AVERAGE = 0.99


def passed_along(block, axis, distance):
    devices = range(lax.axis_size(axis))
    route = [(i - distance, i) for i in devices if i - distance in devices]
    return lax.ppermute(block, axis, route)


def shift_along(values, offset):
    if offset > 0:
        pad_zero = jnp.zeros(values.shape[:-1] + (offset,), values.dtype)
        return jnp.concatenate([values[..., offset:], pad_zero], -1)
    pad_zero = jnp.zeros(values.shape[:-1] + (-offset,), values.dtype)
    return jnp.concatenate([pad_zero, values[..., :offset]], -1)


def spread_kernel_taps(values, reach):
    return jnp.concatenate([shift_along(values, -reach), values, shift_along(values, reach)], 1)


def folded_kernel_taps(grads, reach):
    width = grads.shape[1] // 3
    return (
        shift_along(grads[:, :width], reach)
        + grads[:, width : 2 * width]
        + shift_along(grads[:, 2 * width :], -reach)
    )


def input_taps(signal):
    phases = signal.reshape(signal.shape[0], -1, 2)
    even_part = phases[..., 0]
    odd_part = phases[..., 1]
    return jnp.stack([shift_along(odd_part, -1), even_part, odd_part, shift_along(even_part, 1)], 1)


def mixing(weight, values):
    return jnp.einsum("fw,ywi->yfi", weight, values, preferred_element_type=jnp.float32)


def weight_grad(grads, values):
    return jnp.einsum("bot,bct->oc", grads, values, preferred_element_type=jnp.float32)


def input_gradient_rows(weight, grads):
    return jnp.einsum("oc,bot->bct", weight, grads, preferred_element_type=jnp.float32)


def block_forward(entry_val, convolution_half_weight, point_bf):
    activation_unit = jax.nn.relu(entry_val).astype(jnp.bfloat16)
    spread_signal = spread_kernel_taps(activation_unit, DILATION_SIZE)
    inner_output_rows = mixing(convolution_half_weight, spread_signal)
    act_p = jax.nn.relu(inner_output_rows).astype(jnp.bfloat16)
    return (
        entry_val + mixing(point_bf, act_p),
        (entry_val, spread_signal, inner_output_rows, act_p),
    )


def block_backward(d_result, kept_vals, convolution_half_weight, point_bf):
    entry_val, spread_signal, inner_output_rows, act_p = kept_vals
    d_branch = d_result.astype(jnp.bfloat16)
    d_point = weight_grad(d_branch, act_p)
    inner_gradient = jnp.where(
        inner_output_rows > 0, input_gradient_rows(point_bf, d_branch), 0.0
    ).astype(jnp.bfloat16)
    d_conv = weight_grad(inner_gradient, spread_signal)
    activation_gradient = folded_kernel_taps(
        input_gradient_rows(convolution_half_weight, inner_gradient), DILATION_SIZE
    )
    d_entry = (d_result + jnp.where(entry_val > 0, activation_gradient, 0.0)).astype(jnp.bfloat16)
    return (d_entry, d_conv, d_point)


def encode(signal, convolution_half_weight, point_bf, edge_bf):
    strips = input_taps(signal)
    hidden = jnp.einsum("ck,bkt->bct", edge_bf, strips, preferred_element_type=jnp.float32)
    result, kept_vals = block_forward(hidden, convolution_half_weight, point_bf[0])
    resid_bf = result.astype(jnp.bfloat16)
    latent = mixing(point_bf[1], resid_bf).astype(jnp.bfloat16)
    return (latent, (strips, kept_vals, resid_bf))


def encode_back(d_latent, stash_all, convolution_half_weight, point_bf):
    strips, kept_vals, resid_bf = stash_all
    d_out = weight_grad(d_latent, resid_bf)
    d_result = input_gradient_rows(point_bf[1], d_latent)
    d_hidden, d_conv, d_res = block_backward(
        d_result, kept_vals, convolution_half_weight, point_bf[0]
    )
    d_edge = jnp.einsum("bct,bkt->ck", d_hidden, strips, preferred_element_type=jnp.float32)
    return (d_conv, jnp.stack([d_res, d_out]), d_edge)


def decode_step(
    latent,
    chosen,
    signal,
    frame_mask,
    lat_valid,
    code_rows,
    convolution_half_weight,
    point_bf,
    edge_bf,
    table_rows,
):
    dec_in = mixing(point_bf[0], chosen)
    result, kept_vals = block_forward(dec_in, convolution_half_weight, point_bf[1])
    resid_bf = result.astype(jnp.bfloat16)
    outs_four = jnp.einsum("ck,bct->bkt", edge_bf, resid_bf, preferred_element_type=jnp.float32)
    even_out = outs_four[:, 1] + shift_along(outs_four[:, 3], -1)
    odd_out = outs_four[:, 2] + shift_along(outs_four[:, 0], 1)
    rebuilt = jnp.stack([even_out, odd_out], -1).reshape(signal.shape)
    error = jnp.where(frame_mask, rebuilt - signal.astype(jnp.float32), 0.0)
    gap = jnp.where(
        lat_valid[:, None, :], latent.astype(jnp.float32) - chosen.astype(jnp.float32), 0.0
    )
    part_loss = jnp.sum(error * error) + COMMIT * jnp.sum(gap * gap)
    d_outs = input_taps(2.0 * error).astype(jnp.bfloat16)
    d_edge = jnp.einsum("bkt,bct->ck", d_outs, resid_bf, preferred_element_type=jnp.float32)
    d_result = jnp.einsum("ck,bkt->bct", edge_bf, d_outs, preferred_element_type=jnp.float32)
    d_dec_in, d_conv, d_res = block_backward(
        d_result, kept_vals, convolution_half_weight, point_bf[1]
    )
    d_in_proj = weight_grad(d_dec_in, chosen)
    d_latent = (input_gradient_rows(point_bf[0], d_dec_in) + 2.0 * COMMIT * gap).astype(
        jnp.bfloat16
    )
    code_terms = jnp.swapaxes(-2.0 * COMMIT * gap, 1, 2).reshape(-1, gap.shape[1])
    d_table = jax.ops.segment_sum(code_terms, code_rows.reshape(-1), num_segments=table_rows)
    return (d_latent, (d_conv, jnp.stack([d_in_proj, d_res]), d_edge), d_table, part_loss)


def nesterov(weight, grad, moment, average, rate):
    moment_new = MOMENTUM * moment + grad
    weight_new = weight - rate * (grad + MOMENTUM * moment_new)
    average_new = AVERAGE * average + (1.0 - AVERAGE) * weight_new
    return (weight_new, moment_new, average_new, weight_new.astype(jnp.bfloat16))


def per_device(
    waveform,
    lengths,
    code_ids,
    conv_w,
    point_w,
    edge_w,
    codebook,
    conv_mom,
    point_mom,
    edge_mom,
    code_mom,
    conv_avg,
    point_avg,
    edge_avg,
    code_avg,
    rate_net,
    rate_code,
):
    pipe_rank = lax.axis_index("pipe")
    on_first = pipe_rank == 0
    table = lax.all_gather(codebook.astype(jnp.bfloat16), "pipe", axis=0, tiled=True)
    table_rows = table.shape[0]
    frames = waveform.shape[1]
    half_len = frames // 2
    width = conv_w.shape[1]
    per_micro = waveform.shape[0] // MICRO
    frame_pos = jnp.arange(frames)
    lat_pos = jnp.arange(half_len)
    local_count = jnp.sum(lengths).astype(jnp.float32)
    count_all = lax.psum(local_count, "item")
    empty_grads = (
        jnp.zeros((width, 3 * width), jnp.float32),
        jnp.zeros((2, width, width), jnp.float32),
        jnp.zeros((width, 4), jnp.float32),
    )
    acc_table = jnp.zeros((table_rows, width), jnp.float32)
    acc_loss = jnp.zeros((), jnp.float32)
    convolution_half_weight = conv_w[0].astype(jnp.bfloat16)
    point_bf = point_w[0].astype(jnp.bfloat16)
    edge_bf = edge_w[0].astype(jnp.bfloat16)
    zeros_f = jnp.zeros((per_micro, width, half_len), jnp.float32)
    zeros_b = zeros_f.astype(jnp.bfloat16)
    acc_grads = empty_grads
    for micro_idx in range(MICRO):
        lower = micro_idx * per_micro
        wave_rows = waveform[lower : lower + per_micro]
        len_rows = lengths[lower : lower + per_micro]
        code_rows = code_ids[lower : lower + per_micro]
        frame_mask = frame_pos[None, :] < len_rows[:, None]
        lat_valid = 2 * lat_pos[None, :] < len_rows[:, None]
        signal_in = jnp.where(frame_mask, wave_rows, jnp.zeros_like(wave_rows))

        def run_encode():
            return encode(signal_in, convolution_half_weight, point_bf, edge_bf)

        def skip_encode():
            strips = jnp.zeros((per_micro, 4, half_len), jnp.bfloat16)
            spread_zero = jnp.zeros((per_micro, 3 * width, half_len), jnp.bfloat16)
            return (zeros_b, (strips, (zeros_f, spread_zero, zeros_f, zeros_b), zeros_b))

        latent, stash_all = lax.cond(on_first, run_encode, skip_encode)
        received = passed_along(latent, "pipe", 1)

        def run_decode():
            chosen = jnp.swapaxes(jnp.take(table, code_rows, axis=0), 1, 2)
            return decode_step(
                received,
                chosen,
                wave_rows,
                frame_mask,
                lat_valid,
                code_rows,
                convolution_half_weight,
                point_bf,
                edge_bf,
                table_rows,
            )

        def skip_decode():
            return (
                zeros_b,
                empty_grads,
                jnp.zeros((table_rows, width), jnp.float32),
                jnp.zeros((), jnp.float32),
            )

        d_latent, dec_grads, d_table, part_loss = lax.cond(on_first, skip_decode, run_decode)
        returned = passed_along(d_latent, "pipe", -1)

        def run_back():
            return encode_back(returned, stash_all, convolution_half_weight, point_bf)

        def skip_back():
            return empty_grads

        enc_grads = lax.cond(on_first, run_back, skip_back)
        acc_grads = tuple((a + b + c for a, b, c in zip(acc_grads, dec_grads, enc_grads)))
        acc_table = acc_table + d_table
        acc_loss = acc_loss + part_loss
    summed = lax.psum((acc_grads[0], acc_grads[1], acc_grads[2], acc_table), "item")
    code_sum = lax.psum_scatter(summed[3], "pipe", scatter_dimension=0, tiled=True)
    own_grads = (summed[0][None], summed[1][None], summed[2][None])
    loss_sum = lax.psum(acc_loss, ("item", "pipe"))
    conv_out = nesterov(conv_w, own_grads[0] / count_all, conv_mom, conv_avg, rate_net[0])
    point_out = nesterov(point_w, own_grads[1] / count_all, point_mom, point_avg, rate_net[0])
    edge_out = nesterov(edge_w, own_grads[2] / count_all, edge_mom, edge_avg, rate_net[0])
    code_out = nesterov(codebook, code_sum / count_all, code_mom, code_avg, rate_code[0])
    return (
        loss_sum / count_all,
        conv_out[0],
        conv_out[1],
        conv_out[2],
        conv_out[3],
        point_out[0],
        point_out[1],
        point_out[2],
        point_out[3],
        edge_out[0],
        edge_out[1],
        edge_out[2],
        edge_out[3],
        code_out[0],
        code_out[1],
        code_out[2],
        code_out[3],
    )


def solution(mesh):
    return jax.shard_map(
        per_device,
        mesh=mesh,
        in_specs=(
            P("item", None),
            P("item"),
            P("item", None),
            P("pipe", None, None),
            P("pipe", None, None, None),
            P("pipe", None, None),
            P("pipe", None),
            P("pipe", None, None),
            P("pipe", None, None, None),
            P("pipe", None, None),
            P("pipe", None),
            P("pipe", None, None),
            P("pipe", None, None, None),
            P("pipe", None, None),
            P("pipe", None),
            P(),
            P(),
        ),
        out_specs=(
            P(),
            P("pipe", None, None),
            P("pipe", None, None),
            P("pipe", None, None),
            P("pipe", None, None),
            P("pipe", None, None, None),
            P("pipe", None, None, None),
            P("pipe", None, None, None),
            P("pipe", None, None, None),
            P("pipe", None, None),
            P("pipe", None, None),
            P("pipe", None, None),
            P("pipe", None, None),
            P("pipe", None),
            P("pipe", None),
            P("pipe", None),
            P("pipe", None),
        ),
        check_vma=False,
    )
```

profile of v0, /device:TPU:0, one launch (start us, length us, event | category | flops | bytes accessed | tf_op | source)
XLA Modules:
  0.0 1287.9 jit_solution(11137436909653052054)
XLA Ops:
  16.5 43.4 %conditional.8 = (bf16[16,64,2048]{2,1,0:T(8,128)(2,1)}, bf16[16,4,2048]{2,1,0:T(4,128)(2,1)S(1)}, f32[16,64,2048]{2,1,0:T(8,128)}, bf16[16,192,2048]{2,1,0:T(8,...) conditional(s32[]{:T(128)} %convert_element_type.188, ...), branch_computations={%region_7.9_spmd, %region_8.10_spmd} | conditional | flops 1437663232 | bytes 193450560 | solution.py:214
  22.3 4.8 fusion.199
  27.2 13.4 %fusion.9 = bf16[16,192,2048]{2,1,0:T(8,128)(2,1)S(1)} fusion(bf16[16,64,2045]{2,1,0:T(8,128)(2,1)} %get-tuple-element.451, bf16[16,64,2045]{2,1,0:T(8,128)(2,1)S(1)} %get-tuple-element.450, bf16[16,64,2048]{2,1,0:T(8,128)(2,1)S(1)} %get-tuple-element.454), kind=kLoop, calls=%fused_computation.29 | loop fusion | flops 62914560 | bytes 25153536 | tf_op jit(solution)/shard_map/cond/branch_1_fun/concatenate | solution.py:30
  40.6 7.6 maximum_convert_fusion.2
  48.9 5.6 fusion.11
  54.5 5.4 convert_bitcast_fusion.1
  65.5 47.3 %conditional.6 = (bf16[16,64,2048]{2,1,0:T(8,128)(2,1)}, bf16[16,4,2048]{2,1,0:T(4,128)(2,1)S(1)}, f32[16,64,2048]{2,1,0:T(8,128)}, bf16[16,192,2048]{2,1,0:T(8,...) conditional(s32[]{:T(128)} %convert_element_type.188, ...), branch_computations={%region_0.0_spmd, %region_1.0_spmd} | conditional | flops 1437663232 | bytes 193450560 | solution.py:214
  75.1 4.8 fusion.197
  79.9 13.4 %fusion.2 = bf16[16,192,2048]{2,1,0:T(8,128)(2,1)S(1)} fusion(bf16[16,64,2045]{2,1,0:T(8,128)(2,1)} %get-tuple-element.443, bf16[16,64,2045]{2,1,0:T(8,128)(2,1)S(1)} %get-tuple-element.442, bf16[16,64,2048]{2,1,0:T(8,128)(2,1)S(1)} %get-tuple-element.446), kind=kLoop, calls=%fused_computation.8 | loop fusion | flops 62914560 | bytes 25153536 | tf_op jit(solution)/shard_map/cond/branch_1_fun/concatenate | solution.py:30
  93.3 7.8 maximum_convert_fusion
  101.8 5.6 fusion.4
  107.4 5.4 convert_bitcast_fusion
  117.1 4.1 all_gather.3
  121.9 13.1 %conditional.9 = (bf16[16,64,2048]{2,1,0:T(8,128)(2,1)}, f32[64,192]{1,0:T(8,128)S(1)}, f32[2,64,64]{2,1,0:T(8,128)S(1)}, f32[64,4]{0,1:T(4,128)S(1)}, f32[]{:T(128)}, /*index=5*/f32[2048,64]{0,1:T(8,128)S(1)}) conditional(s32[]{:T(128)} %convert_element_type.188, (s32[32,2048]{1,0:T(8,128)}, bf16[2048,64]{0,1:T(8,128)(2,1)}, ...), branch_computations={%region_9.14_spmd, %region_13.15_spmd} | conditional | flops 4279345152 | bytes 544000576 | solution.py:240
  130.1 4.8 copy.459
  136.4 15.9 %conditional.7 = (bf16[16,64,2048]{2,1,0:T(8,128)(2,1)}, f32[64,192]{1,0:T(8,128)}, f32[2,64,64]{2,1,0:T(8,128)S(1)}, f32[64,4]{0,1:T(4,128)S(1)}, f32[]{:T(128)}, /*index=5*/f32[2048,64]{0,1:T(8,128)S(1)}) conditional(s32[]{:T(128)} %convert_element_type.188, (s32[32,2048]{1,0:T(8,128)}, bf16[2048,64]{0,1:T(8,128)(2,1)}, ...), branch_computations={%region_2.7_spmd, %region_6.8_spmd} | conditional | flops 4279345152 | bytes 544590464 | solution.py:240
  146.9 4.7 copy.433
  158.2 883.8 %psum.42 = f32[]{:T(128)} all-reduce(f32[]{:T(128)S(6)} %add.223), channel_id=1, replica_groups=mesh['item'=16,'pipe'=2] {'item','pipe'}, use_global_device_ids=true, to_apply=%region_14.16 | all-reduce | flops 1 | bytes 8 | tf_op jit(solution)/shard_map/psum | solution.py:256
  1042.0 60.7 %conditional.11 = (f32[64,192]{1,0:T(8,128)}, f32[2,64,64]{2,1,0:T(8,128)S(1)}, f32[64,4]{0,1:T(4,128)S(1)}) conditional(s32[]{:T(128)} %convert_element_type.188, () %tuple.63, (f32[16,64,2048]{2,1,0:T(8,128)}, bf16[2,64,64]{1,2,0:T(8,128)(2,1)S(1)}, bf16[16,64,2048]{2,1,0:T(8,128)(2,1)}, bf16[16,192,2048]{2,1,0:T(8,128)(2,1)}, ...), branch_computations={%region_19.21_spmd, %region_20.22_spmd} | conditional | flops 2717917184 | bytes 235365504 | solution.py:249
  1042.0 5.4 convolution_bitcast_fusion.9
  1052.5 10.8 convolution_bitcast_fusion.8
  1066.8 10.4 convolution_bitcast_fusion.7
  1077.2 11.0 fusion.202
  1088.2 14.5 %fusion.42 = f32[64,4]{0,1:T(4,128)S(1)} fusion(bf16[16,4,2048]{2,1,0:T(4,128)(2,1)S(1)} %get-tuple-element.162, f32[16,192,2048]{2,1,0:T(8,128)} %convolution_bitcast_fusion.7, f32[16,2048,64]{1,2,0:T(8,128)} %copy-done.6, f32[16,64,2045]{2,1,0:T(8,128)} %get-tuple-element.461, f32[16,64,2045]{2,1,0:T(8,128)} %get-tuple-element.460, ...), kind=kOutput, calls=%fused_computation.83 | convolution fusion | flops 29360128 | bytes 42206208 | tf_op jit(solution)/shard_map/cond/branch_1_fun/bct,bkt->ck/dot_general | solution.py:103
  1103.3 61.6 %conditional.10 = (f32[64,192]{1,0:T(8,128)}, f32[2,64,64]{2,1,0:T(8,128)S(1)}, f32[64,4]{0,1:T(4,128)S(1)}) conditional(s32[]{:T(128)} %convert_element_type.188, () %tuple.61, (f32[16,64,2048]{2,1,0:T(8,128)}, bf16[2,64,64]{1,2,0:T(8,128)(2,1)S(1)}, bf16[16,64,2048]{2,1,0:T(8,128)(2,1)}, bf16[16,192,2048]{2,1,0:T(8,128)(2,1)}, ...), branch_computations={%region_17.19_spmd, %region_18.20_spmd} | conditional | flops 2717917184 | bytes 236545216 | solution.py:249
  1103.6 5.4 convolution_bitcast_fusion.6
  1114.0 10.8 convolution_bitcast_fusion.5
  1128.9 10.3 convolution_bitcast_fusion.4
  1139.3 11.1 fusion.201
  1150.4 14.6 %fusion.23 = f32[64,4]{0,1:T(4,128)S(1)} fusion(bf16[16,4,2048]{2,1,0:T(4,128)(2,1)S(1)} %copy-done.34, f32[16,192,2048]{2,1,0:T(8,128)} %convolution_bitcast_fusion.4, f32[16,2048,64]{1,2,0:T(8,128)} %copy-done.7, f32[16,64,2045]{2,1,0:T(8,128)} %get-tuple-element.459, f32[16,64,2045]{2,1,0:T(8,128)} %get-tuple-element.458, ...), kind=kOutput, calls=%fused_computation.60 | convolution fusion | flops 29360128 | bytes 42206208 | tf_op jit(solution)/shard_map/cond/branch_1_fun/bct,bkt->ck/dot_general | solution.py:103
  1167.5 78.5 %all-reduce.33 = (f32[]{:T(128)}, f32[64,192]{1,0:T(8,128)S(1)}, f32[2,64,64]{2,1,0:T(8,128)S(1)}, f32[64,4]{0,1:T(4,128)S(1)}) all-reduce(f32[]{:T(128)S(6)} %convert_element_type.196, f32[64,192]{1,0:T(8,128)S(1)} %add_add_fusion.1, f32[2,64,64]{2,1,0:T(8,128)S(1)} %add_add_fusion, ...), channel_id=1, replica_groups=mesh['item'=16,'pipe'=2] {'item'}, use_global_device_ids=true, to_apply=%region_16.18 | all-reduce | flops 20737 | bytes 165896 | tf_op jit(solution)/shard_map/psum | solution.py:183
  1257.2 18.2 %all-reduce.32.cloned.1.call-done = f32[1024,64]{0,1:T(8,128)} async-done(((f32[1024,64]{0,1:T(8,128)}), f32[1024,64]{0,1:T(8,128)}) %all-reduce.32.cloned.1.call-update) | async-done | bytes 262160 | tf_op jit(solution)/shard_map/psum | solution.py:253
  (165 shorter events, 76.5 us)
Async XLA Ops:
  7.2 1160.3 %reduce-scatter.2.cloned.1.call-start = ((), (), s32[]{:S(2)}) async-start(), calls=%async_computation.1 | async-start | bytes 786432 | tf_op jit(solution)/shard_map/reduce_scatter | solution.py:254
  8.7 7.8 copy-start.52
  20.7 6.5 copy-start.27
  22.3 26.5 %copy-start.10 = (f32[16,64,2048]{2,1,0:T(8,128)}, f32[16,64,2048]{2,1,0:T(8,128)S(1)}, u32[]{:S(2)}) copy-start(f32[16,64,2048]{2,1,0:T(8,128)S(1)} %get-tuple-element.535) | copy-start | bytes 25165828 | tf_op jit(solution)/shard_map/cond
  40.6 8.3 copy-start.8
  54.5 5.5 copy-start.28
  59.9 61.9 %collective-permute-start.1 = (bf16[16,64,2048]{2,1,0:T(8,128)(2,1)}, bf16[16,64,2048]{2,1,0:T(8,128)(2,1)}, u32[]{:S(2)}, u32[]{:S(2)}) collective-permute-start(bf16[16,64,2048]{2,1,0:T(8,128)(2,1)} %get-tuple-element.214), channel_id=1, source_target_pairs={{0,1},{2,3},{4,5},{6,7},{8,9},{10,11},{12,13},{14,15},{16,17},{18,... | collective-permute-start | bytes 12582920 | tf_op jit(solution)/shard_map/ppermute | solution.py:18
  73.5 6.5 copy-start.31
  75.1 26.7 %copy-start.11 = (f32[16,64,2048]{2,1,0:T(8,128)}, f32[16,64,2048]{2,1,0:T(8,128)S(1)}, u32[]{:S(2)}) copy-start(f32[16,64,2048]{2,1,0:T(8,128)S(1)} %get-tuple-element.509) | copy-start | bytes 25165828 | tf_op jit(solution)/shard_map/cond
  93.3 8.4 copy-start.9
  112.9 9.0 copy-start.33
  112.9 23.4 %collective-permute-start = (bf16[16,64,2048]{2,1,0:T(8,128)(2,1)}, bf16[16,64,2048]{2,1,0:T(8,128)(2,1)}, u32[]{:S(2)}, u32[]{:S(2)}) collective-permute-start(bf16[16,64,2048]{2,1,0:T(8,128)(2,1)} %get-tuple-element.212), channel_id=1, source_target_pairs={{0,1},{2,3},{4,5},{6,7},{8,9},{10,11},{12,13},{14,15},{16,17},{18,... | collective-permute-start | bytes 12582920 | tf_op jit(solution)/shard_map/ppermute | solution.py:18
  121.8 14.5 %copy-start.53 = (s32[16]{0:T(128)S(1)}, s32[16]{0:T(128)}, u32[]{:S(2)}) copy-start(s32[16]{0:T(128)} %copy-done.52) | copy-start | bytes 196
  135.0 907.0 %collective-permute-start.3 = (bf16[16,64,2048]{2,1,0:T(8,128)(2,1)}, bf16[16,64,2048]{2,1,0:T(8,128)(2,1)}, u32[]{:S(2)}, u32[]{:S(2)}) collective-permute-start(bf16[16,64,2048]{2,1,0:T(8,128)(2,1)} %get-tuple-element.227), channel_id=1, source_target_pairs={{1,0},{3,2},{5,4},{7,6},{9,8},{11,10},{13,12},{15,14},{17,16},{19,... | collective-permute-start | bytes 12582920 | tf_op jit(solution)/shard_map/ppermute | solution.py:18
  136.3 19.3 %copy-start.57 = (s32[32]{0:T(128)S(1)}, s32[32]{0:T(128)}, u32[]{:S(2)}) copy-start(s32[32]{0:T(128)} %param.32) | copy-start | bytes 388
  136.4 905.6 %copy-start.30 = (bf16[16,4,2048]{2,1,0:T(4,128)(2,1)S(1)}, bf16[16,4,2048]{2,1,0:T(4,128)(2,1)}, u32[]{:S(2)}) copy-start(bf16[16,4,2048]{2,1,0:T(4,128)(2,1)} %copy-done.29) | copy-start | bytes 786436
  152.3 889.7 %copy-start.56 = (f32[64,4]{0,1:T(4,128)}, f32[64,4]{0,1:T(4,128)S(1)}, u32[]{:S(2)}) copy-start(f32[64,4]{0,1:T(4,128)S(1)} %get-tuple-element.238) | copy-start | bytes 3076
  152.3 950.4 %collective-permute-start.2 = (bf16[16,64,2048]{2,1,0:T(8,128)(2,1)}, bf16[16,64,2048]{2,1,0:T(8,128)(2,1)}, u32[]{:S(2)}, u32[]{:S(2)}) collective-permute-start(bf16[16,64,2048]{2,1,0:T(8,128)(2,1)} %get-tuple-element.218), channel_id=1, source_target_pairs={{1,0},{3,2},{5,4},{7,6},{9,8},{11,10},{13,12},{15,14},{17,16},{19,... | collective-permute-start | bytes 12582920 | tf_op jit(solution)/shard_map/ppermute | solution.py:18
  155.6 1119.8 %all-reduce.32.cloned.1.call-start = ((), (), s32[]{:S(2)}) async-start(), calls=%async_computation.2 | async-start | bytes 524288 | tf_op jit(solution)/shard_map/psum | solution.py:253
  1042.0 9.0 slice-start.4
  1051.1 12.2 copy-start.6
  1103.3 62.4 %copy-start.39 = (f32[2,64,64]{2,1,0:T(8,128)S(1)}, f32[2,64,64]{2,1,0:T(8,128)}, u32[]{:S(2)}) copy-start(f32[2,64,64]{2,1,0:T(8,128)} %copy-done.38) | copy-start | bytes 98308
  1103.3 146.4 %copy-start.51 = (f32[1,64,4]{1,2,0:T(4,128)S(1)}, f32[1,64,4]{1,2,0:T(4,128)}, u32[]{:S(2)}) copy-start(f32[1,64,4]{1,2,0:T(4,128)} %param.36) | copy-start | bytes 3076
  1103.3 150.5 %copy-start.54 = (f32[1,64,4]{1,2,0:T(4,128)S(1)}, f32[1,64,4]{1,2,0:T(4,128)}, u32[]{:S(2)}) copy-start(f32[1,64,4]{1,2,0:T(4,128)} %param.44) | copy-start | bytes 3076
  1103.3 172.1 %copy-start.37 = (f32[1024,64]{0,1:T(8,128)S(1)}, f32[1024,64]{0,1:T(8,128)}, u32[]{:S(2)}) copy-start(f32[1024,64]{0,1:T(8,128)} %param.37) | copy-start | bytes 786436
  1103.5 9.0 slice-start.6
  1112.6 12.2 copy-start.7
  1139.3 11.1 copy-start.34
  1150.4 14.6 %copy-start.41 = (f32[2,64,64]{2,1,0:T(8,128)S(1)}, f32[2,64,64]{2,1,0:T(8,128)}, u32[]{:S(2)}) copy-start(f32[2,64,64]{2,1,0:T(8,128)} %pad_maximum_fusion.2) | copy-start | bytes 98308 | tf_op jit(solution)/shard_map/cond
  1248.2 31.5 %copy-start.42 = (f32[1,64,192]{2,1,0:T(8,128)}, f32[1,64,192]{2,1,0:T(8,128)S(1)}, u32[]{:S(2)}) copy-start(f32[1,64,192]{2,1,0:T(8,128)S(1)} %get-tuple-element.440) | copy-start | bytes 147460
  1251.6 28.1 %copy-start.50 = (f32[1,64,4]{1,2,0:T(4,128)}, f32[1,64,4]{1,2,0:T(4,128)S(1)}, u32[]{:S(2)}) copy-start(f32[1,64,4]{1,2,0:T(4,128)S(1)} %get-tuple-element.434) | copy-start | bytes 3076
  1253.8 25.9 %copy-start.43 = (f32[1,2,64,64]{3,2,1,0:T(8,128)}, f32[1,2,64,64]{3,2,1,0:T(8,128)S(1)}, u32[]{:S(2)}) copy-start(f32[1,2,64,64]{3,2,1,0:T(8,128)S(1)} %get-tuple-element.437) | copy-start | bytes 98308
  (15 other events, 37.4 us)
Sparse Core Ops, SparseCore 0:
  155.7 853.5 reduce-scatter.1
  1167.6 107.6 all-reduce.31
where the time goes:
time: 1290 us
  blocking collectives  966 us (75%)
  matrix products  140 us (11%)
  local copies, waits for them, and re-layouts  61.6 us (5%)
  other arithmetic  53.7 us (4%)
  loops' own time  20 us (2%)
  between operations  19 us (1%)
  waiting for transfers between devices  18.2 us (1%)
    psum x1, blocking collectives, per_device(): loss_sum = lax.psum(acc_loss, ('item', 'pipe'))  884 us
    psum x1, blocking collectives, per_device(): count_all = lax.psum(local_count, 'item')  78.5 us
    dot_general x6, matrix products, weight_grad(): jnp.einsum('bot,bct->oc', grads, values, preferred_element_type=jnp.float32)  39.4 us
    dot_general x6, matrix products, mixing(): jnp.einsum('fw,ywi->yfi', weight, values, preferred_element_type=jnp.floa...  37.5 us
    dot_general x6, matrix products, input_gradient_rows(): jnp.einsum('oc,bot->bct', weight, grads, preferred_element_type=jnp.float32)  30.6 us
    dot_general x2, matrix products, encode_back(): jnp.einsum('bct,bkt->ck', d_hidden, strips, preferred_element_type=jnp.fl...  29.1 us
    concatenate x2, other arithmetic, spread_kernel_taps(): jnp.concatenate([shift_along(values, -reach), values, shift_along(values,...  26.8 us
  transfers between devices with their start and end apart: 6, of which 1 were waited for; matrix products, arithmetic and copies ran while one was open for 15% of the time, Pallas kernels for 0%

commit v1 on v0

v1 whole, which is shorter than its diff:
```python
import functools

import jax
import jax.numpy as jnp
from jax import lax
from jax.experimental import pallas as pl
from jax.experimental.pallas import tpu as pltpu
from jax.sharding import PartitionSpec as P

REACH = 3
COMMIT = 0.02
MOMENTUM = 0.9
AVERAGE = 0.99

LANES = 128
TILE = 512
SLOTS = 8
LOW = 256
SPARE = 16
REAL = 8

F32 = jnp.float32
BF16 = jnp.bfloat16


def nn(a, b):
    return lax.dot_general(a, b, (((1,), (0,)), ((), ())), preferred_element_type=F32)


def nt(a, b):
    return lax.dot_general(a, b, (((1,), (1,)), ((), ())), preferred_element_type=F32)


def moved(ext, distance):
    width = ext.shape[1]
    turned = ext if distance == 0 else pltpu.roll(ext, (-distance) % width, 1)
    return turned[:, LANES : width - LANES]


def relu_bf(values):
    return jnp.maximum(values, 0.0).astype(BF16)


def stack(rows, times):
    return jnp.concatenate([rows] * times, axis=0)


def net_kernel(
    rank_ref,
    len_ref,
    wave_ref,
    ids_ref,
    conv_ref,
    conv_t_ref,
    point_ref,
    point_t_ref,
    edge_ref,
    edge_t_ref,
    table_ref,
    g_conv,
    g_point,
    g_edge,
    g_table,
    loss_ref,
    src_list,
    len_list,
    even_scr,
    odd_scr,
    code_scr,
    sig_r,
    msk_r,
    live_r,
    me_r,
    strips_r,
    onehot_r,
    hi_r,
    hidden_r,
    actu_e_r,
    chosen_r,
    decin_r,
    actu_d_r,
    actp_e_r,
    encres_r,
    actp_d_r,
    resb_r,
    gap_r,
    outs_r,
    dres_r,
    dinner_d_r,
    denc_r,
    dinner_e_r,
):
    clips, frames = wave_ref.shape
    half = frames // 2
    per_clip = half // LANES
    width = conv_ref.shape[1]
    groups = table_ref.shape[0] // width
    per_tile = TILE // LANES
    rank = rank_ref[0]

    for ref in (
        sig_r, msk_r, live_r, me_r, strips_r, onehot_r, hi_r, hidden_r, actu_e_r, chosen_r,
        decin_r, actu_d_r, actp_e_r, encres_r, actp_d_r, resb_r, gap_r, outs_r, dres_r,
        dinner_d_r, denc_r, dinner_e_r,
    ):

        @pl.loop(0, SLOTS)
        def _(slot, ref=ref):
            ref[:, pl.ds(pl.multiple_of(slot * TILE, TILE), TILE)] = jnp.zeros(
                (ref.shape[0], TILE), ref.dtype
            )

    for ref in (g_conv, g_point, g_edge, g_table, loss_ref):
        ref[...] = jnp.zeros(ref.shape, ref.dtype)

    row_at = lax.broadcasted_iota(jnp.int32, (2 * LANES, 2 * LANES), 0)
    col_at = lax.broadcasted_iota(jnp.int32, (2 * LANES, 2 * LANES), 1)
    wanted = jnp.where(col_at < LANES, 2 * col_at, 2 * (col_at - LANES) + 1)
    split = jnp.where(row_at == wanted, 1.0, 0.0).astype(BF16)
    for block in range(per_clip):
        parted = nn(wave_ref[:, block * 2 * LANES : (block + 1) * 2 * LANES], split)
        even_scr[block] = parted[:, :LANES]
        odd_scr[block] = parted[:, LANES:]
        code_scr[block] = ids_ref[:, block * LANES : (block + 1) * LANES]

    def put(index, source, length):
        src_list[index] = source
        len_list[index] = length

    put(0, 0, -frames)

    def add_clip(c, filled):
        clip = 2 * c + rank
        length = len_ref[clip]
        blocks = lax.shift_right_logical(
            lax.shift_right_logical(length + 1, 1) + (SPARE + LANES - 1), 7
        )

        def add_block(k, carry):
            put(filled + k, clip * 32 + k, length)
            return carry

        lax.fori_loop(0, blocks, add_block, 0)
        return filled + blocks

    filled = lax.fori_loop(0, clips // 2, add_clip, jnp.int32(1))
    tiles = lax.div(filled - 1 + per_tile - 1, jnp.int32(per_tile)) + 4

    def add_empty(k, carry):
        put(filled + k, 0, -frames)
        return carry

    lax.fori_loop(0, 6 * per_tile + 2, add_empty, 0)

    sub = lax.broadcasted_iota(jnp.int32, (8, LANES), 0)
    lane = lax.broadcasted_iota(jnp.int32, (8, LANES), 1)
    sub_ext = lax.broadcasted_iota(jnp.int32, (8, TILE + 2 * LANES), 0)
    sub_tile = lax.broadcasted_iota(jnp.int32, (8, TILE), 0)
    iota16 = lax.broadcasted_iota(jnp.int32, (16, TILE), 0).astype(F32).astype(BF16)

    def taps(ext):
        later = moved(ext, 1)
        earlier = moved(ext, -1)
        other = jnp.where(sub_tile == 0, later, jnp.where(sub_tile == 1, earlier, 0.0))
        return jnp.concatenate([moved(ext, 0), other], axis=0)

    @pl.loop(0, tiles)
    def _(i):
        def at(lag):
            return pl.multiple_of(lax.rem(i - lag + SLOTS, SLOTS) * TILE, TILE)

        def cur(ref, lag):
            return ref[:, pl.ds(at(lag), TILE)]

        def last_of(ref, lag):
            return ref[:, pl.ds(at(lag) + (TILE - LANES), LANES)]

        def first_of(ref, lag):
            return ref[:, pl.ds(at(lag), LANES)]

        def ext(ref, lag, following):
            return jnp.concatenate([last_of(ref, lag + 1), cur(ref, lag), following], axis=1)

        def keep(ref, lag, value):
            ref[:, pl.ds(at(lag), TILE)] = value

        e2_actu_e = (last_of(actu_e_r, 2), cur(actu_e_r, 1))
        e2_actu_d = (last_of(actu_d_r, 2), cur(actu_d_r, 1))
        e3_outs = (last_of(outs_r, 3), cur(outs_r, 2))
        e4_din = (last_of(dinner_d_r, 4), cur(dinner_d_r, 3))
        e5_din = (last_of(dinner_e_r, 5), cur(dinner_e_r, 4))
        chosen1, chosen3 = cur(chosen_r, 1), cur(chosen_r, 3)
        hidden1, decin1 = cur(hidden_r, 1), cur(decin_r, 1)
        onehot1, hi1, me1 = cur(onehot_r, 1), cur(hi_r, 1), cur(me_r, 1)
        actp_d2, resb2 = cur(actp_d_r, 2), cur(resb_r, 2)
        actu_d3, actp_e3, encres3, gap3, dres3 = (
            cur(actu_d_r, 3), cur(actp_e_r, 3), cur(encres_r, 3), cur(gap_r, 3), cur(dres_r, 3)
        )
        actu_e4, denc4, strips4 = cur(actu_e_r, 4), cur(denc_r, 4), cur(strips_r, 4)
        sig2 = ext(sig_r, 2, first_of(sig_r, 1))
        msk2 = ext(msk_r, 2, first_of(msk_r, 1))
        live2 = cur(live_r, 2)
        live2_ext = ext(live_r, 2, first_of(live_r, 1))

        sigs, msks, lives, mes, los, his = [], [], [], [], [], []
        for j in range(-1, per_tile + 1):
            index = i * per_tile + (j + 1)
            source, length = src_list[index], len_list[index]
            clip = lax.shift_right_logical(source, 5)
            block = jnp.bitwise_and(source, 31)
            here = (jnp.minimum(block, per_clip - 1), pl.ds(clip, 1), slice(None))
            t = block * LANES + lane
            even_ok = 2 * t < length
            odd_ok = 2 * t + 1 < length
            even = jnp.broadcast_to(even_scr[here], (8, LANES))
            odd = jnp.broadcast_to(odd_scr[here], (8, LANES))
            sigs.append(
                jnp.where((sub == 0) & even_ok, even, jnp.where((sub == 1) & odd_ok, odd, 0.0))
            )
            if 0 <= j < per_tile:
                valid = lax.shift_right_arithmetic(length + 1, 1)
                live = t < jnp.minimum(valid + REAL, half)
                code = jnp.broadcast_to(code_scr[here], (8, LANES))
                msks.append(
                    jnp.where(((sub == 0) & even_ok) | ((sub == 1) & odd_ok), 1.0, 0.0)
                )
                lives.append(jnp.where(live, 1.0, 0.0))
                mes.append(jnp.where(even_ok, 1.0, 0.0))
                los.append(jnp.where(live, jnp.bitwise_and(code, LOW - 1), -1).astype(F32))
                his.append(lax.shift_right_logical(code, 8).astype(F32))
        sig_ext = jnp.concatenate(sigs, axis=1)
        live0 = jnp.concatenate(lives, axis=1)
        strips = (taps(sig_ext) * stack(live0, 2)).astype(BF16)
        hidden = nn(edge_ref[0], strips)
        actu_e = relu_bf(hidden)

        low16 = stack(jnp.concatenate(los, axis=1), 2).astype(BF16) - iota16
        onehot = jnp.concatenate(
            [
                jnp.where(low16 == float(16 * r), jnp.ones((), BF16), jnp.zeros((), BF16))
                for r in range(LOW // 16)
            ],
            axis=0,
        )
        picked = nn(table_ref[...], onehot)
        hi0 = jnp.concatenate(his, axis=1)
        parts = [jnp.zeros((8, TILE), F32) for _ in range(width // 8)]
        for h in range(groups):
            here = hi0 == float(h)
            parts = [
                jnp.where(here, picked[h * width + 8 * r : h * width + 8 * r + 8], parts[r])
                for r in range(width // 8)
            ]
        chosen = jnp.concatenate(parts, axis=0).astype(BF16)
        decin = nn(point_ref[2], chosen)
        actu_d = relu_bf(decin)

        keep(sig_r, 0, moved(sig_ext, 0))
        keep(msk_r, 0, jnp.concatenate(msks, axis=1))
        keep(live_r, 0, live0)
        keep(me_r, 0, jnp.concatenate(mes, axis=1))
        keep(hi_r, 0, stack(hi0, 2).astype(BF16))
        keep(strips_r, 0, strips)
        keep(onehot_r, 0, onehot)
        keep(hidden_r, 0, hidden)
        keep(actu_e_r, 0, actu_e)
        keep(chosen_r, 0, chosen)
        keep(decin_r, 0, decin)
        keep(actu_d_r, 0, actu_d)

        def spread(pair, following):
            whole = jnp.concatenate([*pair, following], axis=1)
            return jnp.concatenate([moved(whole, d) for d in (-REACH, 0, REACH)], axis=0)

        def spread_back(pair, following):
            whole = jnp.concatenate([*pair, following], axis=1)
            return jnp.concatenate([moved(whole, d) for d in (REACH, 0, -REACH)], axis=0)

        actp_e = relu_bf(nn(conv_ref[0], spread(e2_actu_e, actu_e[:, :LANES])))
        encres = (hidden1 + nn(point_ref[0], actp_e)).astype(BF16)
        latent = nn(point_ref[1], encres).astype(BF16)
        gap = (latent.astype(F32) - chosen1.astype(F32)) * stack(me1, width // 8)
        gap_bf = gap.astype(BF16)
        square = gap * gap
        loss_rows = square[:8]
        for r in range(1, width // 8):
            loss_rows = loss_rows + square[8 * r : 8 * r + 8]
        terms = []
        for h in range(groups):
            here = hi1 == float(h)
            terms += [
                jnp.where(here, gap_bf[16 * r : 16 * r + 16], jnp.zeros((), BF16))
                for r in range(width // 16)
            ]
        g_table[...] += nt(jnp.concatenate(terms, axis=0), onehot1)

        actp_d = relu_bf(nn(conv_ref[1], spread(e2_actu_d, actu_d[:, :LANES])))
        resb = (decin1 + nn(point_ref[3], actp_d)).astype(BF16)
        outs = nn(edge_t_ref[1], resb)
        keep(actp_e_r, 1, actp_e)
        keep(encres_r, 1, encres)
        keep(gap_r, 1, gap * (2.0 * COMMIT))
        keep(actp_d_r, 1, actp_d)
        keep(resb_r, 1, resb)
        keep(outs_r, 1, outs)

        outs_ext = jnp.concatenate([*e3_outs, outs[:, :LANES]], axis=1) * stack(live2_ext, 2)
        shifted = outs_ext[8:]
        wide = TILE + 2 * LANES
        crossed = jnp.where(
            sub_ext == 0, pltpu.roll(shifted, 1, 1), pltpu.roll(shifted, wide - 1, 1)
        )
        error = (outs_ext[:8] + crossed - sig2) * msk2
        middle = moved(error, 0)
        loss_rows = COMMIT * loss_rows + middle * middle
        loss_sum = loss_rows[:, :LANES]
        for j in range(1, per_tile):
            loss_sum = loss_sum + loss_rows[:, j * LANES : (j + 1) * LANES]
        loss_ref[...] += loss_sum
        douts = (2.0 * taps(error) * stack(live2, 2)).astype(BF16)
        g_edge[1] += nt(resb2, douts)
        dres = nn(edge_ref[1], douts)
        dbranch = dres.astype(BF16)
        g_point[3] += nt(dbranch, actp_d2)
        dinner_d = jnp.where(actp_d2 > 0, nn(point_t_ref[3], dbranch).astype(BF16), 0)
        keep(dres_r, 2, dres)
        keep(dinner_d_r, 2, dinner_d)

        around = spread_back(e4_din, dinner_d[:, :LANES])
        g_conv[1] += nt(around, actu_d3)
        ddecin = (dres3 + jnp.where(actu_d3 > 0, nn(conv_t_ref[1], around), 0.0)).astype(BF16)
        g_point[2] += nt(ddecin, chosen3)
        dlatent = (nn(point_t_ref[2], ddecin) + gap3).astype(BF16)
        g_point[1] += nt(dlatent, encres3)
        denc = nn(point_t_ref[1], dlatent)
        dbranch_e = denc.astype(BF16)
        g_point[0] += nt(dbranch_e, actp_e3)
        dinner_e = jnp.where(actp_e3 > 0, nn(point_t_ref[0], dbranch_e).astype(BF16), 0)
        keep(denc_r, 3, denc)
        keep(dinner_e_r, 3, dinner_e)

        around_e = spread_back(e5_din, dinner_e[:, :LANES])
        g_conv[0] += nt(around_e, actu_e4)
        dhidden = (denc4 + jnp.where(actu_e4 > 0, nn(conv_t_ref[0], around_e), 0.0)).astype(BF16)
        g_edge[0] += nt(dhidden, strips4)


def net(rank, lengths, waveform, code_ids, conv, conv_t, point, point_t, edge, edge_t, table):
    clips, frames = waveform.shape
    width = conv.shape[1]
    columns = SLOTS * TILE
    listed = (clips // 2) * (frames // 2 // LANES + 1) + 8 * (TILE // LANES) + 8
    smem = pl.BlockSpec(memory_space=pltpu.SMEM)
    vmem = pl.BlockSpec(memory_space=pltpu.VMEM)

    def ring(rows, dtype):
        return pltpu.VMEM((rows, columns), dtype)

    return pl.pallas_call(
        net_kernel,
        out_shape=(
            jax.ShapeDtypeStruct((2, 3 * width, width), F32),
            jax.ShapeDtypeStruct((4, width, width), F32),
            jax.ShapeDtypeStruct((2, width, 16), F32),
            jax.ShapeDtypeStruct(table.shape, F32),
            jax.ShapeDtypeStruct((8, LANES), F32),
        ),
        in_specs=[smem, smem] + [vmem] * 9,
        out_specs=(vmem,) * 5,
        scratch_shapes=[
            pltpu.SMEM((listed,), jnp.int32),
            pltpu.SMEM((listed,), jnp.int32),
            pltpu.VMEM((frames // 2 // LANES, clips, LANES), F32),
            pltpu.VMEM((frames // 2 // LANES, clips, LANES), F32),
            pltpu.VMEM((frames // 2 // LANES, clips, LANES), jnp.int32),
            ring(8, F32),
            ring(8, F32),
            ring(8, F32),
            ring(8, F32),
            ring(16, BF16),
            ring(LOW, BF16),
            ring(16, BF16),
            ring(width, F32),
            ring(width, BF16),
            ring(width, BF16),
            ring(width, F32),
            ring(width, BF16),
            ring(width, BF16),
            ring(width, BF16),
            ring(width, BF16),
            ring(width, BF16),
            ring(width, F32),
            ring(16, F32),
            ring(width, F32),
            ring(width, BF16),
            ring(width, F32),
            ring(width, BF16),
        ],
        compiler_params=pltpu.CompilerParams(vmem_limit_bytes=48 * 2**20),
    )(rank, lengths, waveform, code_ids, conv, conv_t, point, point_t, edge, edge_t, table)


def nesterov(weight, grad, moment, average, rate):
    moment_new = MOMENTUM * moment + grad
    weight_new = weight - rate * (grad + MOMENTUM * moment_new)
    average_new = AVERAGE * average + (1.0 - AVERAGE) * weight_new
    return (weight_new, moment_new, average_new, weight_new.astype(jnp.bfloat16))


def per_device(
    waveform,
    lengths,
    code_ids,
    conv_w,
    point_w,
    edge_w,
    codebook,
    conv_mom,
    point_mom,
    edge_mom,
    code_mom,
    conv_avg,
    point_avg,
    edge_avg,
    code_avg,
    rate_net,
    rate_code,
):
    width = conv_w.shape[1]
    rank = lax.axis_index("pipe").reshape(1).astype(jnp.int32)
    own_rows = codebook.shape[0]

    def gathered(block):
        return lax.all_gather(block, "pipe", axis=0, tiled=True)

    own_table = codebook.astype(BF16).reshape(own_rows // LOW, LOW, width)
    own_table = jnp.swapaxes(own_table, 1, 2).reshape(own_rows // LOW * width, LOW)
    table = gathered(own_table)
    conv = gathered(conv_w.astype(BF16))
    point = gathered(point_w.astype(BF16).reshape(2, width, width))
    edge = gathered(edge_w.astype(BF16))
    conv_t = jnp.transpose(conv.reshape(2, width, 3, width), (0, 3, 2, 1)).reshape(conv.shape)
    point_t = jnp.swapaxes(point, 1, 2)
    gaps = jnp.zeros((2, width, 6), BF16)
    edge16 = jnp.concatenate([edge[:, :, 1:3], gaps, edge[:, :, 3:], edge[:, :, :1], gaps], -1)
    edge16_t = jnp.swapaxes(edge16, 1, 2)

    g_conv, g_point, g_edge, g_table, loss_rows = net(
        rank, lengths, waveform, code_ids, conv, conv_t, point, point_t, edge16, edge16_t, table
    )
    code_grad = lax.psum_scatter(g_table, "pipe", scatter_dimension=0, tiled=True)
    code_grad = lax.psum(code_grad, "item")
    net_grad = jnp.concatenate(
        [g_conv.reshape(2, -1), g_point.reshape(2, -1), g_edge.reshape(2, -1)], axis=1
    )
    net_grad = lax.psum_scatter(net_grad, "pipe", scatter_dimension=0, tiled=True)
    net_grad, count_all = lax.psum((net_grad[0], jnp.sum(lengths).astype(F32)), "item")
    loss_sum = lax.psum(jnp.sum(loss_rows), ("item", "pipe"))

    sizes = (3 * width * width, 2 * width * width)
    conv_grad = net_grad[: sizes[0]].reshape(3, width, width)
    conv_grad = jnp.transpose(conv_grad, (1, 0, 2)).reshape(1, width, 3 * width)
    point_grad = net_grad[sizes[0] : sizes[0] + sizes[1]].reshape(1, 2, width, width)
    edge_grad = net_grad[sizes[0] + sizes[1] :].reshape(1, width, 16)
    edge_grad = jnp.concatenate(
        [edge_grad[:, :, 9:10], edge_grad[:, :, :2], edge_grad[:, :, 8:9]], -1
    )
    code_grad = code_grad.reshape(own_rows // LOW, width, LOW)
    code_grad = jnp.swapaxes(code_grad, 1, 2).reshape(own_rows, width) * (-2.0 * COMMIT)
    conv_out = nesterov(conv_w, conv_grad / count_all, conv_mom, conv_avg, rate_net[0])
    point_out = nesterov(point_w, point_grad / count_all, point_mom, point_avg, rate_net[0])
    edge_out = nesterov(edge_w, edge_grad / count_all, edge_mom, edge_avg, rate_net[0])
    code_out = nesterov(codebook, code_grad / count_all, code_mom, code_avg, rate_code[0])
    return (loss_sum / count_all, *conv_out, *point_out, *edge_out, *code_out)


def solution(mesh):
    weights = (
        P("pipe", None, None),
        P("pipe", None, None, None),
        P("pipe", None, None),
        P("pipe", None),
    )
    return jax.shard_map(
        per_device,
        mesh=mesh,
        in_specs=(P("item", None), P("item"), P("item", None), *weights, *weights, *weights, P(), P()),
        out_specs=(P(),) + tuple(spec for spec in weights for _ in range(4)),
        check_vma=False,
    )
```

time: 1290 us -> 354 us (0.27)
  blocking collectives: 966 us -> 89.9 us
  matrix products: 140 us -> 0 us
  waiting for transfers between devices: 18.2 us -> 157 us
  Pallas kernels: 0 us -> 64.1 us
  local copies, waits for them, and re-layouts: 61.6 us -> 12 us
  other arithmetic: 53.7 us -> 10.9 us
  loops' own time: 20 us -> 0 us
    psum x2, blocking collectives: 962 us -> 82.2 us  [the longest x1 41.3 us: per_device(): lax.psum((net_grad[0], jnp.sum(lengths).astype(F32)), 'item')]
    dot_general x22 -> x0, matrix products: 140 us -> none  [the longest x6 39.4 us: weight_grad(): jnp.einsum('bot,bct->oc', grads, values, preferred_element_type=jnp.float32)]
    unnamed x2 -> x4, waiting for transfers between devices: 0.03 us -> 120 us
    pallas_call x0 -> x1, Pallas kernels: none -> 64.1 us  [net(): pl.pallas_call(net_kernel, out_shape=(jax.ShapeDtypeStruct((2, 3 * width,...]
    slice x14 -> x7, local copies, waits for them, and re-layouts: 41.9 us -> 0.99 us  [the longest x1 0.68 us: per_device(): edge_grad = net_grad[sizes[0] + sizes[1]:].reshape(1, width, 16)]
    concatenate x2 -> x1, other arithmetic: 26.8 us -> 0.74 us  [per_device(): jnp.concatenate([g_conv.reshape(2, -1), g_point.reshape(2, -1), g_edge.re...]
    another operation x6 -> x0, loops' own time: 20 us -> none  [the longest x2 18.8 us: per_device(): lax.cond(on_first, skip_decode, run_decode)]
  transfers between devices with their start and end apart: 6 -> 3, of which waited for: 1 -> 3; matrix products, arithmetic and copies ran while one was open for 15% -> 1% of each run, Pallas kernels for 0% -> 0%
where the time goes in v1:
time: 354 us; the launch traced here: 353 us
  waiting for transfers between devices  157 us (44%)
  blocking collectives  89.9 us (25%)
  Pallas kernels  64.1 us (18%)
  between operations  18.4 us (5%)
  local copies, waits for them, and re-layouts  12 us (3%)
  other arithmetic  10.9 us (3%)
    unnamed x4, waiting for transfers between devices  120 us
    pallas_call x1, Pallas kernels, net(): pl.pallas_call(net_kernel, out_shape=(jax.ShapeDtypeStruct((2, 3 * width,...  64.1 us
    psum x1, blocking collectives, per_device(): lax.psum((net_grad[0], jnp.sum(lengths).astype(F32)), 'item')  41.3 us
    psum x1, blocking collectives, per_device(): loss_sum = lax.psum(jnp.sum(loss_rows), ('item', 'pipe'))  40.9 us
    psum x1, waiting for transfers between devices, per_device(): lax.psum((net_grad[0], jnp.sum(lengths).astype(F32)), 'item')  27.8 us
    unnamed x49, local copies, waits for them, and re-layouts  9.7 us
    reduce_scatter x1, waiting for transfers between devices, per_device(): lax.psum_scatter(g_table, 'pipe', scatter_dimension=0, tiled=True)  9.15 us
    all_gather x4, blocking collectives, gathered(): return lax.all_gather(block, 'pipe', axis=0, tiled=True)  7.72 us
  transfers between devices with their start and end apart: 3, of which 3 were waited for; matrix products, arithmetic and copies ran while one was open for 1% of the time, Pallas kernels for 0%

profile of v1, /device:TPU:0, one launch (start us, length us, event | category | flops | bytes accessed | tf_op | source)
XLA Modules:
  0.0 352.8 jit_solution(4901583882285740298)
XLA Ops:
  7.2 0.7 convert_element_type.29
  7.9 1.9 all_gather.14
  10.0 1.9 all_gather.12.conv_ref
  12.9 1.8 all-gather
  14.9 2.1 all_gather.15.table_ref
  17.0 0.6 copy-done.2
  17.7 64.1 %shard_map.296 = (f32[2,192,64]{2,1,0:T(8,128)S(1)}, f32[4,64,64]{2,1,0:T(8,128)S(1)}, f32[2,64,16]{2,1,0:T(8,128)S(1)}, f32[512,256]{1,0:T(8,128)}, f32[8,128]{1,0:T(8,128)S(1)}) custom-call(s32[1]{0:T(128)} %bitcast.rank_ref, s32[32]{0:T(128)S(1)} %copy-done.2, bf16[32,4096]{1,0:T(8,128)(2,1)S(1)} %copy-done, s32[32,2048]{1,0:T(8,128)S(1)} %copy-done.1, ...), custom_call_target="tpu_custom_call" | custom-call | tf_op jit(solution)/shard_map/pallas_call | solution.py:359
  82.1 0.7 pad_maximum_fusion
  83.0 0.7 reduce-scatter.2.cloned.1.call-update
  83.7 0.6 copy-done.19
  85.0 119.6 %all-reduce.5.cloned.1.call-done = f32[2,21504]{1,0:T(2,128)} async-done(((f32[2,21504]{1,0:T(2,128)}), f32[2,21504]{1,0:T(2,128)}) %all-reduce.5.cloned.1.call-update) | async-done | bytes 172048
  204.5 2.3 constant_dynamic-slice_fusion
  206.8 9.2 %reduce-scatter.2.cloned.1.call-done = f32[256,256]{1,0:T(8,128)} async-done(((f32[512,256]{1,0:T(8,128)}), f32[256,256]{1,0:T(8,128)}) %reduce-scatter.2.cloned.1.call-update) | async-done | bytes 262160 | tf_op jit(solution)/shard_map/reduce_scatter | solution.py:451
  216.0 0.6 reduce_sum.19
  217.9 40.9 %psum.28 = f32[]{:T(128)} all-reduce(f32[]{:T(128)} %reduce_sum.18), channel_id=1, replica_groups=mesh['item'=16,'pipe'=2] {'item','pipe'}, use_global_device_ids=true, to_apply=%region_1.0 | all-reduce | flops 1 | bytes 8 | tf_op jit(solution)/shard_map/psum | solution.py:458
  258.8 41.3 %psum.29 = f32[]{:T(128)} all-reduce(f32[]{:T(128)S(6)} %convert_element_type.31), channel_id=1, replica_groups=mesh['item'=16,'pipe'=2] {'item'}, use_global_device_ids=true, to_apply=%region_3.0 | all-reduce | flops 1 | bytes 8 | tf_op jit(solution)/shard_map/psum | solution.py:457
  301.0 0.7 copy-done.13
  303.8 27.8 %all-reduce.7.cloned.1.call-done = (f32[21504]{0:T(1024)}, f32[256,256]{1,0:T(8,128)}) async-done(((f32[21504]{0:T(1024)}, f32[256,256]{1,0:T(8,128)}), (f32[21504]{0:T(1024)}, f32[256,256]{1,0:T(8,128)})) %all-reduce.7.cloned.1.call-update) | async-done | bytes 348176 | tf_op jit(solution)/shard_map/psum | solution.py:457
  331.6 0.7 slice.49
  332.3 1.5 slice_divide_fusion
  333.7 1.4 slice_divide_fusion.1
  335.8 0.7 copy.81
  336.5 0.7 copy.83
  337.3 0.7 copy.82
  338.0 0.7 copy.84
  338.7 0.7 multiply_divide_fusion
  339.5 0.6 copy-done.16
  340.1 1.2 fusion.3
  342.0 0.7 fusion.4
  342.8 0.6 multiply_add_fusion.3
  343.4 0.8 fusion.2
  344.4 0.7 multiply_add_fusion
  (74 shorter events, 5.0 us)
Async XLA Ops:
  7.2 2.8 copy-start.7
  7.2 197.3 %all-reduce.5.cloned.1.call-start = ((), (), s32[]{:S(2)}) async-start(), calls=%async_computation.2 | async-start | bytes 344064
  12.0 0.8 copy-start.9
  12.2 2.7 copy-start.4
  14.9 2.2 copy-start.1
  14.9 2.1 copy-start
  17.0 0.7 copy-start.2
  82.9 133.0 %reduce-scatter.2.cloned.1.call-start = ((), (), s32[]{:S(2)}) async-start(), calls=%async_computation.1 | async-start | bytes 786432 | tf_op jit(solution)/shard_map/reduce_scatter | solution.py:451
  83.7 247.9 %all-reduce.7.cloned.1.call-start = ((), (), s32[]{:S(2)}) async-start(), calls=%async_computation.3 | async-start | bytes 696320 | tf_op jit(solution)/shard_map/psum | solution.py:457
  83.7 0.7 copy-start.19
  300.1 0.8 copy-start.12
  300.9 0.8 copy-start.13
  336.5 2.2 copy-start.6
  339.4 0.7 copy-start.16
  339.4 0.7 copy-start.18
  339.4 1.9 copy-start.17
  339.5 2.5 copy-start.14
  341.4 0.6 copy-start.15
  341.9 0.8 copy-start.11
  341.9 1.5 copy-start.10
  342.6 0.8 copy-start.8
  343.4 1.0 copy-start.5
  344.2 0.9 copy-start.3
Sparse Core Ops, SparseCore 0:
  83.0 121.4 all-reduce.4
  206.8 9.1 reduce-scatter.1
  222.6 108.9 all-reduce.6

commit v2 on v1

--- a/solution.py
+++ b/solution.py
@@ -19,6 +19,7 @@
 SPARE = 16
 REAL = 8
 
+MESH = pl.DeviceIdType.MESH
 F32 = jnp.float32
 BF16 = jnp.bfloat16
 
@@ -46,17 +47,12 @@
 
 
 def net_kernel(
-    rank_ref,
     len_ref,
     wave_ref,
     ids_ref,
-    conv_ref,
-    conv_t_ref,
-    point_ref,
-    point_t_ref,
-    edge_ref,
-    edge_t_ref,
-    table_ref,
+    weight_ref,
+    payload_ref,
+    stats_ref,
     g_conv,
     g_point,
     g_edge,
@@ -90,13 +86,24 @@
     denc_r,
     dinner_e_r,
 ):
-    clips, frames = wave_ref.shape
-    half = frames // 2
-    per_clip = half // LANES
-    width = conv_ref.shape[1]
-    groups = table_ref.shape[0] // width
+    sets, per_clip = wave_ref.shape[:2]
+    half = per_clip * LANES
+    frames = 2 * half
+    width = 64
+    groups = 2 * (weight_ref.shape[1] - 4 * width - 16) // width
+    table_rows = groups // 2 * width
     per_tile = TILE // LANES
-    rank = rank_ref[0]
+
+    def weight(part, start, rows, first, columns):
+        start += table_rows
+        return weight_ref[part, start : start + rows, first : first + columns]
+
+    conv = [weight(part, 0, width, 0, 3 * width) for part in range(2)]
+    conv_t = [weight(part, width, width, 0, 3 * width) for part in range(2)]
+    point = [weight(k // 2, 2 * width, width, k % 2 * width, width) for k in range(4)]
+    point_t = [weight(k // 2, 2 * width, width, (2 + k % 2) * width, width) for k in range(4)]
+    edge = [weight(part, 3 * width, width, 0, 16) for part in range(2)]
+    edge_t = [weight(part, 4 * width, 16, 0, width) for part in range(2)]
 
     for ref in (
         sig_r, msk_r, live_r, me_r, strips_r, onehot_r, hi_r, hidden_r, actu_e_r, chosen_r,
@@ -113,15 +120,13 @@
     for ref in (g_conv, g_point, g_edge, g_table, loss_ref):
         ref[...] = jnp.zeros(ref.shape, ref.dtype)
 
-    row_at = lax.broadcasted_iota(jnp.int32, (2 * LANES, 2 * LANES), 0)
-    col_at = lax.broadcasted_iota(jnp.int32, (2 * LANES, 2 * LANES), 1)
-    wanted = jnp.where(col_at < LANES, 2 * col_at, 2 * (col_at - LANES) + 1)
-    split = jnp.where(row_at == wanted, 1.0, 0.0).astype(BF16)
-    for block in range(per_clip):
-        parted = nn(wave_ref[:, block * 2 * LANES : (block + 1) * 2 * LANES], split)
-        even_scr[block] = parted[:, :LANES]
-        odd_scr[block] = parted[:, LANES:]
-        code_scr[block] = ids_ref[:, block * LANES : (block + 1) * LANES]
+    for k in range(sets):
+        for block in range(per_clip):
+            rows = slice(8 * k, 8 * k + 8)
+            parted = wave_ref[k, block].astype(F32)
+            even_scr[block, rows] = parted[:8]
+            odd_scr[block, rows] = parted[8:]
+            code_scr[block, rows] = ids_ref[k, block]
 
     def put(index, source, length):
         src_list[index] = source
@@ -129,21 +134,21 @@
 
     put(0, 0, -frames)
 
-    def add_clip(c, filled):
-        clip = 2 * c + rank
-        length = len_ref[clip]
+    def add_clip(c, carry):
+        filled, count = carry
+        length = len_ref[jnp.bitwise_and(c, 8), jnp.bitwise_and(c, 7)]
         blocks = lax.shift_right_logical(
             lax.shift_right_logical(length + 1, 1) + (SPARE + LANES - 1), 7
         )
 
         def add_block(k, carry):
-            put(filled + k, clip * 32 + k, length)
+            put(filled + k, c * 32 + k, length)
             return carry
 
         lax.fori_loop(0, blocks, add_block, 0)
-        return filled + blocks
-
-    filled = lax.fori_loop(0, clips // 2, add_clip, jnp.int32(1))
+        return filled + blocks, count + length
+
+    filled, count = lax.fori_loop(0, 8 * sets, add_clip, (jnp.int32(1), jnp.int32(0)))
     tiles = lax.div(filled - 1 + per_tile - 1, jnp.int32(per_tile)) + 4
 
     def add_empty(k, carry):
@@ -157,6 +162,8 @@
     sub_ext = lax.broadcasted_iota(jnp.int32, (8, TILE + 2 * LANES), 0)
     sub_tile = lax.broadcasted_iota(jnp.int32, (8, TILE), 0)
     iota16 = lax.broadcasted_iota(jnp.int32, (16, TILE), 0).astype(F32).astype(BF16)
+
+    table = jnp.concatenate([weight_ref[part, :table_rows] for part in range(2)], axis=0)
 
     def taps(ext):
         later = moved(ext, 1)
@@ -231,7 +238,7 @@
         sig_ext = jnp.concatenate(sigs, axis=1)
         live0 = jnp.concatenate(lives, axis=1)
         strips = (taps(sig_ext) * stack(live0, 2)).astype(BF16)
-        hidden = nn(edge_ref[0], strips)
+        hidden = nn(edge[0], strips)
         actu_e = relu_bf(hidden)
 
         low16 = stack(jnp.concatenate(los, axis=1), 2).astype(BF16) - iota16
@@ -242,7 +249,7 @@
             ],
             axis=0,
         )
-        picked = nn(table_ref[...], onehot)
+        picked = nn(table, onehot)
         hi0 = jnp.concatenate(his, axis=1)
         parts = [jnp.zeros((8, TILE), F32) for _ in range(width // 8)]
         for h in range(groups):
@@ -252,7 +259,7 @@
                 for r in range(width // 8)
             ]
         chosen = jnp.concatenate(parts, axis=0).astype(BF16)
-        decin = nn(point_ref[2], chosen)
+        decin = nn(point[2], chosen)
         actu_d = relu_bf(decin)
 
         keep(sig_r, 0, moved(sig_ext, 0))
@@ -276,9 +283,9 @@
             whole = jnp.concatenate([*pair, following], axis=1)
             return jnp.concatenate([moved(whole, d) for d in (REACH, 0, -REACH)], axis=0)
 
-        actp_e = relu_bf(nn(conv_ref[0], spread(e2_actu_e, actu_e[:, :LANES])))
-        encres = (hidden1 + nn(point_ref[0], actp_e)).astype(BF16)
-        latent = nn(point_ref[1], encres).astype(BF16)
+        actp_e = relu_bf(nn(conv[0], spread(e2_actu_e, actu_e[:, :LANES])))
+        encres = (hidden1 + nn(point[0], actp_e)).astype(BF16)
+        latent = nn(point[1], encres).astype(BF16)
         gap = (latent.astype(F32) - chosen1.astype(F32)) * stack(me1, width // 8)
         gap_bf = gap.astype(BF16)
         square = gap * gap
@@ -294,9 +301,9 @@
             ]
         g_table[...] += nt(jnp.concatenate(terms, axis=0), onehot1)
 
-        actp_d = relu_bf(nn(conv_ref[1], spread(e2_actu_d, actu_d[:, :LANES])))
-        resb = (decin1 + nn(point_ref[3], actp_d)).astype(BF16)
-        outs = nn(edge_t_ref[1], resb)
+        actp_d = relu_bf(nn(conv[1], spread(e2_actu_d, actu_d[:, :LANES])))
+        resb = (decin1 + nn(point[3], actp_d)).astype(BF16)
+        outs = nn(edge_t[1], resb)
         keep(actp_e_r, 1, actp_e)
         keep(encres_r, 1, encres)
         keep(gap_r, 1, gap * (2.0 * COMMIT))
@@ -318,38 +325,62 @@
             loss_sum = loss_sum + loss_rows[:, j * LANES : (j + 1) * LANES]
         loss_ref[...] += loss_sum
         douts = (2.0 * taps(error) * stack(live2, 2)).astype(BF16)
-        g_edge[1] += nt(resb2, douts)
-        dres = nn(edge_ref[1], douts)
+        g_edge[1] += nt(douts, resb2)
+        dres = nn(edge[1], douts)
         dbranch = dres.astype(BF16)
         g_point[3] += nt(dbranch, actp_d2)
-        dinner_d = jnp.where(actp_d2 > 0, nn(point_t_ref[3], dbranch).astype(BF16), 0)
+        dinner_d = jnp.where(actp_d2 > 0, nn(point_t[3], dbranch).astype(BF16), 0)
         keep(dres_r, 2, dres)
         keep(dinner_d_r, 2, dinner_d)
 
         around = spread_back(e4_din, dinner_d[:, :LANES])
         g_conv[1] += nt(around, actu_d3)
-        ddecin = (dres3 + jnp.where(actu_d3 > 0, nn(conv_t_ref[1], around), 0.0)).astype(BF16)
+        ddecin = (dres3 + jnp.where(actu_d3 > 0, nn(conv_t[1], around), 0.0)).astype(BF16)
         g_point[2] += nt(ddecin, chosen3)
-        dlatent = (nn(point_t_ref[2], ddecin) + gap3).astype(BF16)
+        dlatent = (nn(point_t[2], ddecin) + gap3).astype(BF16)
         g_point[1] += nt(dlatent, encres3)
-        denc = nn(point_t_ref[1], dlatent)
+        denc = nn(point_t[1], dlatent)
         dbranch_e = denc.astype(BF16)
         g_point[0] += nt(dbranch_e, actp_e3)
-        dinner_e = jnp.where(actp_e3 > 0, nn(point_t_ref[0], dbranch_e).astype(BF16), 0)
+        dinner_e = jnp.where(actp_e3 > 0, nn(point_t[0], dbranch_e).astype(BF16), 0)
         keep(denc_r, 3, denc)
         keep(dinner_e_r, 3, dinner_e)
 
         around_e = spread_back(e5_din, dinner_e[:, :LANES])
         g_conv[0] += nt(around_e, actu_e4)
-        dhidden = (denc4 + jnp.where(actu_e4 > 0, nn(conv_t_ref[0], around_e), 0.0)).astype(BF16)
-        g_edge[0] += nt(dhidden, strips4)
-
-
-def net(rank, lengths, waveform, code_ids, conv, conv_t, point, point_t, edge, edge_t, table):
-    clips, frames = waveform.shape
-    width = conv.shape[1]
+        dhidden = (denc4 + jnp.where(actu_e4 > 0, nn(conv_t[0], around_e), 0.0)).astype(BF16)
+        g_edge[0] += nt(strips4, dhidden)
+
+    first = jnp.where((sub == 0) & (lane == 0), count, 0).astype(F32)
+    stats_ref[...] = jnp.concatenate([loss_ref[...], first], axis=0)
+    rows = groups // 2 * width
+    for part in range(2):
+        payload_ref[part, :rows] = g_table[part * rows : (part + 1) * rows, :LANES]
+        payload_ref[part, rows : 2 * rows] = g_table[part * rows : (part + 1) * rows, LANES:]
+        conv_rows = [g_conv[part, k * width : (k + 1) * width] for k in range(3)]
+        edge_rows = jnp.concatenate(
+            [g_edge[part], jnp.zeros((width - 16, width), F32)], axis=0
+        )
+        after = 2 * rows
+        for pair in (
+            conv_rows[:2],
+            (conv_rows[2], edge_rows),
+            (g_point[2 * part], g_point[2 * part + 1]),
+        ):
+            payload_ref[part, after : after + width] = jnp.concatenate(pair, axis=1)
+            after += width
+        rest = payload_ref.shape[1] - after
+        if rest:
+            payload_ref[part, after:] = jnp.zeros((rest, LANES), F32)
+
+
+def net(rows, lengths, wave, codes, weights):
+    sets, per_clip = wave.shape[:2]
+    clips = 8 * sets
+    width = 64
+    table_rows = 2 * (weights.shape[1] - 4 * width - 16)
     columns = SLOTS * TILE
-    listed = (clips // 2) * (frames // 2 // LANES + 1) + 8 * (TILE // LANES) + 8
+    listed = clips * (per_clip + 1) + 8 * (TILE // LANES) + 8
     smem = pl.BlockSpec(memory_space=pltpu.SMEM)
     vmem = pl.BlockSpec(memory_space=pltpu.VMEM)
 
@@ -359,20 +390,22 @@
     return pl.pallas_call(
         net_kernel,
         out_shape=(
-            jax.ShapeDtypeStruct((2, 3 * width, width), F32),
-            jax.ShapeDtypeStruct((4, width, width), F32),
-            jax.ShapeDtypeStruct((2, width, 16), F32),
-            jax.ShapeDtypeStruct(table.shape, F32),
-            jax.ShapeDtypeStruct((8, LANES), F32),
+            jax.ShapeDtypeStruct((2, rows, LANES), F32),
+            jax.ShapeDtypeStruct((16, LANES), F32),
         ),
-        in_specs=[smem, smem] + [vmem] * 9,
-        out_specs=(vmem,) * 5,
+        in_specs=[smem] + [vmem] * 3,
+        out_specs=(vmem,) * 2,
         scratch_shapes=[
+            pltpu.VMEM((2, 3 * width, width), F32),
+            pltpu.VMEM((4, width, width), F32),
+            pltpu.VMEM((2, 16, width), F32),
+            pltpu.VMEM((table_rows, LOW), F32),
+            pltpu.VMEM((8, LANES), F32),
             pltpu.SMEM((listed,), jnp.int32),
             pltpu.SMEM((listed,), jnp.int32),
-            pltpu.VMEM((frames // 2 // LANES, clips, LANES), F32),
-            pltpu.VMEM((frames // 2 // LANES, clips, LANES), F32),
-            pltpu.VMEM((frames // 2 // LANES, clips, LANES), jnp.int32),
+            pltpu.VMEM((per_clip, clips, LANES), F32),
+            pltpu.VMEM((per_clip, clips, LANES), F32),
+            pltpu.VMEM((per_clip, clips, LANES), jnp.int32),
             ring(8, F32),
             ring(8, F32),
             ring(8, F32),
@@ -397,14 +430,354 @@
             ring(width, BF16),
         ],
         compiler_params=pltpu.CompilerParams(vmem_limit_bytes=48 * 2**20),
-    )(rank, lengths, waveform, code_ids, conv, conv_t, point, point_t, edge, edge_t, table)
-
-
-def nesterov(weight, grad, moment, average, rate):
-    moment_new = MOMENTUM * moment + grad
-    weight_new = weight - rate * (grad + MOMENTUM * moment_new)
-    average_new = AVERAGE * average + (1.0 - AVERAGE) * weight_new
-    return (weight_new, moment_new, average_new, weight_new.astype(jnp.bfloat16))
+    )(lengths, wave, codes, weights)
+
+
+def remote(src, dst, send, recv, to):
+    return pltpu.make_async_remote_copy(
+        src_ref=src, dst_ref=dst, send_sem=send, recv_sem=recv, device_id=to, device_id_type=MESH
+    )
+
+
+def share_kernel(
+    items,
+    len_ref,
+    wave_ref,
+    ids_ref,
+    conv_ref,
+    point_ref,
+    edge_ref,
+    table_ref,
+    len_out,
+    wave_out,
+    ids_out,
+    weight_out,
+    len_scr,
+    wave_scr,
+    ids_scr,
+    weight_scr,
+    sems,
+):
+    item = lax.axis_index("item")
+    pipe = lax.axis_index("pipe")
+    partner = (item, 1 - pipe)
+    mirror = (items - 1 - item, pipe)
+    per_clip = wave_out.shape[1]
+    width = conv_ref.shape[1]
+    table_rows = weight_scr.shape[1] - 4 * width - 16
+
+    barrier = pltpu.get_barrier_semaphore()
+    for other in (partner, mirror):
+        pl.semaphore_signal(barrier, inc=1, device_id=other, device_id_type=MESH)
+
+    row_at = lax.broadcasted_iota(jnp.int32, (2 * LANES, 2 * LANES), 0)
+    col_at = lax.broadcasted_iota(jnp.int32, (2 * LANES, 2 * LANES), 1)
+    wanted = jnp.where(col_at < LANES, 2 * col_at, 2 * (col_at - LANES) + 1)
+    split = jnp.where(row_at == wanted, 1.0, 0.0).astype(BF16)
+    on_first = pipe == 0
+    lane = lax.broadcasted_iota(jnp.int32, (8, LANES), 1)
+    kept = jnp.zeros((8, LANES), jnp.int32)
+    given = kept
+    for k in range(8):
+        kept = jnp.where(lane == k, jnp.where(on_first, len_ref[k], len_ref[8 + k]), kept)
+        given = jnp.where(lane == k, jnp.where(on_first, len_ref[24 + k], len_ref[16 + k]), given)
+    len_out[:8] = kept
+    len_scr[0] = given
+    for block in range(per_clip):
+        parted = nn(wave_ref[:, block * 2 * LANES : (block + 1) * 2 * LANES], split)
+        codes = ids_ref[:, block * LANES : (block + 1) * LANES]
+        even, odd = parted[:, :LANES], parted[:, LANES:]
+
+        def chosen(values, first, second):
+            return jnp.where(on_first, values[8 * first :][:8], values[8 * second :][:8])
+
+        def both(first, second):
+            return jnp.concatenate(
+                [chosen(even, first, second), chosen(odd, first, second)], axis=0
+            ).astype(BF16)
+
+        wave_out[0, block] = both(0, 1)
+        wave_scr[0, block] = both(3, 2)
+        ids_out[0, block] = chosen(codes, 0, 1)
+        ids_scr[0, block] = chosen(codes, 3, 2)
+
+    pl.semaphore_wait(barrier, 2)
+    copies = [
+        remote(ref.at[0], ref.at[1], sems.at[2 * k], sems.at[2 * k + 1], mirror)
+        for k, ref in enumerate((len_scr, wave_scr, ids_scr))
+    ]
+    for copy in copies:
+        copy.start()
+
+    groups = table_rows // width
+    for h in range(groups):
+        weight_scr[0, h * width : (h + 1) * width] = table_ref[:, h * LOW : (h + 1) * LOW].astype(
+            BF16
+        )
+    blank = jnp.zeros((width, LOW - 3 * width), F32)
+    conv = conv_ref[0]
+    conv_t = [conv[:, k * width : (k + 1) * width].T for k in range(3)]
+    points = [point_ref[0, 0], point_ref[0, 1]]
+    edge = edge_ref[0]
+    empty = jnp.zeros((6, width), F32)
+    edge_t = jnp.concatenate([edge[1:3], empty, edge[3:], edge[:1], empty], axis=0)
+    edge_square = jnp.concatenate([edge_t, jnp.zeros((width - 16, width), F32)], axis=0).T
+    after = table_rows
+    for pieces in (
+        [conv, blank],
+        conv_t + [blank],
+        points + [value.T for value in points],
+        [edge_square, jnp.zeros((width, LOW - width), F32)],
+        [edge_t, jnp.zeros((16, LOW - width), F32)],
+    ):
+        value = jnp.concatenate(pieces, axis=1).astype(BF16)
+        weight_scr[0, after : after + value.shape[0]] = value
+        after += value.shape[0]
+    over = remote(weight_scr.at[0], weight_scr.at[1], sems.at[6], sems.at[7], partner)
+    over.start()
+    weight_out[pipe] = weight_scr[0]
+    over.wait()
+    weight_out[1 - pipe] = weight_scr[1]
+    for copy in copies:
+        copy.wait()
+    len_out[8:] = len_scr[1]
+    wave_out[1] = wave_scr[1]
+    ids_out[1] = ids_scr[1]
+
+
+def shared(items, lengths, waveform, code_ids, conv, point, edge, table):
+    per_clip = code_ids.shape[1] // LANES
+    width = conv.shape[1]
+    weight_rows = table.shape[1] // LOW * width + 4 * width + 16
+    smem = pl.BlockSpec(memory_space=pltpu.SMEM)
+    vmem = pl.BlockSpec(memory_space=pltpu.VMEM)
+    wave_shape = (2, per_clip, 16, LANES)
+    ids_shape = (2, per_clip, 8, LANES)
+    weight_shape = (2, weight_rows, LOW)
+    return pl.pallas_call(
+        functools.partial(share_kernel, items),
+        out_shape=(
+            jax.ShapeDtypeStruct((16, LANES), jnp.int32),
+            jax.ShapeDtypeStruct(wave_shape, BF16),
+            jax.ShapeDtypeStruct(ids_shape, jnp.int32),
+            jax.ShapeDtypeStruct(weight_shape, BF16),
+        ),
+        in_specs=[smem] + [vmem] * 6,
+        out_specs=(vmem,) * 4,
+        scratch_shapes=[
+            pltpu.VMEM((2, 8, LANES), jnp.int32),
+            pltpu.VMEM(wave_shape, BF16),
+            pltpu.VMEM(ids_shape, jnp.int32),
+            pltpu.VMEM(weight_shape, BF16),
+            pltpu.SemaphoreType.DMA((8,)),
+        ],
+        compiler_params=pltpu.CompilerParams(
+            collective_id=0, has_side_effects=True, vmem_limit_bytes=16 * 2**20
+        ),
+    )(lengths, waveform, code_ids, conv, point, edge, table)
+
+
+def sum_kernel(
+    items,
+    payload_ref,
+    stats_ref,
+    sum_ref,
+    stats_out,
+    crossed,
+    crossed_stats,
+    part,
+    part_stats,
+    landed,
+    landed_stats,
+    whole,
+    cross_sem,
+    out_send,
+    out_recv,
+    stats_send,
+    stats_recv,
+    back_send,
+    back_recv,
+):
+    item = lax.axis_index("item")
+    pipe = lax.axis_index("pipe")
+    partner = (item, 1 - pipe)
+    piece = part.shape[1]
+
+    def peer(d):
+        return lax.rem(item + d, items)
+
+    barrier = pltpu.get_barrier_semaphore()
+    pl.semaphore_signal(barrier, inc=1, device_id=partner, device_id_type=MESH)
+
+    @pl.loop(1, items)
+    def _(d):
+        pl.semaphore_signal(barrier, inc=1, device_id=(peer(d), pipe), device_id_type=MESH)
+
+    pl.semaphore_wait(barrier, items)
+
+    over = remote(payload_ref.at[1 - pipe], crossed, cross_sem.at[0], cross_sem.at[1], partner)
+    over_stats = remote(stats_ref, crossed_stats, cross_sem.at[2], cross_sem.at[3], partner)
+    over.start()
+    over_stats.start()
+    over_stats.wait()
+    part_stats[...] = stats_ref[...] + crossed_stats[...]
+    over.wait()
+
+    def out_copy(to):
+        return remote(
+            part.at[to], landed.at[item], out_send.at[to], out_recv.at[item], (to, pipe)
+        )
+
+    def out_copy_stats(to):
+        return remote(
+            part_stats, landed_stats.at[item], stats_send.at[to], stats_recv.at[item], (to, pipe)
+        )
+
+    def add_up(k):
+        rows = pl.ds(pl.multiple_of(k * piece, piece), piece)
+        return payload_ref[pipe, rows] + crossed[rows]
+
+    @pl.loop(1, items)
+    def _(d):
+        to = peer(d)
+        part[to] = add_up(to).astype(BF16)
+        out_copy(to).start()
+        out_copy_stats(to).start()
+
+    total = add_up(item)
+
+    def take(d, carry):
+        total, stats = carry
+        source = peer(items - d)
+        remote(
+            part.at[source], landed.at[source], out_send.at[source], out_recv.at[source],
+            (source, pipe),
+        ).wait_recv()
+        remote(
+            part_stats, landed_stats.at[source], stats_send.at[source], stats_recv.at[source],
+            (source, pipe),
+        ).wait_recv()
+        return total + landed[source].astype(F32), stats + landed_stats[source]
+
+    total, stats = lax.fori_loop(1, items, take, (total, part_stats[...]))
+    whole[item] = total.astype(BF16)
+    stats_out[...] = stats
+
+    def back_copy(place, slot, to):
+        return remote(
+            whole.at[place], whole.at[place], back_send.at[slot], back_recv.at[place], (to, pipe)
+        )
+
+    @pl.loop(1, items)
+    def _(d):
+        to = peer(d)
+        back_copy(item, to, to).start()
+
+    own = pl.ds(pl.multiple_of(item * piece, piece), piece)
+    sum_ref[own] = total.astype(BF16).astype(F32)
+
+    @pl.loop(1, items)
+    def _(d):
+        source = peer(items - d)
+        back_copy(source, source, source).wait_recv()
+        rows = pl.ds(pl.multiple_of(source * piece, piece), piece)
+        sum_ref[rows] = whole[source].astype(F32)
+
+    @pl.loop(1, items)
+    def _(d):
+        to = peer(d)
+        out_copy(to).wait_send()
+        out_copy_stats(to).wait_send()
+        back_copy(item, to, to).wait_send()
+
+
+def summed(items, payload, stats):
+    rows = payload.shape[1]
+    piece = rows // items
+    vmem = pl.BlockSpec(memory_space=pltpu.VMEM)
+    sems = pltpu.SemaphoreType.DMA((items,))
+    return pl.pallas_call(
+        functools.partial(sum_kernel, items),
+        out_shape=(
+            jax.ShapeDtypeStruct((rows, LANES), F32),
+            jax.ShapeDtypeStruct(stats.shape, F32),
+        ),
+        in_specs=[vmem] * 2,
+        out_specs=(vmem,) * 2,
+        scratch_shapes=[
+            pltpu.VMEM((rows, LANES), F32),
+            pltpu.VMEM(stats.shape, F32),
+            pltpu.VMEM((items, piece, LANES), BF16),
+            pltpu.VMEM(stats.shape, F32),
+            pltpu.VMEM((items, piece, LANES), BF16),
+            pltpu.VMEM((items,) + stats.shape, F32),
+            pltpu.VMEM((items, piece, LANES), BF16),
+            pltpu.SemaphoreType.DMA((4,)),
+        ]
+        + [sems] * 6,
+        compiler_params=pltpu.CompilerParams(
+            collective_id=1, has_side_effects=True, vmem_limit_bytes=16 * 2**20
+        ),
+    )(payload, stats)
+
+
+def update_kernel(*refs):
+    rate_net, rate_code, sum_ref, stats_ref = refs[:4]
+    states = refs[4:16]
+    loss_ref = refs[16]
+    results = refs[17:]
+    width = states[0].shape[1]
+    count = jnp.sum(stats_ref[8:], keepdims=True)
+    loss_ref[0] = jnp.sum(stats_ref[:8]) / jnp.sum(stats_ref[8:])
+    scale = 1.0 / count
+
+    def step(kind, place, grad, rate):
+        weight_ref, moment_ref, average_ref = (states[4 * j + kind] for j in range(3))
+        new_ref, moment_new_ref, average_new_ref, copy_ref = results[4 * kind : 4 * kind + 4]
+        grad = grad * scale
+        moment = MOMENTUM * moment_ref[place] + grad
+        weight = weight_ref[place] - rate * (grad + MOMENTUM * moment)
+        new_ref[place] = weight
+        moment_new_ref[place] = moment
+        average_new_ref[place] = AVERAGE * average_ref[place] + (1.0 - AVERAGE) * weight
+        copy_ref[place] = weight.astype(BF16)
+
+    groups = states[3].shape[1] // LOW
+    rows = groups * width
+    for h in range(groups):
+        for side in range(LOW // LANES):
+            start = h * LOW + side * LANES
+            grad = sum_ref[side * rows + h * width : side * rows + (h + 1) * width]
+            place = (slice(None), slice(start, start + LANES))
+            step(3, place, grad * (-2.0 * COMMIT), rate_code[0])
+    first, second, third = (
+        sum_ref[2 * rows + k * width : 2 * rows + (k + 1) * width] for k in range(3)
+    )
+    rate = rate_net[0]
+    step(0, 0, jnp.concatenate([first, second[:, :width]], axis=1), rate)
+    step(1, (0, 0), third[:, :width], rate)
+    step(1, (0, 1), third[:, width:], rate)
+    edge = [second[k : k + 1, width:] for k in (9, 0, 1, 8)]
+    step(2, 0, jnp.concatenate(edge, axis=0), rate)
+
+
+def updated(rates, sums, stats, states):
+    smem = pl.BlockSpec(memory_space=pltpu.SMEM)
+    shapes = [jax.ShapeDtypeStruct((1,), F32)]
+    for weight in states[:4]:
+        shapes += [jax.ShapeDtypeStruct(weight.shape, F32)] * 3
+        shapes += [jax.ShapeDtypeStruct(weight.shape, BF16)]
+    def block(value):
+        return pl.BlockSpec(value.shape, lambda i: (0,) * len(value.shape))
+
+    return pl.pallas_call(
+        update_kernel,
+        grid=(1,),
+        out_shape=tuple(shapes),
+        in_specs=[smem] * 2 + [block(value) for value in (sums, stats, *states)],
+        out_specs=(smem,) + tuple(block(value) for value in shapes[1:]),
+        compiler_params=pltpu.CompilerParams(vmem_limit_bytes=24 * 2**20),
+    )(*rates, sums, stats, *states)
 
 
 def per_device(
@@ -427,51 +800,22 @@
     rate_code,
 ):
     width = conv_w.shape[1]
-    rank = lax.axis_index("pipe").reshape(1).astype(jnp.int32)
-    own_rows = codebook.shape[0]
-
-    def gathered(block):
-        return lax.all_gather(block, "pipe", axis=0, tiled=True)
-
-    own_table = codebook.astype(BF16).reshape(own_rows // LOW, LOW, width)
-    own_table = jnp.swapaxes(own_table, 1, 2).reshape(own_rows // LOW * width, LOW)
-    table = gathered(own_table)
-    conv = gathered(conv_w.astype(BF16))
-    point = gathered(point_w.astype(BF16).reshape(2, width, width))
-    edge = gathered(edge_w.astype(BF16))
-    conv_t = jnp.transpose(conv.reshape(2, width, 3, width), (0, 3, 2, 1)).reshape(conv.shape)
-    point_t = jnp.swapaxes(point, 1, 2)
-    gaps = jnp.zeros((2, width, 6), BF16)
-    edge16 = jnp.concatenate([edge[:, :, 1:3], gaps, edge[:, :, 3:], edge[:, :, :1], gaps], -1)
-    edge16_t = jnp.swapaxes(edge16, 1, 2)
-
-    g_conv, g_point, g_edge, g_table, loss_rows = net(
-        rank, lengths, waveform, code_ids, conv, conv_t, point, point_t, edge16, edge16_t, table
+    items = lax.axis_size("item")
+    edge_w, edge_mom, edge_avg = (jnp.swapaxes(v, 1, 2) for v in (edge_w, edge_mom, edge_avg))
+    codebook, code_mom, code_avg = (v.T for v in (codebook, code_mom, code_avg))
+    rows = 2 * (codebook.shape[1] // LOW) * width + 3 * width
+    piece = -(-rows // (16 * items)) * 16
+    own_inputs = shared(items, lengths, waveform, code_ids, conv_w, point_w, edge_w, codebook)
+    payload, stats = net(piece * items, *own_inputs)
+    sums, stats = summed(items, payload, stats)
+    states = (
+        conv_w, point_w, edge_w, codebook,
+        conv_mom, point_mom, edge_mom, code_mom,
+        conv_avg, point_avg, edge_avg, code_avg,
     )
-    code_grad = lax.psum_scatter(g_table, "pipe", scatter_dimension=0, tiled=True)
-    code_grad = lax.psum(code_grad, "item")
-    net_grad = jnp.concatenate(
-        [g_conv.reshape(2, -1), g_point.reshape(2, -1), g_edge.reshape(2, -1)], axis=1
-    )
-    net_grad = lax.psum_scatter(net_grad, "pipe", scatter_dimension=0, tiled=True)
-    net_grad, count_all = lax.psum((net_grad[0], jnp.sum(lengths).astype(F32)), "item")
-    loss_sum = lax.psum(jnp.sum(loss_rows), ("item", "pipe"))
-
-    sizes = (3 * width * width, 2 * width * width)
-    conv_grad = net_grad[: sizes[0]].reshape(3, width, width)
-    conv_grad = jnp.transpose(conv_grad, (1, 0, 2)).reshape(1, width, 3 * width)
-    point_grad = net_grad[sizes[0] : sizes[0] + sizes[1]].reshape(1, 2, width, width)
-    edge_grad = net_grad[sizes[0] + sizes[1] :].reshape(1, width, 16)
-    edge_grad = jnp.concatenate(
-        [edge_grad[:, :, 9:10], edge_grad[:, :, :2], edge_grad[:, :, 8:9]], -1
-    )
-    code_grad = code_grad.reshape(own_rows // LOW, width, LOW)
-    code_grad = jnp.swapaxes(code_grad, 1, 2).reshape(own_rows, width) * (-2.0 * COMMIT)
-    conv_out = nesterov(conv_w, conv_grad / count_all, conv_mom, conv_avg, rate_net[0])
-    point_out = nesterov(point_w, point_grad / count_all, point_mom, point_avg, rate_net[0])
-    edge_out = nesterov(edge_w, edge_grad / count_all, edge_mom, edge_avg, rate_net[0])
-    code_out = nesterov(codebook, code_grad / count_all, code_mom, code_avg, rate_code[0])
-    return (loss_sum / count_all, *conv_out, *point_out, *edge_out, *code_out)
+    loss, *rest = updated((rate_net, rate_code), sums, stats, states)
+    edges = (jnp.swapaxes(v, 1, 2) for v in rest[8:12])
+    return (loss.reshape(()), *rest[:8], *edges, *(v.T for v in rest[12:]))
 
 
 def solution(mesh):

time: 354 us -> 160 us (0.45)
  waiting for transfers between devices: 157 us -> 0 us
  blocking collectives: 89.9 us -> 0 us
  Pallas kernels: 64.1 us -> 153 us
  between operations: 18.4 us -> 2.16 us
  other arithmetic: 10.9 us -> 0 us
  local copies, waits for them, and re-layouts: 12 us -> 5.84 us
    unnamed x4 -> x0, waiting for transfers between devices: 120 us -> none
    pallas_call x1 -> x4, Pallas kernels: 64.1 us -> 153 us  [the longest x1 106 us: net(): pl.pallas_call(net_kernel, out_shape=(jax.ShapeDtypeStruct((2, rows, LANE...]
    psum x2 -> x0, blocking collectives: 82.2 us -> none  [the longest x1 41.3 us: per_device(): lax.psum((net_grad[0], jnp.sum(lengths).astype(F32)), 'item')]
    psum x1 -> x0, waiting for transfers between devices: 27.8 us -> none  [per_device(): lax.psum((net_grad[0], jnp.sum(lengths).astype(F32)), 'item')]
    reduce_scatter x1 -> x0, waiting for transfers between devices: 9.15 us -> none  [per_device(): lax.psum_scatter(g_table, 'pipe', scatter_dimension=0, tiled=True)]
    all_gather x4 -> x0, blocking collectives: 7.72 us -> none  [gathered(): return lax.all_gather(block, 'pipe', axis=0, tiled=True)]
    unnamed x49 -> x36, local copies, waits for them, and re-layouts: 9.7 us -> 5.84 us
  transfers between devices with their start and end apart: 3 -> 0, of which waited for: 3 -> 0; matrix products, arithmetic and copies ran while one was open for 1% -> 0% of each run, Pallas kernels for 0% -> 0%
where the time goes in v2:
time: 160 us; the launch traced here: 161 us
  Pallas kernels  153 us (96%)
  local copies, waits for them, and re-layouts  5.84 us (4%)
  between operations  2.16 us (1%)
    pallas_call x1, Pallas kernels, net(): pl.pallas_call(net_kernel, out_shape=(jax.ShapeDtypeStruct((2, rows, LANE...  106 us
    pallas_call x1, Pallas kernels, summed(): pl.pallas_call(functools.partial(sum_kernel, items), out_shape=(jax.Shape...  33.3 us
    pallas_call x1, Pallas kernels, shared(): pl.pallas_call(functools.partial(share_kernel, items), out_shape=(jax.Sha...  11.9 us
    unnamed x36, local copies, waits for them, and re-layouts  5.84 us

profile of v2, /device:TPU:0, one launch (start us, length us, event | category | flops | bytes accessed | tf_op | source)
XLA Modules:
  0.0 160.7 jit_solution(6800137638282525921)
XLA Ops:
  1.9 0.0 copy-start.14
  2.0 0.0 copy-start.17
  2.0 0.7 copy-done.14
  2.6 0.0 copy-done.17
  2.6 0.9 copy-done
  3.6 0.9 copy-done.2
  4.5 0.9 copy-done.3
  5.5 0.8 copy-done.4
  6.3 0.8 copy-done.6
  7.2 11.9 %shard_map.296 = (s32[16,128]{1,0:T(8,128)S(1)}, bf16[2,16,16,128]{3,2,1,0:T(8,128)(2,1)S(1)}, s32[2,16,8,128]{3,2,1,0:T(8,128)S(1)}, bf16[2,528,256]{2,1,0:T(8,128)(2,1)S(1)}) custom-call(s32[32]{0:T(128)S(1)} %copy-done.17, bf16[32,4096]{1,0:T(8,128)(2,1)S(1)} %copy-done.2, s32[32,2048]{1,0:T(8,128)S(1)} %copy-done.3, f32[1,64,192]{2,1,0:T(8,128)S(1)} %copy-done.4, ...), custom_call_target="tpu_custom_call" | custom-call | tf_op jit(solution)/shard_map/pallas_call | solution.py:557
  19.1 0.0 copy-start.9
  19.1 0.0 copy-start.12
  19.1 0.0 copy-start.13
  19.1 106.1 %shard_map.297 = (f32[2,768,128]{2,1,0:T(8,128)S(1)}, f32[16,128]{1,0:T(8,128)S(1)}) custom-call(s32[16,128]{1,0:T(8,128)S(1)} %get-tuple-element.42.len_ref, bf16[2,16,16,128]{3,2,1,0:T(8,128)(2,1)S(1)} %get-tuple-element.43.wave_ref, s32[2,16,8,128]{3,2,1,0:T(8,128)S(1)} %get-tuple-element.44.ids_ref, bf16[2,528,256]{2,1,0:T(8,128)(2,1)S(1)} %get-tuple-element.45.weight_ref), custom_call_target="tpu_custom_call" | custom-call | tf_op jit(solution)/shard_map/pallas_call | solution.py:390
  125.3 0.0 copy-start.1
  125.3 0.0 copy-start.5
  125.3 0.0 copy-start.7
  125.3 0.0 copy-start.8
  125.3 0.0 copy-start.10
  125.3 0.0 copy-start.11
  125.3 0.0 copy-start.16
  125.3 33.3 %shard_map.298 = (f32[768,128]{1,0:T(8,128)S(1)}, f32[16,128]{1,0:T(8,128)S(1)}) custom-call(f32[2,768,128]{2,1,0:T(8,128)S(1)} %get-tuple-element.46.payload_ref, f32[16,128]{1,0:T(8,128)S(1)} %get-tuple-element.47.stats_ref), custom_call_target="tpu_custom_call" | custom-call | tf_op jit(solution)/shard_map/pallas_call | solution.py:699
  158.6 0.0 copy-start.15
  158.6 0.0 copy-done.9
  158.7 0.0 copy-done.12
  158.7 0.0 copy-done.13
  158.7 0.0 copy-done.1
  158.7 0.0 copy-done.5
  158.7 0.0 copy-done.7
  158.7 0.0 copy-done.8
  158.7 0.6 copy-done.15
  159.3 1.4 shard_map.299
  (8 shorter events, 0.0 us)
Async XLA Ops:
  1.9 0.7 copy-start.14
  2.0 0.7 copy-start.17
  2.6 1.0 copy-start
  3.6 0.9 copy-start.2
  4.5 0.9 copy-start.3
  5.5 0.8 copy-start.4
  6.3 0.8 copy-start.6
  19.1 139.6 %copy-start.9 = (f32[1024,64]{0,1:T(8,128)S(1)}, f32[1024,64]{0,1:T(8,128)}, u32[]{:S(2)}) copy-start(f32[1024,64]{0,1:T(8,128)} %param.31) | copy-start | bytes 786436
  19.1 139.6 %copy-start.12 = (f32[1,64,192]{2,1,0:T(8,128)S(1)}, f32[1,64,192]{2,1,0:T(8,128)}, u32[]{:S(2)}) copy-start(f32[1,64,192]{2,1,0:T(8,128)} %refs_12_.1) | copy-start | bytes 147460
  19.1 139.5 %copy-start.13 = (f32[1,2,64,64]{3,2,1,0:T(8,128)S(1)}, f32[1,2,64,64]{3,2,1,0:T(8,128)}, u32[]{:S(2)}) copy-start(f32[1,2,64,64]{3,2,1,0:T(8,128)} %refs_13_.1) | copy-start | bytes 98308
  125.3 33.4 %copy-start.1 = (f32[1024,64]{0,1:T(8,128)S(1)}, f32[1024,64]{0,1:T(8,128)}, u32[]{:S(2)}) copy-start(f32[1024,64]{0,1:T(8,128)} %param.23) | copy-start | bytes 786436
  125.3 33.4 %copy-start.5 = (f32[1,64,192]{2,1,0:T(8,128)S(1)}, f32[1,64,192]{2,1,0:T(8,128)}, u32[]{:S(2)}) copy-start(f32[1,64,192]{2,1,0:T(8,128)} %refs_4_.1) | copy-start | bytes 147460
  125.3 33.4 %copy-start.7 = (f32[1,2,64,64]{3,2,1,0:T(8,128)S(1)}, f32[1,2,64,64]{3,2,1,0:T(8,128)}, u32[]{:S(2)}) copy-start(f32[1,2,64,64]{3,2,1,0:T(8,128)} %refs_5_.1) | copy-start | bytes 98308
  125.3 33.4 %copy-start.8 = (f32[1024,64]{0,1:T(8,128)S(1)}, f32[1024,64]{0,1:T(8,128)}, u32[]{:S(2)}) copy-start(f32[1024,64]{0,1:T(8,128)} %param.27) | copy-start | bytes 786436
  125.3 33.4 %copy-start.10 = (f32[1,64,192]{2,1,0:T(8,128)S(1)}, f32[1,64,192]{2,1,0:T(8,128)}, u32[]{:S(2)}) copy-start(f32[1,64,192]{2,1,0:T(8,128)} %refs_8_.1) | copy-start | bytes 147460
  125.3 33.4 %copy-start.11 = (f32[1,2,64,64]{3,2,1,0:T(8,128)S(1)}, f32[1,2,64,64]{3,2,1,0:T(8,128)}, u32[]{:S(2)}) copy-start(f32[1,2,64,64]{3,2,1,0:T(8,128)} %refs_9_.1) | copy-start | bytes 98308
  125.3 33.4 %copy-start.16 = (f32[1,64,4]{1,2,0:T(4,128)S(1)}, f32[1,64,4]{1,2,0:T(4,128)}, u32[]{:S(2)}) copy-start(f32[1,64,4]{1,2,0:T(4,128)} %param.30) | copy-start | bytes 3076
  158.6 0.7 copy-start.15

commit v3 on v2

--- a/solution.py
+++ b/solution.py
@@ -15,6 +15,8 @@
 LANES = 128
 TILE = 512
 SLOTS = 8
+LAG = TILE // LANES + 1
+DEPTH = -(-4 * LAG * LANES // TILE)
 LOW = 256
 SPARE = 16
 REAL = 8
@@ -58,8 +60,6 @@
     g_edge,
     g_table,
     loss_ref,
-    src_list,
-    len_list,
     even_scr,
     odd_scr,
     code_scr,
@@ -67,9 +67,11 @@
     msk_r,
     live_r,
     me_r,
+    low_r,
+    high_r,
+    hi_r,
     strips_r,
     onehot_r,
-    hi_r,
     hidden_r,
     actu_e_r,
     chosen_r,
@@ -80,6 +82,7 @@
     actp_d_r,
     resb_r,
     gap_r,
+    gapb_r,
     outs_r,
     dres_r,
     dinner_d_r,
@@ -105,17 +108,17 @@
     edge = [weight(part, 3 * width, width, 0, 16) for part in range(2)]
     edge_t = [weight(part, 4 * width, 16, 0, width) for part in range(2)]
 
-    for ref in (
-        sig_r, msk_r, live_r, me_r, strips_r, onehot_r, hi_r, hidden_r, actu_e_r, chosen_r,
-        decin_r, actu_d_r, actp_e_r, encres_r, actp_d_r, resb_r, gap_r, outs_r, dres_r,
-        dinner_d_r, denc_r, dinner_e_r,
-    ):
-
-        @pl.loop(0, SLOTS)
-        def _(slot, ref=ref):
-            ref[:, pl.ds(pl.multiple_of(slot * TILE, TILE), TILE)] = jnp.zeros(
-                (ref.shape[0], TILE), ref.dtype
-            )
+    rings = (
+        sig_r, msk_r, live_r, me_r, low_r, high_r, hi_r, strips_r, onehot_r, hidden_r, actu_e_r,
+        chosen_r, decin_r, actu_d_r, actp_e_r, encres_r, actp_d_r, resb_r, gap_r, gapb_r, outs_r,
+        dres_r, dinner_d_r, denc_r, dinner_e_r,
+    )
+    slots = SLOTS * per_tile
+
+    @pl.loop(slots - 4 * LAG - 2, slots)
+    def _(slot):
+        for ref in rings:
+            ref[slot] = jnp.zeros(ref.shape[1:], ref.dtype)
 
     for ref in (g_conv, g_point, g_edge, g_table, loss_ref):
         ref[...] = jnp.zeros(ref.shape, ref.dtype)
@@ -128,34 +131,21 @@
             odd_scr[block, rows] = parted[8:]
             code_scr[block, rows] = ids_ref[k, block]
 
-    def put(index, source, length):
-        src_list[index] = source
-        len_list[index] = length
-
-    put(0, 0, -frames)
+    clips = 8 * sets
+
+    def blocks_of(length):
+        valid = lax.shift_right_arithmetic(length + 1, 1)
+        return lax.shift_right_arithmetic(valid + (SPARE + LANES - 1), 7)
+
+    def length_of(clip):
+        return len_ref[jnp.bitwise_and(clip, 8), jnp.bitwise_and(clip, 7)]
 
     def add_clip(c, carry):
-        filled, count = carry
-        length = len_ref[jnp.bitwise_and(c, 8), jnp.bitwise_and(c, 7)]
-        blocks = lax.shift_right_logical(
-            lax.shift_right_logical(length + 1, 1) + (SPARE + LANES - 1), 7
-        )
-
-        def add_block(k, carry):
-            put(filled + k, c * 32 + k, length)
-            return carry
-
-        lax.fori_loop(0, blocks, add_block, 0)
-        return filled + blocks, count + length
-
-    filled, count = lax.fori_loop(0, 8 * sets, add_clip, (jnp.int32(1), jnp.int32(0)))
-    tiles = lax.div(filled - 1 + per_tile - 1, jnp.int32(per_tile)) + 4
-
-    def add_empty(k, carry):
-        put(filled + k, 0, -frames)
-        return carry
-
-    lax.fori_loop(0, 6 * per_tile + 2, add_empty, 0)
+        length = length_of(c)
+        return carry[0] + blocks_of(length), carry[1] + length
+
+    blocks, count = lax.fori_loop(0, clips, add_clip, (jnp.int32(0), jnp.int32(0)))
+    tiles = lax.div(blocks + per_tile - 1, jnp.int32(per_tile)) + DEPTH
 
     sub = lax.broadcasted_iota(jnp.int32, (8, LANES), 0)
     lane = lax.broadcasted_iota(jnp.int32, (8, LANES), 1)
@@ -171,185 +161,242 @@
         other = jnp.where(sub_tile == 0, later, jnp.where(sub_tile == 1, earlier, 0.0))
         return jnp.concatenate([moved(ext, 0), other], axis=0)
 
-    @pl.loop(0, tiles)
-    def _(i):
-        def at(lag):
-            return pl.multiple_of(lax.rem(i - lag + SLOTS, SLOTS) * TILE, TILE)
-
-        def cur(ref, lag):
-            return ref[:, pl.ds(at(lag), TILE)]
-
-        def last_of(ref, lag):
-            return ref[:, pl.ds(at(lag) + (TILE - LANES), LANES)]
-
-        def first_of(ref, lag):
-            return ref[:, pl.ds(at(lag), LANES)]
-
-        def ext(ref, lag, following):
-            return jnp.concatenate([last_of(ref, lag + 1), cur(ref, lag), following], axis=1)
+    def fetch(state, slot):
+        clip, place = state
+        real = clip < clips
+        length = jnp.where(real, length_of(clip), -frames)
+        row = pl.ds(jnp.minimum(clip, clips - 1), 1)
+        here = (jnp.minimum(place, per_clip - 1), row, slice(None))
+        t = place * LANES + lane
+        even_ok = 2 * t < length
+        odd_ok = 2 * t + 1 < length
+        even = jnp.broadcast_to(even_scr[here], (8, LANES))
+        odd = jnp.broadcast_to(odd_scr[here], (8, LANES))
+        code = jnp.broadcast_to(code_scr[here], (8, LANES))
+        live = t < jnp.minimum(lax.shift_right_arithmetic(length + 1, 1) + REAL, half)
+        low = jnp.where(live, jnp.bitwise_and(code, LOW - 1), -1).astype(F32)
+        high = lax.shift_right_logical(code, 8).astype(F32)
+        sig_r[slot] = jnp.where(
+            (sub == 0) & even_ok, even, jnp.where((sub == 1) & odd_ok, odd, 0.0)
+        )
+        msk_r[slot] = jnp.where(((sub == 0) & even_ok) | ((sub == 1) & odd_ok), 1.0, 0.0)
+        live_r[slot] = jnp.where(live, 1.0, 0.0)
+        me_r[slot] = jnp.where(even_ok, 1.0, 0.0)
+        low_r[slot] = stack(low, 2).astype(BF16)
+        high_r[slot] = high
+        hi_r[slot] = stack(high, 2).astype(BF16)
+        done = place + 1 >= blocks_of(length)
+        clip = jnp.where(done, jnp.minimum(clip + 1, clips), clip)
+        return clip, jnp.where(done, 0, place + 1)
+
+    state = (jnp.int32(0), jnp.int32(0))
+    for b in range(per_tile + 1):
+        state = fetch(state, b)
+
+    def tile_step(i, state):
+        def block(lag, b):
+            return jnp.bitwise_and(i * per_tile - lag + b, slots - 1)
+
+        def load(ref, lag, first=0, last=per_tile):
+            return jnp.concatenate([ref[block(lag, b)] for b in range(first, last)], axis=1)
+
+        def load_ext(ref, lag):
+            return load(ref, lag, -1, per_tile + 1)
+
+        stores = []
 
         def keep(ref, lag, value):
-            ref[:, pl.ds(at(lag), TILE)] = value
-
-        e2_actu_e = (last_of(actu_e_r, 2), cur(actu_e_r, 1))
-        e2_actu_d = (last_of(actu_d_r, 2), cur(actu_d_r, 1))
-        e3_outs = (last_of(outs_r, 3), cur(outs_r, 2))
-        e4_din = (last_of(dinner_d_r, 4), cur(dinner_d_r, 3))
-        e5_din = (last_of(dinner_e_r, 5), cur(dinner_e_r, 4))
-        chosen1, chosen3 = cur(chosen_r, 1), cur(chosen_r, 3)
-        hidden1, decin1 = cur(hidden_r, 1), cur(decin_r, 1)
-        onehot1, hi1, me1 = cur(onehot_r, 1), cur(hi_r, 1), cur(me_r, 1)
-        actp_d2, resb2 = cur(actp_d_r, 2), cur(resb_r, 2)
-        actu_d3, actp_e3, encres3, gap3, dres3 = (
-            cur(actu_d_r, 3), cur(actp_e_r, 3), cur(encres_r, 3), cur(gap_r, 3), cur(dres_r, 3)
-        )
-        actu_e4, denc4, strips4 = cur(actu_e_r, 4), cur(denc_r, 4), cur(strips_r, 4)
-        sig2 = ext(sig_r, 2, first_of(sig_r, 1))
-        msk2 = ext(msk_r, 2, first_of(msk_r, 1))
-        live2 = cur(live_r, 2)
-        live2_ext = ext(live_r, 2, first_of(live_r, 1))
-
-        sigs, msks, lives, mes, los, his = [], [], [], [], [], []
-        for j in range(-1, per_tile + 1):
-            index = i * per_tile + (j + 1)
-            source, length = src_list[index], len_list[index]
-            clip = lax.shift_right_logical(source, 5)
-            block = jnp.bitwise_and(source, 31)
-            here = (jnp.minimum(block, per_clip - 1), pl.ds(clip, 1), slice(None))
-            t = block * LANES + lane
-            even_ok = 2 * t < length
-            odd_ok = 2 * t + 1 < length
-            even = jnp.broadcast_to(even_scr[here], (8, LANES))
-            odd = jnp.broadcast_to(odd_scr[here], (8, LANES))
-            sigs.append(
-                jnp.where((sub == 0) & even_ok, even, jnp.where((sub == 1) & odd_ok, odd, 0.0))
+            stores.append((ref, lag, value))
+
+        def spread(ext, way):
+            return jnp.concatenate([moved(ext, d * way) for d in (-REACH, 0, REACH)], axis=0)
+
+        def first_step():
+            lag = 0
+            sig_ext, live0 = load_ext(sig_r, lag), load(live_r, lag)
+            hi0 = load(high_r, lag)
+            low16 = load(low_r, lag) - iota16
+            strips = (taps(sig_ext) * stack(live0, 2)).astype(BF16)
+            onehot = jnp.concatenate(
+                [
+                    jnp.where(low16 == float(16 * r), jnp.ones((), BF16), jnp.zeros((), BF16))
+                    for r in range(LOW // 16)
+                ],
+                axis=0,
             )
-            if 0 <= j < per_tile:
-                valid = lax.shift_right_arithmetic(length + 1, 1)
-                live = t < jnp.minimum(valid + REAL, half)
-                code = jnp.broadcast_to(code_scr[here], (8, LANES))
-                msks.append(
-                    jnp.where(((sub == 0) & even_ok) | ((sub == 1) & odd_ok), 1.0, 0.0)
-                )
-                lives.append(jnp.where(live, 1.0, 0.0))
-                mes.append(jnp.where(even_ok, 1.0, 0.0))
-                los.append(jnp.where(live, jnp.bitwise_and(code, LOW - 1), -1).astype(F32))
-                his.append(lax.shift_right_logical(code, 8).astype(F32))
-        sig_ext = jnp.concatenate(sigs, axis=1)
-        live0 = jnp.concatenate(lives, axis=1)
-        strips = (taps(sig_ext) * stack(live0, 2)).astype(BF16)
-        hidden = nn(edge[0], strips)
-        actu_e = relu_bf(hidden)
-
-        low16 = stack(jnp.concatenate(los, axis=1), 2).astype(BF16) - iota16
-        onehot = jnp.concatenate(
-            [
-                jnp.where(low16 == float(16 * r), jnp.ones((), BF16), jnp.zeros((), BF16))
-                for r in range(LOW // 16)
-            ],
-            axis=0,
-        )
-        picked = nn(table, onehot)
-        hi0 = jnp.concatenate(his, axis=1)
-        parts = [jnp.zeros((8, TILE), F32) for _ in range(width // 8)]
-        for h in range(groups):
-            here = hi0 == float(h)
-            parts = [
-                jnp.where(here, picked[h * width + 8 * r : h * width + 8 * r + 8], parts[r])
-                for r in range(width // 8)
-            ]
-        chosen = jnp.concatenate(parts, axis=0).astype(BF16)
-        decin = nn(point[2], chosen)
-        actu_d = relu_bf(decin)
-
-        keep(sig_r, 0, moved(sig_ext, 0))
-        keep(msk_r, 0, jnp.concatenate(msks, axis=1))
-        keep(live_r, 0, live0)
-        keep(me_r, 0, jnp.concatenate(mes, axis=1))
-        keep(hi_r, 0, stack(hi0, 2).astype(BF16))
-        keep(strips_r, 0, strips)
-        keep(onehot_r, 0, onehot)
-        keep(hidden_r, 0, hidden)
-        keep(actu_e_r, 0, actu_e)
-        keep(chosen_r, 0, chosen)
-        keep(decin_r, 0, decin)
-        keep(actu_d_r, 0, actu_d)
-
-        def spread(pair, following):
-            whole = jnp.concatenate([*pair, following], axis=1)
-            return jnp.concatenate([moved(whole, d) for d in (-REACH, 0, REACH)], axis=0)
-
-        def spread_back(pair, following):
-            whole = jnp.concatenate([*pair, following], axis=1)
-            return jnp.concatenate([moved(whole, d) for d in (REACH, 0, -REACH)], axis=0)
-
-        actp_e = relu_bf(nn(conv[0], spread(e2_actu_e, actu_e[:, :LANES])))
-        encres = (hidden1 + nn(point[0], actp_e)).astype(BF16)
-        latent = nn(point[1], encres).astype(BF16)
-        gap = (latent.astype(F32) - chosen1.astype(F32)) * stack(me1, width // 8)
-        gap_bf = gap.astype(BF16)
-        square = gap * gap
-        loss_rows = square[:8]
-        for r in range(1, width // 8):
-            loss_rows = loss_rows + square[8 * r : 8 * r + 8]
-        terms = []
-        for h in range(groups):
-            here = hi1 == float(h)
-            terms += [
-                jnp.where(here, gap_bf[16 * r : 16 * r + 16], jnp.zeros((), BF16))
-                for r in range(width // 16)
-            ]
-        g_table[...] += nt(jnp.concatenate(terms, axis=0), onehot1)
-
-        actp_d = relu_bf(nn(conv[1], spread(e2_actu_d, actu_d[:, :LANES])))
-        resb = (decin1 + nn(point[3], actp_d)).astype(BF16)
-        outs = nn(edge_t[1], resb)
-        keep(actp_e_r, 1, actp_e)
-        keep(encres_r, 1, encres)
-        keep(gap_r, 1, gap * (2.0 * COMMIT))
-        keep(actp_d_r, 1, actp_d)
-        keep(resb_r, 1, resb)
-        keep(outs_r, 1, outs)
-
-        outs_ext = jnp.concatenate([*e3_outs, outs[:, :LANES]], axis=1) * stack(live2_ext, 2)
-        shifted = outs_ext[8:]
-        wide = TILE + 2 * LANES
-        crossed = jnp.where(
-            sub_ext == 0, pltpu.roll(shifted, 1, 1), pltpu.roll(shifted, wide - 1, 1)
-        )
-        error = (outs_ext[:8] + crossed - sig2) * msk2
-        middle = moved(error, 0)
-        loss_rows = COMMIT * loss_rows + middle * middle
-        loss_sum = loss_rows[:, :LANES]
-        for j in range(1, per_tile):
-            loss_sum = loss_sum + loss_rows[:, j * LANES : (j + 1) * LANES]
-        loss_ref[...] += loss_sum
-        douts = (2.0 * taps(error) * stack(live2, 2)).astype(BF16)
-        g_edge[1] += nt(douts, resb2)
-        dres = nn(edge[1], douts)
-        dbranch = dres.astype(BF16)
-        g_point[3] += nt(dbranch, actp_d2)
-        dinner_d = jnp.where(actp_d2 > 0, nn(point_t[3], dbranch).astype(BF16), 0)
-        keep(dres_r, 2, dres)
-        keep(dinner_d_r, 2, dinner_d)
-
-        around = spread_back(e4_din, dinner_d[:, :LANES])
-        g_conv[1] += nt(around, actu_d3)
-        ddecin = (dres3 + jnp.where(actu_d3 > 0, nn(conv_t[1], around), 0.0)).astype(BF16)
-        g_point[2] += nt(ddecin, chosen3)
-        dlatent = (nn(point_t[2], ddecin) + gap3).astype(BF16)
-        g_point[1] += nt(dlatent, encres3)
-        denc = nn(point_t[1], dlatent)
-        dbranch_e = denc.astype(BF16)
-        g_point[0] += nt(dbranch_e, actp_e3)
-        dinner_e = jnp.where(actp_e3 > 0, nn(point_t[0], dbranch_e).astype(BF16), 0)
-        keep(denc_r, 3, denc)
-        keep(dinner_e_r, 3, dinner_e)
-
-        around_e = spread_back(e5_din, dinner_e[:, :LANES])
-        g_conv[0] += nt(around_e, actu_e4)
-        dhidden = (denc4 + jnp.where(actu_e4 > 0, nn(conv_t[0], around_e), 0.0)).astype(BF16)
-        g_edge[0] += nt(strips4, dhidden)
+            keep(strips_r, lag, strips)
+            keep(onehot_r, lag, onehot)
+            yield
+            picked = nn(table, onehot)
+            hidden = nn(edge[0], strips)
+            yield
+            parts = [jnp.zeros((8, TILE), F32) for _ in range(width // 8)]
+            for h in range(groups):
+                here = hi0 == float(h)
+                parts = [
+                    jnp.where(here, picked[h * width + 8 * r : h * width + 8 * r + 8], parts[r])
+                    for r in range(width // 8)
+                ]
+            chosen = jnp.concatenate(parts, axis=0).astype(BF16)
+            keep(chosen_r, lag, chosen)
+            keep(hidden_r, lag, hidden)
+            keep(actu_e_r, lag, relu_bf(hidden))
+            yield
+            decin = nn(point[2], chosen)
+            yield
+            keep(decin_r, lag, decin)
+            keep(actu_d_r, lag, relu_bf(decin))
+
+        def second_step():
+            lag = LAG
+            actu_e, actu_d = load_ext(actu_e_r, lag), load_ext(actu_d_r, lag)
+            hidden, decin = load(hidden_r, lag), load(decin_r, lag)
+            chosen, me = load(chosen_r, lag), load(me_r, lag)
+            yield
+            inner_e = nn(conv[0], spread(actu_e, 1))
+            inner_d = nn(conv[1], spread(actu_d, 1))
+            yield
+            actp_e = relu_bf(inner_e)
+            actp_d = relu_bf(inner_d)
+            keep(actp_e_r, lag, actp_e)
+            keep(actp_d_r, lag, actp_d)
+            yield
+            branch_e = nn(point[0], actp_e)
+            branch_d = nn(point[3], actp_d)
+            yield
+            encres = (hidden + branch_e).astype(BF16)
+            resb = (decin + branch_d).astype(BF16)
+            keep(encres_r, lag, encres)
+            keep(resb_r, lag, resb)
+            yield
+            latent = nn(point[1], encres)
+            outs = nn(edge_t[1], resb)
+            yield
+            keep(outs_r, lag, outs)
+            gap = (latent.astype(BF16).astype(F32) - chosen.astype(F32)) * stack(me, width // 8)
+            keep(gap_r, lag, gap * (2.0 * COMMIT))
+            keep(gapb_r, lag, gap.astype(BF16))
+            square = gap * gap
+            rows = square[:8]
+            for r in range(1, width // 8):
+                rows = rows + square[8 * r : 8 * r + 8]
+            add_loss(COMMIT * rows)
+
+        def scatter_step():
+            lag = LAG + per_tile
+            onehot, hi, gap = load(onehot_r, lag), load(hi_r, lag), load(gapb_r, lag)
+            yield
+            terms = []
+            for h in range(groups):
+                here = hi == float(h)
+                terms += [
+                    jnp.where(here, gap[16 * r : 16 * r + 16], jnp.zeros((), BF16))
+                    for r in range(width // 16)
+                ]
+            found = nt(jnp.concatenate(terms, axis=0), onehot)
+            yield
+            g_table[...] += found
+
+        def add_loss(rows):
+            total = rows[:, :LANES]
+            for j in range(1, per_tile):
+                total = total + rows[:, j * LANES : (j + 1) * LANES]
+            loss_ref[...] += total
+
+        def third_step():
+            lag = 2 * LAG
+            outs_ext, live_ext = load_ext(outs_r, lag), load_ext(live_r, lag)
+            sig_ext, msk_ext = load_ext(sig_r, lag), load_ext(msk_r, lag)
+            actp, resb = load(actp_d_r, lag), load(resb_r, lag)
+            outs_ext = outs_ext * stack(live_ext, 2)
+            shifted = outs_ext[8:]
+            wide = TILE + 2 * LANES
+            crossed = jnp.where(
+                sub_ext == 0, pltpu.roll(shifted, 1, 1), pltpu.roll(shifted, wide - 1, 1)
+            )
+            error = (outs_ext[:8] + crossed - sig_ext) * msk_ext
+            middle = moved(error, 0)
+            douts = (2.0 * taps(error) * stack(moved(live_ext, 0), 2)).astype(BF16)
+            yield
+            dres = nn(edge[1], douts)
+            yield
+            dbranch = dres.astype(BF16)
+            keep(dres_r, lag, dres)
+            add_loss(middle * middle)
+            yield
+            dinner = nn(point_t[3], dbranch)
+            yield
+            keep(dinner_d_r, lag, jnp.where(actp > 0, dinner.astype(BF16), 0))
+            yield
+            g_point[3] += nt(dbranch, actp)
+            g_edge[1] += nt(douts, resb)
+
+        def fourth_step():
+            lag = 3 * LAG
+            around = spread(load_ext(dinner_d_r, lag), -1)
+            actu, decin, chosen = load(actu_d_r, lag), load(decin_r, lag), load(chosen_r, lag)
+            actp, encres = load(actp_e_r, lag), load(encres_r, lag)
+            gap, dres = load(gap_r, lag), load(dres_r, lag)
+            yield
+            du = nn(conv_t[1], around)
+            yield
+            ddecin = (dres + jnp.where(decin > 0, du, 0.0)).astype(BF16)
+            yield
+            back = nn(point_t[2], ddecin)
+            yield
+            dlatent = (back + gap).astype(BF16)
+            yield
+            denc = nn(point_t[1], dlatent)
+            yield
+            dbranch = denc.astype(BF16)
+            keep(denc_r, lag, denc)
+            yield
+            dinner = nn(point_t[0], dbranch)
+            g_conv[1] += nt(around, actu)
+            yield
+            keep(dinner_e_r, lag, jnp.where(actp > 0, dinner.astype(BF16), 0))
+            yield
+            g_point[2] += nt(ddecin, chosen)
+            g_point[1] += nt(dlatent, encres)
+            g_point[0] += nt(dbranch, actp)
+
+        def fifth_step():
+            lag = 4 * LAG
+            around = spread(load_ext(dinner_e_r, lag), -1)
+            actu, hidden = load(actu_e_r, lag), load(hidden_r, lag)
+            denc, strips = load(denc_r, lag), load(strips_r, lag)
+            yield
+            du = nn(conv_t[0], around)
+            yield
+            dhidden = (denc + jnp.where(hidden > 0, du, 0.0)).astype(BF16)
+            yield
+            g_conv[0] += nt(around, actu)
+            yield
+            g_edge[0] += nt(strips, dhidden)
+
+        steps = [
+            f()
+            for f in (
+                first_step, fourth_step, second_step, scatter_step, third_step, fifth_step
+            )
+        ]
+        while steps:
+            left = []
+            for step in steps:
+                try:
+                    next(step)
+                    left.append(step)
+                except StopIteration:
+                    pass
+            steps = left
+        for ref, lag, value in stores:
+            for b in range(per_tile):
+                ref[block(lag, b)] = value[:, b * LANES : (b + 1) * LANES]
+        for b in range(per_tile):
+            state = fetch(state, block(-LAG, b))
+        return state
+
+    lax.fori_loop(0, tiles, tile_step, state)
 
     first = jnp.where((sub == 0) & (lane == 0), count, 0).astype(F32)
     stats_ref[...] = jnp.concatenate([loss_ref[...], first], axis=0)
@@ -379,13 +426,12 @@
     clips = 8 * sets
     width = 64
     table_rows = 2 * (weights.shape[1] - 4 * width - 16)
-    columns = SLOTS * TILE
-    listed = clips * (per_clip + 1) + 8 * (TILE // LANES) + 8
+    slots = SLOTS * TILE // LANES
     smem = pl.BlockSpec(memory_space=pltpu.SMEM)
     vmem = pl.BlockSpec(memory_space=pltpu.VMEM)
 
     def ring(rows, dtype):
-        return pltpu.VMEM((rows, columns), dtype)
+        return pltpu.VMEM((slots, rows, LANES), dtype)
 
     return pl.pallas_call(
         net_kernel,
@@ -401,8 +447,6 @@
             pltpu.VMEM((2, 16, width), F32),
             pltpu.VMEM((table_rows, LOW), F32),
             pltpu.VMEM((8, LANES), F32),
-            pltpu.SMEM((listed,), jnp.int32),
-            pltpu.SMEM((listed,), jnp.int32),
             pltpu.VMEM((per_clip, clips, LANES), F32),
             pltpu.VMEM((per_clip, clips, LANES), F32),
             pltpu.VMEM((per_clip, clips, LANES), jnp.int32),
@@ -411,8 +455,10 @@
             ring(8, F32),
             ring(8, F32),
             ring(16, BF16),
+            ring(8, F32),
+            ring(16, BF16),
+            ring(16, BF16),
             ring(LOW, BF16),
-            ring(16, BF16),
             ring(width, F32),
             ring(width, BF16),
             ring(width, BF16),
@@ -423,6 +469,7 @@
             ring(width, BF16),
             ring(width, BF16),
             ring(width, F32),
+            ring(width, BF16),
             ring(16, F32),
             ring(width, F32),
             ring(width, BF16),

time: 160 us -> 105 us (0.66)
  Pallas kernels: 153 us -> 96.2 us
    pallas_call x1, Pallas kernels: 106 us -> 59.5 us  [net(): pl.pallas_call(net_kernel, out_shape=(jax.ShapeDtypeStruct((2, rows, LANE...]
    pallas_call x1, Pallas kernels: 33.3 us -> 23.4 us  [summed(): pl.pallas_call(functools.partial(sum_kernel, items), out_shape=(jax.Shape...]
where the time goes in v3:
time: 105 us; the launch traced here: 104 us
  Pallas kernels  96.2 us (92%)
  local copies, waits for them, and re-layouts  5.84 us (6%)
  between operations  2.16 us (2%)
    pallas_call x1, Pallas kernels, net(): pl.pallas_call(net_kernel, out_shape=(jax.ShapeDtypeStruct((2, rows, LANE...  59.5 us
    pallas_call x1, Pallas kernels, summed(): pl.pallas_call(functools.partial(sum_kernel, items), out_shape=(jax.Shape...  23.4 us
    pallas_call x1, Pallas kernels, shared(): pl.pallas_call(functools.partial(share_kernel, items), out_shape=(jax.Sha...  11.9 us
    unnamed x36, local copies, waits for them, and re-layouts  5.84 us

profile of v3, /device:TPU:0, one launch (start us, length us, event | category | flops | bytes accessed | tf_op | source)
XLA Modules:
  0.0 104.2 jit_solution(5062997339552095045)
XLA Ops:
  1.9 0.0 copy-start.14
  2.0 0.0 copy-start.17
  2.0 0.7 copy-done.14
  2.6 0.0 copy-done.17
  2.6 0.9 copy-done
  3.6 0.9 copy-done.2
  4.5 0.9 copy-done.3
  5.5 0.8 copy-done.4
  6.3 0.8 copy-done.6
  7.2 11.9 %shard_map.296 = (s32[16,128]{1,0:T(8,128)S(1)}, bf16[2,16,16,128]{3,2,1,0:T(8,128)(2,1)S(1)}, s32[2,16,8,128]{3,2,1,0:T(8,128)S(1)}, bf16[2,528,256]{2,1,0:T(8,128)(2,1)S(1)}) custom-call(s32[32]{0:T(128)S(1)} %copy-done.17, bf16[32,4096]{1,0:T(8,128)(2,1)S(1)} %copy-done.2, s32[32,2048]{1,0:T(8,128)S(1)} %copy-done.3, f32[1,64,192]{2,1,0:T(8,128)S(1)} %copy-done.4, ...), custom_call_target="tpu_custom_call" | custom-call | tf_op jit(solution)/shard_map/pallas_call | solution.py:604
  19.1 0.0 copy-start.9
  19.1 0.0 copy-start.12
  19.1 0.0 copy-start.13
  19.1 59.5 %shard_map.297 = (f32[2,768,128]{2,1,0:T(8,128)S(1)}, f32[16,128]{1,0:T(8,128)S(1)}) custom-call(s32[16,128]{1,0:T(8,128)S(1)} %get-tuple-element.42.len_ref, bf16[2,16,16,128]{3,2,1,0:T(8,128)(2,1)S(1)} %get-tuple-element.43.wave_ref, s32[2,16,8,128]{3,2,1,0:T(8,128)S(1)} %get-tuple-element.44.ids_ref, bf16[2,528,256]{2,1,0:T(8,128)(2,1)S(1)} %get-tuple-element.45.weight_ref), custom_call_target="tpu_custom_call" | custom-call | tf_op jit(solution)/shard_map/pallas_call | solution.py:436
  78.6 0.0 copy-start.1
  78.6 0.0 copy-start.5
  78.7 0.0 copy-start.7
  78.7 0.0 copy-start.8
  78.7 0.0 copy-start.10
  78.7 0.0 copy-start.11
  78.7 0.0 copy-start.16
  78.7 23.4 %shard_map.298 = (f32[768,128]{1,0:T(8,128)S(1)}, f32[16,128]{1,0:T(8,128)S(1)}) custom-call(f32[2,768,128]{2,1,0:T(8,128)S(1)} %get-tuple-element.46.payload_ref, f32[16,128]{1,0:T(8,128)S(1)} %get-tuple-element.47.stats_ref), custom_call_target="tpu_custom_call" | custom-call | tf_op jit(solution)/shard_map/pallas_call | solution.py:746
  102.1 0.0 copy-start.15
  102.1 0.0 copy-done.9
  102.2 0.0 copy-done.12
  102.2 0.0 copy-done.13
  102.2 0.0 copy-done.1
  102.2 0.0 copy-done.5
  102.2 0.0 copy-done.7
  102.2 0.0 copy-done.8
  102.2 0.6 copy-done.15
  102.8 1.4 %shard_map.299 = (f32[1]{0:T(128)}, f32[1,64,192]{2,1,0:T(8,128)}, f32[1,64,192]{2,1,0:T(8,128)}, f32[1,64,192]{2,1,0:T(8,128)}, bf16[1,64,192]{2,1,0:T(8,128)(2...) custom-call(f32[1]{0:T(128)S(6)} %copy.34.refs_0_, ...), custom_call_target="tpu_custom_call" | custom-call | tf_op jit(solution)/shard_map/pallas_call | solution.py:820
  (8 shorter events, 0.0 us)
Async XLA Ops:
  1.9 0.7 copy-start.14
  2.0 0.7 copy-start.17
  2.6 1.0 copy-start
  3.6 0.9 copy-start.2
  4.5 0.9 copy-start.3
  5.5 0.8 copy-start.4
  6.3 0.8 copy-start.6
  19.1 83.1 %copy-start.9 = (f32[1024,64]{0,1:T(8,128)S(1)}, f32[1024,64]{0,1:T(8,128)}, u32[]{:S(2)}) copy-start(f32[1024,64]{0,1:T(8,128)} %param.31) | copy-start | bytes 786436
  19.1 83.0 %copy-start.12 = (f32[1,64,192]{2,1,0:T(8,128)S(1)}, f32[1,64,192]{2,1,0:T(8,128)}, u32[]{:S(2)}) copy-start(f32[1,64,192]{2,1,0:T(8,128)} %refs_12_.1) | copy-start | bytes 147460
  19.1 83.0 %copy-start.13 = (f32[1,2,64,64]{3,2,1,0:T(8,128)S(1)}, f32[1,2,64,64]{3,2,1,0:T(8,128)}, u32[]{:S(2)}) copy-start(f32[1,2,64,64]{3,2,1,0:T(8,128)} %refs_13_.1) | copy-start | bytes 98308
  78.6 23.5 %copy-start.1 = (f32[1024,64]{0,1:T(8,128)S(1)}, f32[1024,64]{0,1:T(8,128)}, u32[]{:S(2)}) copy-start(f32[1024,64]{0,1:T(8,128)} %param.23) | copy-start | bytes 786436
  78.6 23.5 %copy-start.5 = (f32[1,64,192]{2,1,0:T(8,128)S(1)}, f32[1,64,192]{2,1,0:T(8,128)}, u32[]{:S(2)}) copy-start(f32[1,64,192]{2,1,0:T(8,128)} %refs_4_.1) | copy-start | bytes 147460
  78.7 23.5 %copy-start.7 = (f32[1,2,64,64]{3,2,1,0:T(8,128)S(1)}, f32[1,2,64,64]{3,2,1,0:T(8,128)}, u32[]{:S(2)}) copy-start(f32[1,2,64,64]{3,2,1,0:T(8,128)} %refs_5_.1) | copy-start | bytes 98308
  78.7 23.5 %copy-start.8 = (f32[1024,64]{0,1:T(8,128)S(1)}, f32[1024,64]{0,1:T(8,128)}, u32[]{:S(2)}) copy-start(f32[1024,64]{0,1:T(8,128)} %param.27) | copy-start | bytes 786436
  78.7 23.5 %copy-start.10 = (f32[1,64,192]{2,1,0:T(8,128)S(1)}, f32[1,64,192]{2,1,0:T(8,128)}, u32[]{:S(2)}) copy-start(f32[1,64,192]{2,1,0:T(8,128)} %refs_8_.1) | copy-start | bytes 147460
  78.7 23.5 %copy-start.11 = (f32[1,2,64,64]{3,2,1,0:T(8,128)S(1)}, f32[1,2,64,64]{3,2,1,0:T(8,128)}, u32[]{:S(2)}) copy-start(f32[1,2,64,64]{3,2,1,0:T(8,128)} %refs_9_.1) | copy-start | bytes 98308
  78.7 23.5 %copy-start.16 = (f32[1,64,4]{1,2,0:T(4,128)S(1)}, f32[1,64,4]{1,2,0:T(4,128)}, u32[]{:S(2)}) copy-start(f32[1,64,4]{1,2,0:T(4,128)} %param.30) | copy-start | bytes 3076
  102.1 0.7 copy-start.15

commit v4 on v3

--- a/solution.py
+++ b/solution.py
@@ -49,13 +49,18 @@
 
 
 def net_kernel(
+    len_src,
+    wave_src,
+    ids_src,
+    weight_src,
+    payload_ref,
+    stats_ref,
     len_ref,
     wave_ref,
     ids_ref,
     weight_ref,
-    payload_ref,
-    stats_ref,
-    g_conv,
+    load_sems,
+    g_mix,
     g_point,
     g_edge,
     g_table,
@@ -72,23 +77,31 @@
     hi_r,
     strips_r,
     onehot_r,
-    hidden_r,
     actu_e_r,
     chosen_r,
-    decin_r,
     actu_d_r,
     actp_e_r,
     encres_r,
     actp_d_r,
     resb_r,
-    gap_r,
     gapb_r,
     outs_r,
-    dres_r,
+    douts_r,
+    dbranch_d_r,
     dinner_d_r,
-    denc_r,
+    dlatent_r,
+    dbranch_e_r,
     dinner_e_r,
 ):
+    pairs = (
+        (len_src, len_ref), (wave_src, wave_ref), (ids_src, ids_ref), (weight_src, weight_ref)
+    )
+    loads = [
+        pltpu.make_async_copy(source, place, load_sems.at[k])
+        for k, (source, place) in enumerate(pairs)
+    ]
+    for load in loads:
+        load.start()
     sets, per_clip = wave_ref.shape[:2]
     half = per_clip * LANES
     frames = 2 * half
@@ -97,6 +110,24 @@
     table_rows = groups // 2 * width
     per_tile = TILE // LANES
 
+    rings = (
+        sig_r, msk_r, live_r, me_r, low_r, high_r, hi_r, strips_r, onehot_r, actu_e_r, chosen_r,
+        actu_d_r, actp_e_r, encres_r, actp_d_r, resb_r, gapb_r, outs_r, douts_r, dbranch_d_r,
+        dinner_d_r, dlatent_r, dbranch_e_r, dinner_e_r,
+    )
+    slots = SLOTS * per_tile
+
+    @pl.loop(slots - 4 * LAG - 2, slots)
+    def _(slot):
+        for ref in rings:
+            ref[slot] = jnp.zeros(ref.shape[1:], ref.dtype)
+
+    for ref in (g_mix, g_point, g_edge, g_table, loss_ref):
+        ref[...] = jnp.zeros(ref.shape, ref.dtype)
+
+    for load in loads:
+        load.wait()
+
     def weight(part, start, rows, first, columns):
         start += table_rows
         return weight_ref[part, start : start + rows, first : first + columns]
@@ -108,20 +139,20 @@
     edge = [weight(part, 3 * width, width, 0, 16) for part in range(2)]
     edge_t = [weight(part, 4 * width, 16, 0, width) for part in range(2)]
 
-    rings = (
-        sig_r, msk_r, live_r, me_r, low_r, high_r, hi_r, strips_r, onehot_r, hidden_r, actu_e_r,
-        chosen_r, decin_r, actu_d_r, actp_e_r, encres_r, actp_d_r, resb_r, gap_r, gapb_r, outs_r,
-        dres_r, dinner_d_r, denc_r, dinner_e_r,
+    def beside(*parts):
+        return jnp.concatenate(parts, axis=1)
+
+    same = lax.broadcasted_iota(jnp.int32, (width, width), 0) == lax.broadcasted_iota(
+        jnp.int32, (width, width), 1
     )
-    slots = SLOTS * per_tile
-
-    @pl.loop(slots - 4 * LAG - 2, slots)
-    def _(slot):
-        for ref in rings:
-            ref[slot] = jnp.zeros(ref.shape[1:], ref.dtype)
-
-    for ref in (g_conv, g_point, g_edge, g_table, loss_ref):
-        ref[...] = jnp.zeros(ref.shape, ref.dtype)
+    share = jnp.where(same, 2.0 * COMMIT, 0.0)
+    share_bf = share.astype(BF16)
+    share_rest = (share - share_bf.astype(F32)).astype(BF16)
+    result_e = beside(point[0], edge[0])
+    result_d = beside(point[3], point[2])
+    back_d = beside(conv_t[1], edge[1])
+    back_latent = beside(point_t[2], share_bf, share_rest)
+    back_e = beside(conv_t[0], point_t[1])
 
     for k in range(sets):
         for block in range(per_clip):
@@ -193,7 +224,7 @@
     for b in range(per_tile + 1):
         state = fetch(state, b)
 
-    def tile_step(i, state):
+    def tile_step(names, i, state):
         def block(lag, b):
             return jnp.bitwise_and(i * per_tile - lag + b, slots - 1)
 
@@ -239,19 +270,16 @@
                 ]
             chosen = jnp.concatenate(parts, axis=0).astype(BF16)
             keep(chosen_r, lag, chosen)
-            keep(hidden_r, lag, hidden)
             keep(actu_e_r, lag, relu_bf(hidden))
             yield
             decin = nn(point[2], chosen)
             yield
-            keep(decin_r, lag, decin)
             keep(actu_d_r, lag, relu_bf(decin))
 
         def second_step():
             lag = LAG
             actu_e, actu_d = load_ext(actu_e_r, lag), load_ext(actu_d_r, lag)
-            hidden, decin = load(hidden_r, lag), load(decin_r, lag)
-            chosen, me = load(chosen_r, lag), load(me_r, lag)
+            strips, chosen, me = load(strips_r, lag), load(chosen_r, lag), load(me_r, lag)
             yield
             inner_e = nn(conv[0], spread(actu_e, 1))
             inner_d = nn(conv[1], spread(actu_d, 1))
@@ -261,11 +289,11 @@
             keep(actp_e_r, lag, actp_e)
             keep(actp_d_r, lag, actp_d)
             yield
-            branch_e = nn(point[0], actp_e)
-            branch_d = nn(point[3], actp_d)
-            yield
-            encres = (hidden + branch_e).astype(BF16)
-            resb = (decin + branch_d).astype(BF16)
+            sum_e = nn(result_e, jnp.concatenate([actp_e, strips], axis=0))
+            sum_d = nn(result_d, jnp.concatenate([actp_d, chosen], axis=0))
+            yield
+            encres = sum_e.astype(BF16)
+            resb = sum_d.astype(BF16)
             keep(encres_r, lag, encres)
             keep(resb_r, lag, resb)
             yield
@@ -274,7 +302,6 @@
             yield
             keep(outs_r, lag, outs)
             gap = (latent.astype(BF16).astype(F32) - chosen.astype(F32)) * stack(me, width // 8)
-            keep(gap_r, lag, gap * (2.0 * COMMIT))
             keep(gapb_r, lag, gap.astype(BF16))
             square = gap * gap
             rows = square[:8]
@@ -321,65 +348,73 @@
             dres = nn(edge[1], douts)
             yield
             dbranch = dres.astype(BF16)
-            keep(dres_r, lag, dres)
+            keep(douts_r, lag, douts)
+            keep(dbranch_d_r, lag, dbranch)
             add_loss(middle * middle)
             yield
             dinner = nn(point_t[3], dbranch)
             yield
             keep(dinner_d_r, lag, jnp.where(actp > 0, dinner.astype(BF16), 0))
             yield
-            g_point[3] += nt(dbranch, actp)
+            g_point[1] += nt(dbranch, actp)
             g_edge[1] += nt(douts, resb)
 
         def fourth_step():
             lag = 3 * LAG
             around = spread(load_ext(dinner_d_r, lag), -1)
-            actu, decin, chosen = load(actu_d_r, lag), load(decin_r, lag), load(chosen_r, lag)
-            actp, encres = load(actp_e_r, lag), load(encres_r, lag)
-            gap, dres = load(gap_r, lag), load(dres_r, lag)
-            yield
-            du = nn(conv_t[1], around)
-            yield
-            ddecin = (dres + jnp.where(decin > 0, du, 0.0)).astype(BF16)
-            yield
-            back = nn(point_t[2], ddecin)
-            yield
-            dlatent = (back + gap).astype(BF16)
+            actu, chosen, douts = load(actu_d_r, lag), load(chosen_r, lag), load(douts_r, lag)
+            actp = load(actp_e_r, lag)
+            gap, dbranch_d = load(gapb_r, lag), load(dbranch_d_r, lag)
+            yield
+            both = nn(back_d, jnp.concatenate([around, douts], axis=0))
+            yield
+            ddecin = jnp.where(actu > 0, both.astype(BF16), dbranch_d)
+            yield
+            back = nn(back_latent, jnp.concatenate([ddecin, gap, gap], axis=0))
+            yield
+            dlatent = back.astype(BF16)
+            keep(dlatent_r, lag, dlatent)
             yield
             denc = nn(point_t[1], dlatent)
             yield
             dbranch = denc.astype(BF16)
-            keep(denc_r, lag, denc)
+            keep(dbranch_e_r, lag, dbranch)
             yield
             dinner = nn(point_t[0], dbranch)
-            g_conv[1] += nt(around, actu)
             yield
             keep(dinner_e_r, lag, jnp.where(actp > 0, dinner.astype(BF16), 0))
             yield
-            g_point[2] += nt(ddecin, chosen)
-            g_point[1] += nt(dlatent, encres)
+            g_mix[1] += nt(
+                jnp.concatenate([actu, chosen], axis=0), jnp.concatenate([around, ddecin], axis=0)
+            )
             g_point[0] += nt(dbranch, actp)
 
         def fifth_step():
             lag = 4 * LAG
             around = spread(load_ext(dinner_e_r, lag), -1)
-            actu, hidden = load(actu_e_r, lag), load(hidden_r, lag)
-            denc, strips = load(denc_r, lag), load(strips_r, lag)
-            yield
-            du = nn(conv_t[0], around)
-            yield
-            dhidden = (denc + jnp.where(hidden > 0, du, 0.0)).astype(BF16)
-            yield
-            g_conv[0] += nt(around, actu)
+            actu, strips = load(actu_e_r, lag), load(strips_r, lag)
+            dlatent, dbranch = load(dlatent_r, lag), load(dbranch_e_r, lag)
+            encres = load(encres_r, lag)
+            yield
+            both = nn(back_e, jnp.concatenate([around, dlatent], axis=0))
+            yield
+            dhidden = jnp.where(actu > 0, both.astype(BF16), dbranch)
+            yield
+            g_mix[0] += nt(
+                jnp.concatenate([actu, encres], axis=0), jnp.concatenate([around, dlatent], axis=0)
+            )
             yield
             g_edge[0] += nt(strips, dhidden)
 
-        steps = [
-            f()
-            for f in (
-                first_step, fourth_step, second_step, scatter_step, third_step, fifth_step
-            )
-        ]
+        known = {
+            1: first_step,
+            4: fourth_step,
+            2: second_step,
+            0: scatter_step,
+            3: third_step,
+            5: fifth_step,
+        }
+        steps = [f() for name, f in known.items() if name in names]
         while steps:
             left = []
             for step in steps:
@@ -392,19 +427,31 @@
         for ref, lag, value in stores:
             for b in range(per_tile):
                 ref[block(lag, b)] = value[:, b * LANES : (b + 1) * LANES]
-        for b in range(per_tile):
-            state = fetch(state, block(-LAG, b))
+        if 1 in names:
+            for b in range(per_tile):
+                state = fetch(state, block(-LAG, b))
         return state
 
-    lax.fori_loop(0, tiles, tile_step, state)
-
-    first = jnp.where((sub == 0) & (lane == 0), count, 0).astype(F32)
-    stats_ref[...] = jnp.concatenate([loss_ref[...], first], axis=0)
+    ranges = (
+        ((1, 2), 0, 2),
+        (range(6), 2, tiles - 2),
+        ((4, 5), tiles - 2, tiles - 1),
+        ((5,), tiles - 1, tiles),
+    )
+    for names, begin, end in ranges:
+        state = lax.fori_loop(begin, end, functools.partial(tile_step, names), state)
+
+    loss_row = jnp.sum(loss_ref[...], axis=0, keepdims=True)
+    count_row = jnp.where(lane == 0, count, 0).astype(F32)
+    stats_ref[...] = jnp.where(
+        jnp.bitwise_and(sub, 1) == 0, jnp.broadcast_to(loss_row, (8, LANES)), count_row
+    )
     rows = groups // 2 * width
     for part in range(2):
         payload_ref[part, :rows] = g_table[part * rows : (part + 1) * rows, :LANES]
         payload_ref[part, rows : 2 * rows] = g_table[part * rows : (part + 1) * rows, LANES:]
-        conv_rows = [g_conv[part, k * width : (k + 1) * width] for k in range(3)]
+        conv_rows = [g_mix[part, :width, k * width : (k + 1) * width].T for k in range(3)]
+        mixed = g_mix[part, width:, 3 * width :].T
         edge_rows = jnp.concatenate(
             [g_edge[part], jnp.zeros((width - 16, width), F32)], axis=0
         )
@@ -412,7 +459,7 @@
         for pair in (
             conv_rows[:2],
             (conv_rows[2], edge_rows),
-            (g_point[2 * part], g_point[2 * part + 1]),
+            (mixed, g_point[1]) if part else (g_point[0], mixed),
         ):
             payload_ref[part, after : after + width] = jnp.concatenate(pair, axis=1)
             after += width
@@ -427,7 +474,6 @@
     width = 64
     table_rows = 2 * (weights.shape[1] - 4 * width - 16)
     slots = SLOTS * TILE // LANES
-    smem = pl.BlockSpec(memory_space=pltpu.SMEM)
     vmem = pl.BlockSpec(memory_space=pltpu.VMEM)
 
     def ring(rows, dtype):
@@ -437,46 +483,35 @@
         net_kernel,
         out_shape=(
             jax.ShapeDtypeStruct((2, rows, LANES), F32),
-            jax.ShapeDtypeStruct((16, LANES), F32),
+            jax.ShapeDtypeStruct((8, LANES), F32),
         ),
-        in_specs=[smem] + [vmem] * 3,
+        in_specs=[pl.BlockSpec(memory_space=pl.ANY)] * 4,
         out_specs=(vmem,) * 2,
         scratch_shapes=[
-            pltpu.VMEM((2, 3 * width, width), F32),
-            pltpu.VMEM((4, width, width), F32),
+            pltpu.SMEM(lengths.shape, lengths.dtype),
+            pltpu.VMEM(wave.shape, wave.dtype),
+            pltpu.VMEM(codes.shape, codes.dtype),
+            pltpu.VMEM(weights.shape, weights.dtype),
+            pltpu.SemaphoreType.DMA((4,)),
+            pltpu.VMEM((2, 2 * width, 4 * width), F32),
+            pltpu.VMEM((2, width, width), F32),
             pltpu.VMEM((2, 16, width), F32),
             pltpu.VMEM((table_rows, LOW), F32),
             pltpu.VMEM((8, LANES), F32),
             pltpu.VMEM((per_clip, clips, LANES), F32),
             pltpu.VMEM((per_clip, clips, LANES), F32),
             pltpu.VMEM((per_clip, clips, LANES), jnp.int32),
-            ring(8, F32),
-            ring(8, F32),
-            ring(8, F32),
-            ring(8, F32),
+            *(ring(8, F32) for _ in range(4)),
             ring(16, BF16),
             ring(8, F32),
+            *(ring(16, BF16) for _ in range(2)),
+            ring(LOW, BF16),
+            *(ring(width, BF16) for _ in range(8)),
+            ring(16, F32),
             ring(16, BF16),
-            ring(16, BF16),
-            ring(LOW, BF16),
-            ring(width, F32),
-            ring(width, BF16),
-            ring(width, BF16),
-            ring(width, F32),
-            ring(width, BF16),
-            ring(width, BF16),
-            ring(width, BF16),
-            ring(width, BF16),
-            ring(width, BF16),
-            ring(width, F32),
-            ring(width, BF16),
-            ring(16, F32),
-            ring(width, F32),
-            ring(width, BF16),
-            ring(width, F32),
-            ring(width, BF16),
+            *(ring(width, BF16) for _ in range(5)),
         ],
-        compiler_params=pltpu.CompilerParams(vmem_limit_bytes=48 * 2**20),
+        compiler_params=pltpu.CompilerParams(vmem_limit_bytes=60 * 2**20),
     )(lengths, wave, codes, weights)
 
 
@@ -486,25 +521,16 @@
     )
 
 
-def share_kernel(
-    items,
-    len_ref,
-    wave_ref,
-    ids_ref,
-    conv_ref,
-    point_ref,
-    edge_ref,
-    table_ref,
-    len_out,
-    wave_out,
-    ids_out,
-    weight_out,
-    len_scr,
-    wave_scr,
-    ids_scr,
-    weight_scr,
-    sems,
-):
+def share_kernel(items, *refs):
+    sources, (len_out, wave_out, ids_out, weight_out), inputs = refs[:7], refs[7:11], refs[11:18]
+    len_ref, wave_ref, ids_ref, conv_ref, point_ref, edge_ref, table_ref = inputs
+    len_scr, wave_scr, ids_scr, weight_scr, sems, load_sems = refs[18:]
+    loads = [
+        pltpu.make_async_copy(source, place, load_sems.at[k])
+        for k, (source, place) in enumerate(zip(sources, inputs))
+    ]
+    for load in loads:
+        load.start()
     item = lax.axis_index("item")
     pipe = lax.axis_index("pipe")
     partner = (item, 1 - pipe)
@@ -522,6 +548,8 @@
     wanted = jnp.where(col_at < LANES, 2 * col_at, 2 * (col_at - LANES) + 1)
     split = jnp.where(row_at == wanted, 1.0, 0.0).astype(BF16)
     on_first = pipe == 0
+    for load in loads[:3]:
+        load.wait()
     lane = lax.broadcasted_iota(jnp.int32, (8, LANES), 1)
     kept = jnp.zeros((8, LANES), jnp.int32)
     given = kept
@@ -530,23 +558,28 @@
         given = jnp.where(lane == k, jnp.where(on_first, len_ref[24 + k], len_ref[16 + k]), given)
     len_out[:8] = kept
     len_scr[0] = given
-    for block in range(per_clip):
-        parted = nn(wave_ref[:, block * 2 * LANES : (block + 1) * 2 * LANES], split)
-        codes = ids_ref[:, block * LANES : (block + 1) * LANES]
-        even, odd = parted[:, :LANES], parted[:, LANES:]
-
-        def chosen(values, first, second):
-            return jnp.where(on_first, values[8 * first :][:8], values[8 * second :][:8])
-
-        def both(first, second):
-            return jnp.concatenate(
-                [chosen(even, first, second), chosen(odd, first, second)], axis=0
-            ).astype(BF16)
-
-        wave_out[0, block] = both(0, 1)
-        wave_scr[0, block] = both(3, 2)
-        ids_out[0, block] = chosen(codes, 0, 1)
-        ids_scr[0, block] = chosen(codes, 3, 2)
+    clips = wave_ref.shape[0]
+    strips = [wave_ref[:, k * 2 * LANES : (k + 1) * 2 * LANES] for k in range(per_clip)]
+    parted = nn(jnp.concatenate(strips, axis=0), split)
+
+    def chosen(values, first, second):
+        return jnp.where(on_first, values[8 * first :][:8], values[8 * second :][:8])
+
+    def both(values, first, second):
+        pair = [
+            chosen(side, first, second) for side in (values[:, :LANES], values[:, LANES:])
+        ]
+        return jnp.concatenate(pair, axis=0).astype(BF16)
+
+    codes = [ids_ref[:, k * LANES : (k + 1) * LANES] for k in range(per_clip)]
+    for k in range(per_clip):
+        values = parted[clips * k : clips * (k + 1)]
+        wave_scr[0, k] = both(values, 3, 2)
+        wave_out[0, k] = both(values, 0, 1)
+        ids_out[0, k] = chosen(codes[k], 0, 1)
+    for k in range(per_clip // 2):
+        pair = [chosen(codes[2 * k + j], 3, 2) for j in range(2)]
+        ids_scr[0, k] = jnp.concatenate(pair, axis=0).astype(jnp.int16)
 
     pl.semaphore_wait(barrier, 2)
     copies = [
@@ -556,6 +589,8 @@
     for copy in copies:
         copy.start()
 
+    for load in loads[3:]:
+        load.wait()
     groups = table_rows // width
     for h in range(groups):
         weight_scr[0, h * width : (h + 1) * width] = table_ref[:, h * LOW : (h + 1) * LOW].astype(
@@ -589,14 +624,15 @@
         copy.wait()
     len_out[8:] = len_scr[1]
     wave_out[1] = wave_scr[1]
-    ids_out[1] = ids_scr[1]
+    for k in range(per_clip // 2):
+        pair = ids_scr[1, k].astype(jnp.int32)
+        ids_out[1, 2 * k], ids_out[1, 2 * k + 1] = pair[:8], pair[8:]
 
 
 def shared(items, lengths, waveform, code_ids, conv, point, edge, table):
     per_clip = code_ids.shape[1] // LANES
     width = conv.shape[1]
     weight_rows = table.shape[1] // LOW * width + 4 * width + 16
-    smem = pl.BlockSpec(memory_space=pltpu.SMEM)
     vmem = pl.BlockSpec(memory_space=pltpu.VMEM)
     wave_shape = (2, per_clip, 16, LANES)
     ids_shape = (2, per_clip, 8, LANES)
@@ -609,17 +645,23 @@
             jax.ShapeDtypeStruct(ids_shape, jnp.int32),
             jax.ShapeDtypeStruct(weight_shape, BF16),
         ),
-        in_specs=[smem] + [vmem] * 6,
+        in_specs=[pl.BlockSpec(memory_space=pl.ANY)] * 7,
         out_specs=(vmem,) * 4,
-        scratch_shapes=[
+        scratch_shapes=[pltpu.SMEM(lengths.shape, jnp.int32)]
+        + [
+            pltpu.VMEM(value.shape, value.dtype)
+            for value in (waveform, code_ids, conv, point, edge, table)
+        ]
+        + [
             pltpu.VMEM((2, 8, LANES), jnp.int32),
             pltpu.VMEM(wave_shape, BF16),
-            pltpu.VMEM(ids_shape, jnp.int32),
+            pltpu.VMEM((2, per_clip // 2, 16, LANES), jnp.int16),
             pltpu.VMEM(weight_shape, BF16),
             pltpu.SemaphoreType.DMA((8,)),
+            pltpu.SemaphoreType.DMA((7,)),
         ],
         compiler_params=pltpu.CompilerParams(
-            collective_id=0, has_side_effects=True, vmem_limit_bytes=16 * 2**20
+            collective_id=0, has_side_effects=True, vmem_limit_bytes=60 * 2**20
         ),
     )(lengths, waveform, code_ids, conv, point, edge, table)
 
@@ -633,15 +675,13 @@
     crossed,
     crossed_stats,
     part,
-    part_stats,
     landed,
-    landed_stats,
     whole,
-    cross_sem,
+    stats_sem,
+    cross_send,
+    cross_recv,
     out_send,
     out_recv,
-    stats_send,
-    stats_recv,
     back_send,
     back_recv,
 ):
@@ -651,7 +691,12 @@
     piece = part.shape[1]
 
     def peer(d):
-        return lax.rem(item + d, items)
+        if items & (items - 1):
+            return lax.rem(item + d, items)
+        return jnp.bitwise_and(item + d, items - 1)
+
+    def rows_of(k):
+        return pl.ds(pl.multiple_of(k * piece, piece), piece)
 
     barrier = pltpu.get_barrier_semaphore()
     pl.semaphore_signal(barrier, inc=1, device_id=partner, device_id_type=MESH)
@@ -662,80 +707,78 @@
 
     pl.semaphore_wait(barrier, items)
 
-    over = remote(payload_ref.at[1 - pipe], crossed, cross_sem.at[0], cross_sem.at[1], partner)
-    over_stats = remote(stats_ref, crossed_stats, cross_sem.at[2], cross_sem.at[3], partner)
-    over.start()
+    def cross_copy(k):
+        return remote(
+            payload_ref.at[1 - pipe, rows_of(k)], crossed.at[rows_of(k)],
+            cross_send.at[k], cross_recv.at[k], partner,
+        )
+
+    over_stats = remote(stats_ref, crossed_stats, stats_sem.at[0], stats_sem.at[1], partner)
+
+    @pl.loop(1, items + 1)
+    def _(d):
+        cross_copy(peer(d)).start()
+
     over_stats.start()
-    over_stats.wait()
-    part_stats[...] = stats_ref[...] + crossed_stats[...]
-    over.wait()
-
-    def out_copy(to):
+
+    def out_copy(to, place):
         return remote(
-            part.at[to], landed.at[item], out_send.at[to], out_recv.at[item], (to, pipe)
+            part.at[to], landed.at[place], out_send.at[to], out_recv.at[place], (to, pipe)
         )
-
-    def out_copy_stats(to):
-        return remote(
-            part_stats, landed_stats.at[item], stats_send.at[to], stats_recv.at[item], (to, pipe)
-        )
-
-    def add_up(k):
-        rows = pl.ds(pl.multiple_of(k * piece, piece), piece)
-        return payload_ref[pipe, rows] + crossed[rows]
 
     @pl.loop(1, items)
     def _(d):
         to = peer(d)
-        part[to] = add_up(to).astype(BF16)
-        out_copy(to).start()
-        out_copy_stats(to).start()
-
-    total = add_up(item)
-
-    def take(d, carry):
-        total, stats = carry
+        cross_copy(to).wait_recv()
+        part[to] = (payload_ref[pipe, rows_of(to)] + crossed[rows_of(to)]).astype(BF16)
+        out_copy(to, item).start()
+
+    cross_copy(item).wait_recv()
+    total = payload_ref[pipe, rows_of(item)] + crossed[rows_of(item)]
+    over_stats.wait()
+    stats = stats_ref[...] + crossed_stats[...]
+    high = stats.astype(BF16).astype(F32)
+    middle = (stats - high).astype(BF16).astype(F32)
+    low = stats - high - middle
+    sub = lax.broadcasted_iota(jnp.int32, (8, LANES), 0)
+    message = jnp.where(sub < 2, high, jnp.where(sub < 4, middle, jnp.where(sub < 6, low, 0.0)))
+    whole[item, piece:] = jnp.concatenate([message, jnp.zeros_like(message)], axis=0).astype(BF16)
+
+    def take(d, total):
         source = peer(items - d)
-        remote(
-            part.at[source], landed.at[source], out_send.at[source], out_recv.at[source],
-            (source, pipe),
-        ).wait_recv()
-        remote(
-            part_stats, landed_stats.at[source], stats_send.at[source], stats_recv.at[source],
-            (source, pipe),
-        ).wait_recv()
-        return total + landed[source].astype(F32), stats + landed_stats[source]
-
-    total, stats = lax.fori_loop(1, items, take, (total, part_stats[...]))
-    whole[item] = total.astype(BF16)
-    stats_out[...] = stats
-
-    def back_copy(place, slot, to):
+        out_copy(source, source).wait_recv()
+        return total + landed[source].astype(F32)
+
+    total = lax.fori_loop(1, items, take, total)
+    whole[item, :piece] = total.astype(BF16)
+
+    def back_copy(place, to):
         return remote(
-            whole.at[place], whole.at[place], back_send.at[slot], back_recv.at[place], (to, pipe)
+            whole.at[place], whole.at[place], back_send.at[to], back_recv.at[place], (to, pipe)
         )
+
+    @pl.loop(1, items)
+    def _(d):
+        back_copy(item, peer(d)).start()
+
+    sum_ref[rows_of(item)] = whole[item, :piece].astype(F32)
+
+    def gather(d, stats):
+        source = peer(items - d)
+        back_copy(source, source).wait_recv()
+        sum_ref[rows_of(source)] = whole[source, :piece].astype(F32)
+        return stats + whole[source, piece:].astype(F32)[:8]
+
+    stats_out[...] = lax.fori_loop(1, items, gather, whole[item, piece:].astype(F32)[:8])
 
     @pl.loop(1, items)
     def _(d):
         to = peer(d)
-        back_copy(item, to, to).start()
-
-    own = pl.ds(pl.multiple_of(item * piece, piece), piece)
-    sum_ref[own] = total.astype(BF16).astype(F32)
-
-    @pl.loop(1, items)
-    def _(d):
-        source = peer(items - d)
-        back_copy(source, source, source).wait_recv()
-        rows = pl.ds(pl.multiple_of(source * piece, piece), piece)
-        sum_ref[rows] = whole[source].astype(F32)
-
-    @pl.loop(1, items)
-    def _(d):
-        to = peer(d)
-        out_copy(to).wait_send()
-        out_copy_stats(to).wait_send()
-        back_copy(item, to, to).wait_send()
+        cross_copy(to).wait_send()
+        out_copy(to, item).wait_send()
+        back_copy(item, to).wait_send()
+
+    cross_copy(item).wait_send()
 
 
 def summed(items, payload, stats):
@@ -755,11 +798,9 @@
             pltpu.VMEM((rows, LANES), F32),
             pltpu.VMEM(stats.shape, F32),
             pltpu.VMEM((items, piece, LANES), BF16),
-            pltpu.VMEM(stats.shape, F32),
             pltpu.VMEM((items, piece, LANES), BF16),
-            pltpu.VMEM((items,) + stats.shape, F32),
-            pltpu.VMEM((items, piece, LANES), BF16),
-            pltpu.SemaphoreType.DMA((4,)),
+            pltpu.VMEM((items, piece + 16, LANES), BF16),
+            pltpu.SemaphoreType.DMA((2,)),
         ]
         + [sems] * 6,
         compiler_params=pltpu.CompilerParams(
@@ -774,9 +815,10 @@
     loss_ref = refs[16]
     results = refs[17:]
     width = states[0].shape[1]
-    count = jnp.sum(stats_ref[8:], keepdims=True)
-    loss_ref[0] = jnp.sum(stats_ref[:8]) / jnp.sum(stats_ref[8:])
-    scale = 1.0 / count
+    odd = jnp.bitwise_and(lax.broadcasted_iota(jnp.int32, stats_ref.shape, 0), 1) == 1
+    counts = jnp.where(odd, stats_ref[...], 0.0)
+    loss_ref[0] = jnp.sum(jnp.where(odd, 0.0, stats_ref[...])) / jnp.sum(counts)
+    scale = 1.0 / jnp.sum(counts, keepdims=True)
 
     def step(kind, place, grad, rate):
         weight_ref, moment_ref, average_ref = (states[4 * j + kind] for j in range(3))

time: 105 us -> 91.2 us (0.87)
  Pallas kernels: 96.2 us -> 85.5 us
  local copies, waits for them, and re-layouts: 5.84 us -> 2.44 us
    pallas_call x1, Pallas kernels: 23.4 us -> 17.4 us  [summed(): pl.pallas_call(functools.partial(sum_kernel, items), out_shape=(jax.Shape...]
    pallas_call x1, Pallas kernels: 59.5 us -> 54.4 us  [net(): pl.pallas_call(net_kernel, out_shape=(jax.ShapeDtypeStruct((2, rows, LANE...]
    unnamed x36 -> x28, local copies, waits for them, and re-layouts: 5.84 us -> 2.44 us
where the time goes in v4:
time: 91.2 us; the launch traced here: 90.1 us
  Pallas kernels  85.5 us (94%)
  local copies, waits for them, and re-layouts  2.44 us (3%)
  between operations  2.14 us (2%)
    pallas_call x1, Pallas kernels, net(): pl.pallas_call(net_kernel, out_shape=(jax.ShapeDtypeStruct((2, rows, LANE...  54.4 us
    pallas_call x1, Pallas kernels, summed(): pl.pallas_call(functools.partial(sum_kernel, items), out_shape=(jax.Shape...  17.4 us
    pallas_call x1, Pallas kernels, shared(): pl.pallas_call(functools.partial(share_kernel, items), out_shape=(jax.Sha...  12.2 us
    unnamed x28, local copies, waits for them, and re-layouts  2.44 us

profile of v4, /device:TPU:0, one launch (start us, length us, event | category | flops | bytes accessed | tf_op | source)
XLA Modules:
  0.0 90.1 jit_solution(4060097112046083050)
XLA Ops:
  1.9 12.2 %shard_map.296 = (s32[16,128]{1,0:T(8,128)}, bf16[2,16,16,128]{3,2,1,0:T(8,128)(2,1)}, s32[2,16,8,128]{3,2,1,0:T(8,128)}, bf16[2,528,256]{2,1,0:T(8,128)(2,1)}) custom-call(s32[32]{0:T(128)} %refs_0_.2, bf16[32,4096]{1,0:T(8,128)(2,1)} %refs_1_.2, s32[32,2048]{1,0:T(8,128)} %refs_2_.1, f32[1,64,192]{2,1,0:T(8,128)} %refs_4_.3, f32[1,2,64,64]{3,2,1,0:T(8,128)} %refs_5_.1, ...), custom_call_target="tpu_custom_call" | custom-call | tf_op jit(solution)/shard_map/pallas_call | solution.py:640
  14.2 0.0 copy-start.5
  14.2 0.0 copy-start.8
  14.2 0.0 copy-start.9
  14.2 54.4 %shard_map.297 = (f32[2,768,128]{2,1,0:T(8,128)}, f32[8,128]{1,0:T(8,128)}) custom-call(s32[16,128]{1,0:T(8,128)} %get-tuple-element.42.len_src, bf16[2,16,16,128]{3,2,1,0:T(8,128)(2,1)} %get-tuple-element.43.wave_src, s32[2,16,8,128]{3,2,1,0:T(8,128)} %get-tuple-element.44.ids_src, bf16[2,528,256]{2,1,0:T(8,128)(2,1)} %get-tuple-element.45.weight_src), custom_call_target="tpu_custom_call" | custom-call | tf_op jit(solution)/shard_map/pallas_call | solution.py:482
  68.7 0.0 copy-start.1
  68.7 1.1 %copy-done.1 = f32[2,768,128]{2,1,0:T(8,128)S(1)} copy-done((f32[2,768,128]{2,1,0:T(8,128)S(1)}, f32[2,768,128]{2,1,0:T(8,128)}, u32[]{:S(2)}) %copy-start.1) | copy-done | bytes 786456
  69.8 0.0 copy-start.11
  69.8 0.7 copy-done.11
  70.5 0.0 copy-start
  70.5 0.0 copy-start.2
  70.5 0.0 copy-start.3
  70.5 0.0 copy-start.4
  70.5 0.0 copy-start.6
  70.5 0.0 copy-start.7
  70.5 0.0 copy-start.12
  70.5 0.0 copy-start.13
  70.5 17.4 %shard_map.298 = (f32[768,128]{1,0:T(8,128)S(1)}, f32[8,128]{1,0:T(8,128)S(1)}) custom-call(f32[2,768,128]{2,1,0:T(8,128)S(1)} %copy-done.1, f32[8,128]{1,0:T(8,128)S(1)} %copy-done.11), custom_call_target="tpu_custom_call" | custom-call | tf_op jit(solution)/shard_map/pallas_call | solution.py:789
  88.0 0.0 copy-start.10
  88.0 0.0 copy-done.5
  88.0 0.0 copy-done.8
  88.0 0.0 copy-done.9
  88.0 0.0 copy-done
  88.0 0.0 copy-done.2
  88.1 0.0 copy-done.3
  88.1 0.0 copy-done.4
  88.1 0.0 copy-done.6
  88.1 0.0 copy-done.7
  88.1 0.0 copy-done.12
  88.1 0.0 copy-done.13
  88.1 0.6 copy-done.10
  88.7 1.4 %shard_map.299 = (f32[1]{0:T(128)}, f32[1,64,192]{2,1,0:T(8,128)}, f32[1,64,192]{2,1,0:T(8,128)}, f32[1,64,192]{2,1,0:T(8,128)}, bf16[1,64,192]{2,1,0:T(8,128)(2...) custom-call(f32[1]{0:T(128)S(6)} %copy.34.refs_0_, ...), custom_call_target="tpu_custom_call" | custom-call | tf_op jit(solution)/shard_map/pallas_call | solution.py:862
Async XLA Ops:
  14.2 73.8 %copy-start.5 = (f32[1024,64]{0,1:T(8,128)S(1)}, f32[1024,64]{0,1:T(8,128)}, u32[]{:S(2)}) copy-start(f32[1024,64]{0,1:T(8,128)} %param.31) | copy-start | bytes 786436
  14.2 73.8 %copy-start.8 = (f32[1,64,192]{2,1,0:T(8,128)S(1)}, f32[1,64,192]{2,1,0:T(8,128)}, u32[]{:S(2)}) copy-start(f32[1,64,192]{2,1,0:T(8,128)} %refs_12_.1) | copy-start | bytes 147460
  14.2 73.8 %copy-start.9 = (f32[1,2,64,64]{3,2,1,0:T(8,128)S(1)}, f32[1,2,64,64]{3,2,1,0:T(8,128)}, u32[]{:S(2)}) copy-start(f32[1,2,64,64]{3,2,1,0:T(8,128)} %refs_13_.1) | copy-start | bytes 98308
  68.7 1.1 %copy-start.1 = (f32[2,768,128]{2,1,0:T(8,128)S(1)}, f32[2,768,128]{2,1,0:T(8,128)}, u32[]{:S(2)}) copy-start(f32[2,768,128]{2,1,0:T(8,128)} %get-tuple-element.46.payload_ref) | copy-start | bytes 2359300
  69.8 0.7 copy-start.11
  70.5 17.6 %copy-start = (f32[1024,64]{0,1:T(8,128)S(1)}, f32[1024,64]{0,1:T(8,128)}, u32[]{:S(2)}) copy-start(f32[1024,64]{0,1:T(8,128)} %param.23) | copy-start | bytes 786436
  70.5 17.6 %copy-start.2 = (f32[1,64,192]{2,1,0:T(8,128)S(1)}, f32[1,64,192]{2,1,0:T(8,128)}, u32[]{:S(2)}) copy-start(f32[1,64,192]{2,1,0:T(8,128)} %refs_4_.3) | copy-start | bytes 147460
  70.5 17.6 %copy-start.3 = (f32[1,2,64,64]{3,2,1,0:T(8,128)S(1)}, f32[1,2,64,64]{3,2,1,0:T(8,128)}, u32[]{:S(2)}) copy-start(f32[1,2,64,64]{3,2,1,0:T(8,128)} %refs_5_.1) | copy-start | bytes 98308
  70.5 17.6 %copy-start.4 = (f32[1024,64]{0,1:T(8,128)S(1)}, f32[1024,64]{0,1:T(8,128)}, u32[]{:S(2)}) copy-start(f32[1024,64]{0,1:T(8,128)} %param.27) | copy-start | bytes 786436
  70.5 17.6 %copy-start.6 = (f32[1,64,192]{2,1,0:T(8,128)S(1)}, f32[1,64,192]{2,1,0:T(8,128)}, u32[]{:S(2)}) copy-start(f32[1,64,192]{2,1,0:T(8,128)} %refs_8_.1) | copy-start | bytes 147460
  70.5 17.6 %copy-start.7 = (f32[1,2,64,64]{3,2,1,0:T(8,128)S(1)}, f32[1,2,64,64]{3,2,1,0:T(8,128)}, u32[]{:S(2)}) copy-start(f32[1,2,64,64]{3,2,1,0:T(8,128)} %refs_9_.1) | copy-start | bytes 98308
  70.5 17.6 %copy-start.12 = (f32[1,64,4]{1,2,0:T(4,128)S(1)}, f32[1,64,4]{1,2,0:T(4,128)}, u32[]{:S(2)}) copy-start(f32[1,64,4]{1,2,0:T(4,128)} %param.26) | copy-start | bytes 3076
  70.5 17.6 %copy-start.13 = (f32[1,64,4]{1,2,0:T(4,128)S(1)}, f32[1,64,4]{1,2,0:T(4,128)}, u32[]{:S(2)}) copy-start(f32[1,64,4]{1,2,0:T(4,128)} %param.30) | copy-start | bytes 3076
  88.0 0.7 copy-start.10

commit v5 on v4

--- a/solution.py
+++ b/solution.py
@@ -16,12 +16,14 @@
 TILE = 512
 SLOTS = 8
 LAG = TILE // LANES + 1
+HEAD = 2
 DEPTH = -(-4 * LAG * LANES // TILE)
 LOW = 256
-SPARE = 16
-REAL = 8
+SPARE = 8
+REAL = 4
 
 MESH = pl.DeviceIdType.MESH
+ORDER = (1, 6, 2, 3, 4, 0, 5, 7, 1, 6, 2, 3, 4, 0, 5, 7, 1, 6, 2, 3, 4, 0, 5, 7, 1, 6, 2, 3, 0, 5, 7, 1, 6, 2, 3, 5, 7, 6, 2, 3, 5, 7, 6, 2, 3, 5, 7, 6, 2, 5, 6, 5, 6, 6, 6)
 F32 = jnp.float32
 BF16 = jnp.bfloat16
 
@@ -54,7 +56,6 @@
     ids_src,
     weight_src,
     payload_ref,
-    stats_ref,
     len_ref,
     wave_ref,
     ids_ref,
@@ -117,7 +118,7 @@
     )
     slots = SLOTS * per_tile
 
-    @pl.loop(slots - 4 * LAG - 2, slots)
+    @pl.loop(slots - (4 * LAG + 1 - HEAD * per_tile), slots)
     def _(slot):
         for ref in rings:
             ref[slot] = jnp.zeros(ref.shape[1:], ref.dtype)
@@ -152,6 +153,8 @@
     result_d = beside(point[3], point[2])
     back_d = beside(conv_t[1], edge[1])
     back_latent = beside(point_t[2], share_bf, share_rest)
+    blank = jnp.zeros((width, width), BF16)
+    finish = jnp.concatenate([beside(point[1], blank), beside(blank[:16], edge_t[1])], axis=0)
     back_e = beside(conv_t[0], point_t[1])
 
     for k in range(sets):
@@ -234,20 +237,25 @@
         def load_ext(ref, lag):
             return load(ref, lag, -1, per_tile + 1)
 
-        stores = []
-
         def keep(ref, lag, value):
-            stores.append((ref, lag, value))
+            for b in range(per_tile):
+                ref[block(lag, b)] = value[:, b * LANES : (b + 1) * LANES]
 
         def spread(ext, way):
             return jnp.concatenate([moved(ext, d * way) for d in (-REACH, 0, REACH)], axis=0)
 
-        def first_step():
-            lag = 0
-            sig_ext, live0 = load_ext(sig_r, lag), load(live_r, lag)
-            hi0 = load(high_r, lag)
-            low16 = load(low_r, lag) - iota16
-            strips = (taps(sig_ext) * stack(live0, 2)).astype(BF16)
+        def strips_step():
+            sig_ext, live = load_ext(sig_r, 0), load(live_r, 0)
+            yield
+            strips = (taps(sig_ext) * stack(live, 2)).astype(BF16)
+            keep(strips_r, 0, strips)
+            yield
+            hidden = nn(edge[0], strips)
+            yield
+            keep(actu_e_r, 0, relu_bf(hidden))
+
+        def lookup_step():
+            low16, hi = load(low_r, 0) - iota16, load(high_r, 0)
             onehot = jnp.concatenate(
                 [
                     jnp.where(low16 == float(16 * r), jnp.ones((), BF16), jnp.zeros((), BF16))
@@ -255,64 +263,71 @@
                 ],
                 axis=0,
             )
-            keep(strips_r, lag, strips)
-            keep(onehot_r, lag, onehot)
+            keep(onehot_r, 0, onehot)
             yield
             picked = nn(table, onehot)
-            hidden = nn(edge[0], strips)
             yield
             parts = [jnp.zeros((8, TILE), F32) for _ in range(width // 8)]
             for h in range(groups):
-                here = hi0 == float(h)
+                here = hi == float(h)
                 parts = [
                     jnp.where(here, picked[h * width + 8 * r : h * width + 8 * r + 8], parts[r])
                     for r in range(width // 8)
                 ]
             chosen = jnp.concatenate(parts, axis=0).astype(BF16)
-            keep(chosen_r, lag, chosen)
-            keep(actu_e_r, lag, relu_bf(hidden))
+            keep(chosen_r, 0, chosen)
             yield
             decin = nn(point[2], chosen)
             yield
-            keep(actu_d_r, lag, relu_bf(decin))
-
-        def second_step():
+            keep(actu_d_r, 0, relu_bf(decin))
+
+        def encode_step():
             lag = LAG
-            actu_e, actu_d = load_ext(actu_e_r, lag), load_ext(actu_d_r, lag)
-            strips, chosen, me = load(strips_r, lag), load(chosen_r, lag), load(me_r, lag)
-            yield
-            inner_e = nn(conv[0], spread(actu_e, 1))
-            inner_d = nn(conv[1], spread(actu_d, 1))
-            yield
-            actp_e = relu_bf(inner_e)
-            actp_d = relu_bf(inner_d)
-            keep(actp_e_r, lag, actp_e)
-            keep(actp_d_r, lag, actp_d)
-            yield
-            sum_e = nn(result_e, jnp.concatenate([actp_e, strips], axis=0))
-            sum_d = nn(result_d, jnp.concatenate([actp_d, chosen], axis=0))
-            yield
-            encres = sum_e.astype(BF16)
-            resb = sum_d.astype(BF16)
+            around = spread(load_ext(actu_e_r, lag), 1)
+            yield
+            inner = nn(conv[0], around)
+            yield
+            actp, strips = relu_bf(inner), load(strips_r, lag)
+            keep(actp_e_r, lag, actp)
+            yield
+            result = nn(result_e, jnp.concatenate([actp, strips], axis=0))
+            yield
+            encres = result.astype(BF16)
             keep(encres_r, lag, encres)
-            keep(resb_r, lag, resb)
             yield
             latent = nn(point[1], encres)
-            outs = nn(edge_t[1], resb)
-            yield
-            keep(outs_r, lag, outs)
+            chosen, me = load(chosen_r, lag), load(me_r, lag)
+            yield
             gap = (latent.astype(BF16).astype(F32) - chosen.astype(F32)) * stack(me, width // 8)
             keep(gapb_r, lag, gap.astype(BF16))
+            yield
             square = gap * gap
             rows = square[:8]
             for r in range(1, width // 8):
                 rows = rows + square[8 * r : 8 * r + 8]
             add_loss(COMMIT * rows)
 
+        def decode_step():
+            lag = LAG
+            around = spread(load_ext(actu_d_r, lag), 1)
+            yield
+            inner = nn(conv[1], around)
+            yield
+            actp, chosen = relu_bf(inner), load(chosen_r, lag)
+            keep(actp_d_r, lag, actp)
+            yield
+            result = nn(result_d, jnp.concatenate([actp, chosen], axis=0))
+            yield
+            resb = result.astype(BF16)
+            keep(resb_r, lag, resb)
+            yield
+            outs = nn(edge_t[1], resb)
+            yield
+            keep(outs_r, lag, outs)
+
         def scatter_step():
             lag = LAG + per_tile
-            onehot, hi, gap = load(onehot_r, lag), load(hi_r, lag), load(gapb_r, lag)
-            yield
+            hi, gap = load(hi_r, lag), load(gapb_r, lag)
             terms = []
             for h in range(groups):
                 here = hi == float(h)
@@ -320,6 +335,8 @@
                     jnp.where(here, gap[16 * r : 16 * r + 16], jnp.zeros((), BF16))
                     for r in range(width // 16)
                 ]
+            onehot = load(onehot_r, lag)
+            yield
             found = nt(jnp.concatenate(terms, axis=0), onehot)
             yield
             g_table[...] += found
@@ -330,11 +347,10 @@
                 total = total + rows[:, j * LANES : (j + 1) * LANES]
             loss_ref[...] += total
 
-        def third_step():
+        def error_step():
             lag = 2 * LAG
             outs_ext, live_ext = load_ext(outs_r, lag), load_ext(live_r, lag)
             sig_ext, msk_ext = load_ext(sig_r, lag), load_ext(msk_r, lag)
-            actp, resb = load(actp_d_r, lag), load(resb_r, lag)
             outs_ext = outs_ext * stack(live_ext, 2)
             shifted = outs_ext[8:]
             wide = TILE + 2 * LANES
@@ -343,32 +359,38 @@
             )
             error = (outs_ext[:8] + crossed - sig_ext) * msk_ext
             middle = moved(error, 0)
+            add_loss(middle * middle)
+            yield
             douts = (2.0 * taps(error) * stack(moved(live_ext, 0), 2)).astype(BF16)
+            keep(douts_r, lag, douts)
             yield
             dres = nn(edge[1], douts)
             yield
             dbranch = dres.astype(BF16)
-            keep(douts_r, lag, douts)
             keep(dbranch_d_r, lag, dbranch)
-            add_loss(middle * middle)
             yield
             dinner = nn(point_t[3], dbranch)
+            actp = load(actp_d_r, lag)
             yield
             keep(dinner_d_r, lag, jnp.where(actp > 0, dinner.astype(BF16), 0))
             yield
-            g_point[1] += nt(dbranch, actp)
-            g_edge[1] += nt(douts, resb)
-
-        def fourth_step():
+            found = nt(dbranch, actp)
+            yield
+            g_point[1] += found
+            yield
+            found = nt(douts, load(resb_r, lag))
+            yield
+            g_edge[1] += found
+
+        def middle_step():
             lag = 3 * LAG
-            around = spread(load_ext(dinner_d_r, lag), -1)
-            actu, chosen, douts = load(actu_d_r, lag), load(chosen_r, lag), load(douts_r, lag)
-            actp = load(actp_e_r, lag)
-            gap, dbranch_d = load(gapb_r, lag), load(dbranch_d_r, lag)
+            around, douts = spread(load_ext(dinner_d_r, lag), -1), load(douts_r, lag)
             yield
             both = nn(back_d, jnp.concatenate([around, douts], axis=0))
+            actu, dbranch_d = load(actu_d_r, lag), load(dbranch_d_r, lag)
             yield
             ddecin = jnp.where(actu > 0, both.astype(BF16), dbranch_d)
+            gap = load(gapb_r, lag)
             yield
             back = nn(back_latent, jnp.concatenate([ddecin, gap, gap], axis=0))
             yield
@@ -379,71 +401,78 @@
             yield
             dbranch = denc.astype(BF16)
             keep(dbranch_e_r, lag, dbranch)
+            actp = load(actp_e_r, lag)
             yield
             dinner = nn(point_t[0], dbranch)
             yield
             keep(dinner_e_r, lag, jnp.where(actp > 0, dinner.astype(BF16), 0))
             yield
-            g_mix[1] += nt(
-                jnp.concatenate([actu, chosen], axis=0), jnp.concatenate([around, ddecin], axis=0)
+            found = nt(
+                jnp.concatenate([actu, load(chosen_r, lag)], axis=0),
+                jnp.concatenate([around, ddecin], axis=0),
             )
-            g_point[0] += nt(dbranch, actp)
-
-        def fifth_step():
+            yield
+            g_mix[1] += found
+            yield
+            found = nt(dbranch, actp)
+            yield
+            g_point[0] += found
+
+        def last_step():
             lag = 4 * LAG
             around = spread(load_ext(dinner_e_r, lag), -1)
-            actu, strips = load(actu_e_r, lag), load(strips_r, lag)
-            dlatent, dbranch = load(dlatent_r, lag), load(dbranch_e_r, lag)
-            encres = load(encres_r, lag)
+            dlatent = load(dlatent_r, lag)
             yield
             both = nn(back_e, jnp.concatenate([around, dlatent], axis=0))
+            actu, dbranch = load(actu_e_r, lag), load(dbranch_e_r, lag)
             yield
             dhidden = jnp.where(actu > 0, both.astype(BF16), dbranch)
             yield
-            g_mix[0] += nt(
-                jnp.concatenate([actu, encres], axis=0), jnp.concatenate([around, dlatent], axis=0)
+            found = nt(
+                jnp.concatenate([actu, load(encres_r, lag)], axis=0),
+                jnp.concatenate([around, dlatent], axis=0),
             )
             yield
-            g_edge[0] += nt(strips, dhidden)
-
-        known = {
-            1: first_step,
-            4: fourth_step,
-            2: second_step,
-            0: scatter_step,
-            3: third_step,
-            5: fifth_step,
-        }
-        steps = [f() for name, f in known.items() if name in names]
-        while steps:
-            left = []
-            for step in steps:
-                try:
-                    next(step)
-                    left.append(step)
-                except StopIteration:
-                    pass
-            steps = left
-        for ref, lag, value in stores:
-            for b in range(per_tile):
-                ref[block(lag, b)] = value[:, b * LANES : (b + 1) * LANES]
-        if 1 in names:
+            g_mix[0] += found
+            yield
+            found = nt(load(strips_r, lag), dhidden)
+            yield
+            g_edge[0] += found
+
+        functions = (
+            strips_step,
+            lookup_step,
+            encode_step,
+            decode_step,
+            scatter_step,
+            error_step,
+            middle_step,
+            last_step,
+        )
+        steps = {k: functions[k]() for k in names}
+        for k in ORDER:
+            if k in steps:
+                next(steps[k], None)
+        for step in steps.values():
+            for _ in step:
+                pass
+        if 0 in names:
             for b in range(per_tile):
                 state = fetch(state, block(-LAG, b))
         return state
 
     ranges = (
-        ((1, 2), 0, 2),
-        (range(6), 2, tiles - 2),
-        ((4, 5), tiles - 2, tiles - 1),
-        ((5,), tiles - 1, tiles),
+        ((0, 1, 2, 3), 0, HEAD),
+        (range(8), HEAD, tiles - 2),
+        ((6, 7), tiles - 2, tiles - 1),
+        ((7,), tiles - 1, tiles),
     )
     for names, begin, end in ranges:
         state = lax.fori_loop(begin, end, functools.partial(tile_step, names), state)
 
     loss_row = jnp.sum(loss_ref[...], axis=0, keepdims=True)
     count_row = jnp.where(lane == 0, count, 0).astype(F32)
-    stats_ref[...] = jnp.where(
+    stats = jnp.where(
         jnp.bitwise_and(sub, 1) == 0, jnp.broadcast_to(loss_row, (8, LANES)), count_row
     )
     rows = groups // 2 * width
@@ -463,6 +492,8 @@
         ):
             payload_ref[part, after : after + width] = jnp.concatenate(pair, axis=1)
             after += width
+        payload_ref[part, after : after + 8] = stats
+        after += 8
         rest = payload_ref.shape[1] - after
         if rest:
             payload_ref[part, after:] = jnp.zeros((rest, LANES), F32)
@@ -481,12 +512,9 @@
 
     return pl.pallas_call(
         net_kernel,
-        out_shape=(
-            jax.ShapeDtypeStruct((2, rows, LANES), F32),
-            jax.ShapeDtypeStruct((8, LANES), F32),
-        ),
+        out_shape=jax.ShapeDtypeStruct((2, rows, LANES), F32),
         in_specs=[pl.BlockSpec(memory_space=pl.ANY)] * 4,
-        out_specs=(vmem,) * 2,
+        out_specs=vmem,
         scratch_shapes=[
             pltpu.SMEM(lengths.shape, lengths.dtype),
             pltpu.VMEM(wave.shape, wave.dtype),
@@ -668,16 +696,15 @@
 
 def sum_kernel(
     items,
+    stats_row,
     payload_ref,
-    stats_ref,
     sum_ref,
-    stats_out,
+    own,
     crossed,
-    crossed_stats,
     part,
     landed,
     whole,
-    stats_sem,
+    own_sem,
     cross_send,
     cross_recv,
     out_send,
@@ -698,6 +725,8 @@
     def rows_of(k):
         return pl.ds(pl.multiple_of(k * piece, piece), piece)
 
+    load = pltpu.make_async_copy(payload_ref.at[pipe], own, own_sem)
+    load.start()
     barrier = pltpu.get_barrier_semaphore()
     pl.semaphore_signal(barrier, inc=1, device_id=partner, device_id_type=MESH)
 
@@ -713,13 +742,11 @@
             cross_send.at[k], cross_recv.at[k], partner,
         )
 
-    over_stats = remote(stats_ref, crossed_stats, stats_sem.at[0], stats_sem.at[1], partner)
-
     @pl.loop(1, items + 1)
     def _(d):
         cross_copy(peer(d)).start()
 
-    over_stats.start()
+    load.wait()
 
     def out_copy(to, place):
         return remote(
@@ -730,13 +757,12 @@
     def _(d):
         to = peer(d)
         cross_copy(to).wait_recv()
-        part[to] = (payload_ref[pipe, rows_of(to)] + crossed[rows_of(to)]).astype(BF16)
+        part[to] = (own[rows_of(to)] + crossed[rows_of(to)]).astype(BF16)
         out_copy(to, item).start()
 
     cross_copy(item).wait_recv()
-    total = payload_ref[pipe, rows_of(item)] + crossed[rows_of(item)]
-    over_stats.wait()
-    stats = stats_ref[...] + crossed_stats[...]
+    total = own[rows_of(item)] + crossed[rows_of(item)]
+    stats = own[stats_row : stats_row + 8] + crossed[stats_row : stats_row + 8]
     high = stats.astype(BF16).astype(F32)
     middle = (stats - high).astype(BF16).astype(F32)
     low = stats - high - middle
@@ -763,61 +789,66 @@
 
     sum_ref[rows_of(item)] = whole[item, :piece].astype(F32)
 
+    @pl.loop(1, items)
+    def _(d):
+        to = peer(d)
+        cross_copy(to).wait_send()
+        out_copy(to, item).wait_send()
+
+    cross_copy(item).wait_send()
+
     def gather(d, stats):
         source = peer(items - d)
         back_copy(source, source).wait_recv()
         sum_ref[rows_of(source)] = whole[source, :piece].astype(F32)
         return stats + whole[source, piece:].astype(F32)[:8]
 
-    stats_out[...] = lax.fori_loop(1, items, gather, whole[item, piece:].astype(F32)[:8])
+    stats = lax.fori_loop(1, items, gather, whole[item, piece:].astype(F32)[:8])
+    sum_ref[stats_row : stats_row + 8] = stats
 
     @pl.loop(1, items)
     def _(d):
-        to = peer(d)
-        cross_copy(to).wait_send()
-        out_copy(to, item).wait_send()
-        back_copy(item, to).wait_send()
-
-    cross_copy(item).wait_send()
-
-
-def summed(items, payload, stats):
+        back_copy(item, peer(d)).wait_send()
+
+
+def summed(items, stats_row, payload):
     rows = payload.shape[1]
     piece = rows // items
     vmem = pl.BlockSpec(memory_space=pltpu.VMEM)
     sems = pltpu.SemaphoreType.DMA((items,))
     return pl.pallas_call(
-        functools.partial(sum_kernel, items),
-        out_shape=(
-            jax.ShapeDtypeStruct((rows, LANES), F32),
-            jax.ShapeDtypeStruct(stats.shape, F32),
-        ),
-        in_specs=[vmem] * 2,
-        out_specs=(vmem,) * 2,
+        functools.partial(sum_kernel, items, stats_row),
+        out_shape=jax.ShapeDtypeStruct((rows, LANES), F32),
+        in_specs=[pl.BlockSpec(memory_space=pl.ANY)],
+        out_specs=vmem,
         scratch_shapes=[
             pltpu.VMEM((rows, LANES), F32),
-            pltpu.VMEM(stats.shape, F32),
+            pltpu.VMEM((rows, LANES), F32),
             pltpu.VMEM((items, piece, LANES), BF16),
             pltpu.VMEM((items, piece, LANES), BF16),
             pltpu.VMEM((items, piece + 16, LANES), BF16),
-            pltpu.SemaphoreType.DMA((2,)),
+            pltpu.SemaphoreType.DMA,
         ]
         + [sems] * 6,
         compiler_params=pltpu.CompilerParams(
             collective_id=1, has_side_effects=True, vmem_limit_bytes=16 * 2**20
         ),
-    )(payload, stats)
+    )(payload)
 
 
 def update_kernel(*refs):
-    rate_net, rate_code, sum_ref, stats_ref = refs[:4]
-    states = refs[4:16]
-    loss_ref = refs[16]
-    results = refs[17:]
+    rate_net, rate_code, sum_ref = refs[:3]
+    states = refs[3:15]
+    loss_ref = refs[15]
+    results = refs[16:]
     width = states[0].shape[1]
-    odd = jnp.bitwise_and(lax.broadcasted_iota(jnp.int32, stats_ref.shape, 0), 1) == 1
-    counts = jnp.where(odd, stats_ref[...], 0.0)
-    loss_ref[0] = jnp.sum(jnp.where(odd, 0.0, stats_ref[...])) / jnp.sum(counts)
+    groups = states[3].shape[1] // LOW
+    rows = groups * width
+    stats_row = 2 * rows + 3 * width
+    stats = sum_ref[stats_row : stats_row + 8]
+    odd = jnp.bitwise_and(lax.broadcasted_iota(jnp.int32, stats.shape, 0), 1) == 1
+    counts = jnp.where(odd, stats, 0.0)
+    loss_ref[0] = jnp.sum(jnp.where(odd, 0.0, stats)) / jnp.sum(counts)
     scale = 1.0 / jnp.sum(counts, keepdims=True)
 
     def step(kind, place, grad, rate):
@@ -831,8 +862,6 @@
         average_new_ref[place] = AVERAGE * average_ref[place] + (1.0 - AVERAGE) * weight
         copy_ref[place] = weight.astype(BF16)
 
-    groups = states[3].shape[1] // LOW
-    rows = groups * width
     for h in range(groups):
         for side in range(LOW // LANES):
             start = h * LOW + side * LANES
@@ -850,7 +879,7 @@
     step(2, 0, jnp.concatenate(edge, axis=0), rate)
 
 
-def updated(rates, sums, stats, states):
+def updated(rates, sums, states):
     smem = pl.BlockSpec(memory_space=pltpu.SMEM)
     shapes = [jax.ShapeDtypeStruct((1,), F32)]
     for weight in states[:4]:
@@ -863,10 +892,10 @@
         update_kernel,
         grid=(1,),
         out_shape=tuple(shapes),
-        in_specs=[smem] * 2 + [block(value) for value in (sums, stats, *states)],
+        in_specs=[smem] * 2 + [block(value) for value in (sums, *states)],
         out_specs=(smem,) + tuple(block(value) for value in shapes[1:]),
         compiler_params=pltpu.CompilerParams(vmem_limit_bytes=24 * 2**20),
-    )(*rates, sums, stats, *states)
+    )(*rates, sums, *states)
 
 
 def per_device(
@@ -893,16 +922,16 @@
     edge_w, edge_mom, edge_avg = (jnp.swapaxes(v, 1, 2) for v in (edge_w, edge_mom, edge_avg))
     codebook, code_mom, code_avg = (v.T for v in (codebook, code_mom, code_avg))
     rows = 2 * (codebook.shape[1] // LOW) * width + 3 * width
-    piece = -(-rows // (16 * items)) * 16
+    piece = -(-(rows + 8) // (16 * items)) * 16
     own_inputs = shared(items, lengths, waveform, code_ids, conv_w, point_w, edge_w, codebook)
-    payload, stats = net(piece * items, *own_inputs)
-    sums, stats = summed(items, payload, stats)
+    payload = net(piece * items, *own_inputs)
+    sums = summed(items, rows, payload)
     states = (
         conv_w, point_w, edge_w, codebook,
         conv_mom, point_mom, edge_mom, code_mom,
         conv_avg, point_avg, edge_avg, code_avg,
     )
-    loss, *rest = updated((rate_net, rate_code), sums, stats, states)
+    loss, *rest = updated((rate_net, rate_code), sums, states)
     edges = (jnp.swapaxes(v, 1, 2) for v in rest[8:12])
     return (loss.reshape(()), *rest[:8], *edges, *(v.T for v in rest[12:]))
 

time: 91.2 us -> 83.7 us (0.918)
  Pallas kernels: 85.5 us -> 79.7 us
  local copies, waits for them, and re-layouts: 2.44 us -> 1.19 us
    pallas_call x2, Pallas kernels: 71.9 us -> 66.1 us  [the longest x1 47.6 us: net(): pl.pallas_call(net_kernel, out_shape=jax.ShapeDtypeStruct((2, rows, LANES...]
    unnamed x28 -> x26, local copies, waits for them, and re-layouts: 2.44 us -> 1.19 us
where the time goes in v5:
time: 83.7 us; the launch traced here: 83 us
  Pallas kernels  79.7 us (95%)
  between operations  2.14 us (3%)
  local copies, waits for them, and re-layouts  1.19 us (1%)
    pallas_call x1, Pallas kernels, net(): pl.pallas_call(net_kernel, out_shape=jax.ShapeDtypeStruct((2, rows, LANES...  47.6 us
    pallas_call x1, Pallas kernels, summed(): pl.pallas_call(functools.partial(sum_kernel, items, stats_row), out_shape...  18.5 us
    pallas_call x1, Pallas kernels, shared(): pl.pallas_call(functools.partial(share_kernel, items), out_shape=(jax.Sha...  12.2 us

profile of v5, /device:TPU:0, one launch (start us, length us, event | category | flops | bytes accessed | tf_op | source)
XLA Modules:
  0.0 83.0 jit_solution(10804527614129800140)
XLA Ops:
  1.9 12.2 %shard_map.296 = (s32[16,128]{1,0:T(8,128)}, bf16[2,16,16,128]{3,2,1,0:T(8,128)(2,1)}, s32[2,16,8,128]{3,2,1,0:T(8,128)}, bf16[2,528,256]{2,1,0:T(8,128)(2,1)}) custom-call(s32[32]{0:T(128)} %refs_0_.2, bf16[32,4096]{1,0:T(8,128)(2,1)} %refs_1_.2, s32[32,2048]{1,0:T(8,128)} %refs_2_.1, f32[1,64,192]{2,1,0:T(8,128)} %refs_3_.3, f32[1,2,64,64]{3,2,1,0:T(8,128)} %refs_4_.3, ...), custom_call_target="tpu_custom_call" | custom-call | tf_op jit(solution)/shard_map/pallas_call | solution.py:668
  14.2 0.0 copy-start.10
  14.2 0.0 copy-start.11
  14.2 0.0 copy-start.12
  14.2 47.6 %shard_map.297.payload_ref = f32[2,768,128]{2,1,0:T(8,128)} custom-call(s32[16,128]{1,0:T(8,128)} %get-tuple-element.38.len_src, bf16[2,16,16,128]{3,2,1,0:T(8,128)(2,1)} %get-tuple-element.39.wave_src, s32[2,16,8,128]{3,2,1,0:T(8,128)} %get-tuple-element.40.ids_src, bf16[2,528,256]{2,1,0:T(8,128)(2,1)} %get-tuple-element.41.weight_src), custom_call_target="tpu_custom_call" | custom-call | tf_op jit(solution)/shard_map/pallas_call | solution.py:513
  61.8 0.0 copy-start
  61.8 1.1 %copy-done = f32[2,768,128]{2,1,0:T(8,128)S(1)} copy-done((f32[2,768,128]{2,1,0:T(8,128)S(1)}, f32[2,768,128]{2,1,0:T(8,128)}, u32[]{:S(2)}) %copy-start) | copy-done | bytes 786456
  62.9 0.0 copy-start.1
  62.9 0.0 copy-start.2
  62.9 0.0 copy-start.3
  63.0 0.0 copy-start.4
  63.0 0.0 copy-start.5
  63.0 0.0 copy-start.6
  63.0 0.0 copy-start.7
  63.0 0.0 copy-start.8
  63.0 0.0 copy-start.9
  63.0 18.5 %shard_map.298.refs_2_ = f32[768,128]{1,0:T(8,128)S(1)} custom-call(f32[2,768,128]{2,1,0:T(8,128)S(1)} %copy-done), custom_call_target="tpu_custom_call" | custom-call | tf_op jit(solution)/shard_map/pallas_call | solution.py:819
  81.5 0.0 copy-done.10
  81.5 0.0 copy-done.11
  81.5 0.0 copy-done.12
  81.5 0.0 copy-done.1
  81.5 0.0 copy-done.2
  81.5 0.0 copy-done.3
  81.6 0.0 copy-done.4
  81.6 0.0 copy-done.5
  81.6 0.0 copy-done.6
  81.6 0.0 copy-done.7
  81.6 0.0 copy-done.8
  81.6 0.0 copy-done.9
  81.6 1.4 %shard_map.299 = (f32[1]{0:T(128)}, f32[1,64,192]{2,1,0:T(8,128)}, f32[1,64,192]{2,1,0:T(8,128)}, f32[1,64,192]{2,1,0:T(8,128)}, bf16[1,64,192]{2,1,0:T(8,128)(2...) custom-call(f32[1]{0:T(128)S(6)} %copy.34.refs_0_, ...), custom_call_target="tpu_custom_call" | custom-call | tf_op jit(solution)/shard_map/pallas_call | solution.py:891
Async XLA Ops:
  14.2 67.3 %copy-start.10 = (f32[1,64,4]{1,2,0:T(4,128)S(1)}, f32[1,64,4]{1,2,0:T(4,128)}, u32[]{:S(2)}) copy-start(f32[1,64,4]{1,2,0:T(4,128)} %param.22) | copy-start | bytes 3076
  14.2 67.3 %copy-start.11 = (f32[1,64,4]{1,2,0:T(4,128)S(1)}, f32[1,64,4]{1,2,0:T(4,128)}, u32[]{:S(2)}) copy-start(f32[1,64,4]{1,2,0:T(4,128)} %param.26) | copy-start | bytes 3076
  14.2 67.3 %copy-start.12 = (f32[1,64,4]{1,2,0:T(4,128)S(1)}, f32[1,64,4]{1,2,0:T(4,128)}, u32[]{:S(2)}) copy-start(f32[1,64,4]{1,2,0:T(4,128)} %param.30) | copy-start | bytes 3076
  61.8 1.1 %copy-start = (f32[2,768,128]{2,1,0:T(8,128)S(1)}, f32[2,768,128]{2,1,0:T(8,128)}, u32[]{:S(2)}) copy-start(f32[2,768,128]{2,1,0:T(8,128)} %shard_map.297.payload_ref) | copy-start | bytes 2359300
  62.9 18.6 %copy-start.1 = (f32[1024,64]{0,1:T(8,128)S(1)}, f32[1024,64]{0,1:T(8,128)}, u32[]{:S(2)}) copy-start(f32[1024,64]{0,1:T(8,128)} %param.23) | copy-start | bytes 786436
  62.9 18.6 %copy-start.2 = (f32[1,64,192]{2,1,0:T(8,128)S(1)}, f32[1,64,192]{2,1,0:T(8,128)}, u32[]{:S(2)}) copy-start(f32[1,64,192]{2,1,0:T(8,128)} %refs_3_.3) | copy-start | bytes 147460
  62.9 18.6 %copy-start.3 = (f32[1,2,64,64]{3,2,1,0:T(8,128)S(1)}, f32[1,2,64,64]{3,2,1,0:T(8,128)}, u32[]{:S(2)}) copy-start(f32[1,2,64,64]{3,2,1,0:T(8,128)} %refs_4_.3) | copy-start | bytes 98308
  63.0 18.6 %copy-start.4 = (f32[1024,64]{0,1:T(8,128)S(1)}, f32[1024,64]{0,1:T(8,128)}, u32[]{:S(2)}) copy-start(f32[1024,64]{0,1:T(8,128)} %param.27) | copy-start | bytes 786436
  63.0 18.6 %copy-start.5 = (f32[1024,64]{0,1:T(8,128)S(1)}, f32[1024,64]{0,1:T(8,128)}, u32[]{:S(2)}) copy-start(f32[1024,64]{0,1:T(8,128)} %param.31) | copy-start | bytes 786436
  63.0 18.6 %copy-start.6 = (f32[1,64,192]{2,1,0:T(8,128)S(1)}, f32[1,64,192]{2,1,0:T(8,128)}, u32[]{:S(2)}) copy-start(f32[1,64,192]{2,1,0:T(8,128)} %refs_7_.1) | copy-start | bytes 147460
  63.0 18.6 %copy-start.7 = (f32[1,2,64,64]{3,2,1,0:T(8,128)S(1)}, f32[1,2,64,64]{3,2,1,0:T(8,128)}, u32[]{:S(2)}) copy-start(f32[1,2,64,64]{3,2,1,0:T(8,128)} %refs_8_.1) | copy-start | bytes 98308
  63.0 18.6 %copy-start.8 = (f32[1,64,192]{2,1,0:T(8,128)S(1)}, f32[1,64,192]{2,1,0:T(8,128)}, u32[]{:S(2)}) copy-start(f32[1,64,192]{2,1,0:T(8,128)} %refs_11_.1) | copy-start | bytes 147460
  63.0 18.6 %copy-start.9 = (f32[1,2,64,64]{3,2,1,0:T(8,128)S(1)}, f32[1,2,64,64]{3,2,1,0:T(8,128)}, u32[]{:S(2)}) copy-start(f32[1,2,64,64]{3,2,1,0:T(8,128)} %refs_12_.1) | copy-start | bytes 98308

commit v6 on v5

--- a/solution.py
+++ b/solution.py
@@ -23,7 +23,7 @@
 REAL = 4
 
 MESH = pl.DeviceIdType.MESH
-ORDER = (1, 6, 2, 3, 4, 0, 5, 7, 1, 6, 2, 3, 4, 0, 5, 7, 1, 6, 2, 3, 4, 0, 5, 7, 1, 6, 2, 3, 0, 5, 7, 1, 6, 2, 3, 5, 7, 6, 2, 3, 5, 7, 6, 2, 3, 5, 7, 6, 2, 5, 6, 5, 6, 6, 6)
+ORDER = (1, 6, 3, 2, 4, 7, 5, 0, 1, 6, 3, 2, 4, 7, 5, 0, 1, 6, 3, 2, 4, 7, 5, 0, 1, 6, 3, 2, 7, 5, 0, 1, 6, 3, 2, 7, 5, 6, 2, 7, 5, 6, 7, 6, 6)
 F32 = jnp.float32
 BF16 = jnp.bfloat16
 
@@ -62,7 +62,7 @@
     weight_ref,
     load_sems,
     g_mix,
-    g_point,
+    g_outs,
     g_edge,
     g_table,
     loss_ref,
@@ -82,16 +82,12 @@
     chosen_r,
     actu_d_r,
     actp_e_r,
-    encres_r,
     actp_d_r,
-    resb_r,
     gapb_r,
     outs_r,
     douts_r,
-    dbranch_d_r,
     dinner_d_r,
     dlatent_r,
-    dbranch_e_r,
     dinner_e_r,
 ):
     pairs = (
@@ -113,8 +109,7 @@
 
     rings = (
         sig_r, msk_r, live_r, me_r, low_r, high_r, hi_r, strips_r, onehot_r, actu_e_r, chosen_r,
-        actu_d_r, actp_e_r, encres_r, actp_d_r, resb_r, gapb_r, outs_r, douts_r, dbranch_d_r,
-        dinner_d_r, dlatent_r, dbranch_e_r, dinner_e_r,
+        actu_d_r, actp_e_r, actp_d_r, gapb_r, outs_r, douts_r, dinner_d_r, dlatent_r, dinner_e_r,
     )
     slots = SLOTS * per_tile
 
@@ -123,7 +118,7 @@
         for ref in rings:
             ref[slot] = jnp.zeros(ref.shape[1:], ref.dtype)
 
-    for ref in (g_mix, g_point, g_edge, g_table, loss_ref):
+    for ref in (g_mix, g_outs, g_edge, g_table, loss_ref):
         ref[...] = jnp.zeros(ref.shape, ref.dtype)
 
     for load in loads:
@@ -146,15 +141,18 @@
     same = lax.broadcasted_iota(jnp.int32, (width, width), 0) == lax.broadcasted_iota(
         jnp.int32, (width, width), 1
     )
-    share = jnp.where(same, 2.0 * COMMIT, 0.0)
-    share_bf = share.astype(BF16)
-    share_rest = (share - share_bf.astype(F32)).astype(BF16)
-    result_e = beside(point[0], edge[0])
-    result_d = beside(point[3], point[2])
+    same_bf = jnp.where(same, 1.0, 0.0).astype(BF16)
+
+    def halves(value):
+        high = value.astype(BF16)
+        return high, (value - high.astype(F32)).astype(BF16)
+
+    latent_w = beside(*halves(nn(point[1], point[0])), *halves(nn(point[1], edge[0])))
+    outs_w = jnp.concatenate(halves(nn(edge_t[1], beside(point[3], point[2]))), axis=0)
+    inner_d_w = beside(*halves(nn(point_t[3], edge[1])))
+    inner_e_w = beside(*halves(nn(point_t[0], point_t[1])))
     back_d = beside(conv_t[1], edge[1])
-    back_latent = beside(point_t[2], share_bf, share_rest)
-    blank = jnp.zeros((width, width), BF16)
-    finish = jnp.concatenate([beside(point[1], blank), beside(blank[:16], edge_t[1])], axis=0)
+    back_latent = beside(point_t[2], same_bf)
     back_e = beside(conv_t[0], point_t[1])
 
     for k in range(sets):
@@ -290,16 +288,11 @@
             actp, strips = relu_bf(inner), load(strips_r, lag)
             keep(actp_e_r, lag, actp)
             yield
-            result = nn(result_e, jnp.concatenate([actp, strips], axis=0))
-            yield
-            encres = result.astype(BF16)
-            keep(encres_r, lag, encres)
-            yield
-            latent = nn(point[1], encres)
+            latent = nn(latent_w, jnp.concatenate([actp, actp, strips, strips], axis=0))
             chosen, me = load(chosen_r, lag), load(me_r, lag)
             yield
             gap = (latent.astype(BF16).astype(F32) - chosen.astype(F32)) * stack(me, width // 8)
-            keep(gapb_r, lag, gap.astype(BF16))
+            keep(gapb_r, lag, (gap * (2.0 * COMMIT)).astype(BF16))
             yield
             square = gap * gap
             rows = square[:8]
@@ -316,14 +309,9 @@
             actp, chosen = relu_bf(inner), load(chosen_r, lag)
             keep(actp_d_r, lag, actp)
             yield
-            result = nn(result_d, jnp.concatenate([actp, chosen], axis=0))
-            yield
-            resb = result.astype(BF16)
-            keep(resb_r, lag, resb)
-            yield
-            outs = nn(edge_t[1], resb)
-            yield
-            keep(outs_r, lag, outs)
+            outs = nn(outs_w, jnp.concatenate([actp, chosen], axis=0))
+            yield
+            keep(outs_r, lag, outs[:16] + outs[16:])
 
         def scatter_step():
             lag = LAG + per_tile
@@ -364,46 +352,33 @@
             douts = (2.0 * taps(error) * stack(moved(live_ext, 0), 2)).astype(BF16)
             keep(douts_r, lag, douts)
             yield
-            dres = nn(edge[1], douts)
-            yield
-            dbranch = dres.astype(BF16)
-            keep(dbranch_d_r, lag, dbranch)
-            yield
-            dinner = nn(point_t[3], dbranch)
+            dinner = nn(inner_d_w, jnp.concatenate([douts, douts], axis=0))
             actp = load(actp_d_r, lag)
             yield
             keep(dinner_d_r, lag, jnp.where(actp > 0, dinner.astype(BF16), 0))
             yield
-            found = nt(dbranch, actp)
-            yield
-            g_point[1] += found
-            yield
-            found = nt(douts, load(resb_r, lag))
-            yield
-            g_edge[1] += found
+            found = nt(jnp.concatenate([actp, load(chosen_r, lag)], axis=0), douts)
+            yield
+            g_outs[...] += found
 
         def middle_step():
             lag = 3 * LAG
             around, douts = spread(load_ext(dinner_d_r, lag), -1), load(douts_r, lag)
             yield
             both = nn(back_d, jnp.concatenate([around, douts], axis=0))
-            actu, dbranch_d = load(actu_d_r, lag), load(dbranch_d_r, lag)
-            yield
-            ddecin = jnp.where(actu > 0, both.astype(BF16), dbranch_d)
+            dres = nn(edge[1], douts)
+            actu = load(actu_d_r, lag)
+            yield
+            ddecin = jnp.where(actu > 0, both.astype(BF16), dres.astype(BF16))
             gap = load(gapb_r, lag)
             yield
-            back = nn(back_latent, jnp.concatenate([ddecin, gap, gap], axis=0))
+            back = nn(back_latent, jnp.concatenate([ddecin, gap], axis=0))
             yield
             dlatent = back.astype(BF16)
             keep(dlatent_r, lag, dlatent)
             yield
-            denc = nn(point_t[1], dlatent)
-            yield
-            dbranch = denc.astype(BF16)
-            keep(dbranch_e_r, lag, dbranch)
+            dinner = nn(inner_e_w, jnp.concatenate([dlatent, dlatent], axis=0))
             actp = load(actp_e_r, lag)
-            yield
-            dinner = nn(point_t[0], dbranch)
             yield
             keep(dinner_e_r, lag, jnp.where(actp > 0, dinner.astype(BF16), 0))
             yield
@@ -412,11 +387,8 @@
                 jnp.concatenate([around, ddecin], axis=0),
             )
             yield
-            g_mix[1] += found
-            yield
-            found = nt(dbranch, actp)
-            yield
-            g_point[0] += found
+            g_mix[1, :width] += found[:width]
+            g_mix[1, width : 2 * width, LANES:] += found[width:, LANES:]
 
         def last_step():
             lag = 4 * LAG
@@ -424,20 +396,23 @@
             dlatent = load(dlatent_r, lag)
             yield
             both = nn(back_e, jnp.concatenate([around, dlatent], axis=0))
-            actu, dbranch = load(actu_e_r, lag), load(dbranch_e_r, lag)
-            yield
-            dhidden = jnp.where(actu > 0, both.astype(BF16), dbranch)
+            denc = nn(point_t[1], dlatent)
+            actu = load(actu_e_r, lag)
+            yield
+            dhidden = jnp.where(actu > 0, both.astype(BF16), denc.astype(BF16))
+            strips = load(strips_r, lag)
             yield
             found = nt(
-                jnp.concatenate([actu, load(encres_r, lag)], axis=0),
+                jnp.concatenate([actu, load(actp_e_r, lag), strips], axis=0),
                 jnp.concatenate([around, dlatent], axis=0),
             )
             yield
-            g_mix[0] += found
-            yield
-            found = nt(load(strips_r, lag), dhidden)
-            yield
-            g_edge[0] += found
+            g_mix[0, :width] += found[:width]
+            g_mix[0, width:, LANES:] += found[width:, LANES:]
+            yield
+            found = nt(dhidden, strips)
+            yield
+            g_edge[...] += found
 
         functions = (
             strips_step,
@@ -475,20 +450,37 @@
     stats = jnp.where(
         jnp.bitwise_and(sub, 1) == 0, jnp.broadcast_to(loss_row, (8, LANES)), count_row
     )
+    def exact(a, b, axis):
+        return lax.dot_general(
+            a.astype(F32),
+            b.astype(F32),
+            (((1,), (axis,)), ((), ())),
+            preferred_element_type=F32,
+            precision=lax.Precision.HIGHEST,
+        )
+
+    by_latent = g_mix[0, width : 2 * width, 3 * width :].T
+    by_strips = g_mix[0, 2 * width :, 3 * width :].T
+    by_inner, by_chosen = g_outs[:width].T, g_outs[width:].T
+    points = (
+        (
+            exact(point_t[1], by_latent, 0),
+            exact(by_latent, point[0], 1) + exact(by_strips, edge[0], 1),
+        ),
+        (g_mix[1, width : 2 * width, 3 * width :].T, exact(edge[1], by_inner, 0)),
+    )
+    edges = (g_edge[...].T, exact(by_inner, point[3], 1) + exact(by_chosen, point[2], 1))
     rows = groups // 2 * width
     for part in range(2):
         payload_ref[part, :rows] = g_table[part * rows : (part + 1) * rows, :LANES]
         payload_ref[part, rows : 2 * rows] = g_table[part * rows : (part + 1) * rows, LANES:]
         conv_rows = [g_mix[part, :width, k * width : (k + 1) * width].T for k in range(3)]
-        mixed = g_mix[part, width:, 3 * width :].T
-        edge_rows = jnp.concatenate(
-            [g_edge[part], jnp.zeros((width - 16, width), F32)], axis=0
-        )
+        edge_rows = jnp.concatenate([edges[part], jnp.zeros((width - 16, width), F32)], axis=0)
         after = 2 * rows
         for pair in (
             conv_rows[:2],
             (conv_rows[2], edge_rows),
-            (mixed, g_point[1]) if part else (g_point[0], mixed),
+            points[part],
         ):
             payload_ref[part, after : after + width] = jnp.concatenate(pair, axis=1)
             after += width
@@ -521,9 +513,9 @@
             pltpu.VMEM(codes.shape, codes.dtype),
             pltpu.VMEM(weights.shape, weights.dtype),
             pltpu.SemaphoreType.DMA((4,)),
-            pltpu.VMEM((2, 2 * width, 4 * width), F32),
-            pltpu.VMEM((2, width, width), F32),
-            pltpu.VMEM((2, 16, width), F32),
+            pltpu.VMEM((2, 2 * width + 16, 4 * width), F32),
+            pltpu.VMEM((2 * width, 16), F32),
+            pltpu.VMEM((width, 16), F32),
             pltpu.VMEM((table_rows, LOW), F32),
             pltpu.VMEM((8, LANES), F32),
             pltpu.VMEM((per_clip, clips, LANES), F32),
@@ -534,10 +526,10 @@
             ring(8, F32),
             *(ring(16, BF16) for _ in range(2)),
             ring(LOW, BF16),
-            *(ring(width, BF16) for _ in range(8)),
+            *(ring(width, BF16) for _ in range(6)),
             ring(16, F32),
             ring(16, BF16),
-            *(ring(width, BF16) for _ in range(5)),
+            *(ring(width, BF16) for _ in range(3)),
         ],
         compiler_params=pltpu.CompilerParams(vmem_limit_bytes=60 * 2**20),
     )(lengths, wave, codes, weights)
@@ -867,7 +859,7 @@
             start = h * LOW + side * LANES
             grad = sum_ref[side * rows + h * width : side * rows + (h + 1) * width]
             place = (slice(None), slice(start, start + LANES))
-            step(3, place, grad * (-2.0 * COMMIT), rate_code[0])
+            step(3, place, -grad, rate_code[0])
     first, second, third = (
         sum_ref[2 * rows + k * width : 2 * rows + (k + 1) * width] for k in range(3)
     )

time: 83.7 us -> 81.4 us (0.973); the launches traced: 83 us -> 82.2 us
  Pallas kernels: 79.7 us -> 78.8 us
    pallas_call x1, Pallas kernels: 47.6 us -> 46.1 us  [net(): pl.pallas_call(net_kernel, out_shape=jax.ShapeDtypeStruct((2, rows, LANES...]
where the time goes in v6:
time: 81.4 us; the launch traced here: 82.2 us
  Pallas kernels  78.8 us (97%)
  between operations  2.14 us (3%)
  local copies, waits for them, and re-layouts  1.19 us (1%)
    pallas_call x1, Pallas kernels, net(): pl.pallas_call(net_kernel, out_shape=jax.ShapeDtypeStruct((2, rows, LANES...  46.1 us
    pallas_call x1, Pallas kernels, summed(): pl.pallas_call(functools.partial(sum_kernel, items, stats_row), out_shape...  19.1 us
    pallas_call x1, Pallas kernels, shared(): pl.pallas_call(functools.partial(share_kernel, items), out_shape=(jax.Sha...  12.2 us

profile of v6, /device:TPU:0, one launch (start us, length us, event | category | flops | bytes accessed | tf_op | source)
XLA Modules:
  0.0 82.2 jit_solution(11733058339070782039)
XLA Ops:
  1.9 12.2 %shard_map.296 = (s32[16,128]{1,0:T(8,128)}, bf16[2,16,16,128]{3,2,1,0:T(8,128)(2,1)}, s32[2,16,8,128]{3,2,1,0:T(8,128)}, bf16[2,528,256]{2,1,0:T(8,128)(2,1)}) custom-call(s32[32]{0:T(128)} %refs_0_.2, bf16[32,4096]{1,0:T(8,128)(2,1)} %refs_1_.2, s32[32,2048]{1,0:T(8,128)} %refs_2_.1, f32[1,64,192]{2,1,0:T(8,128)} %refs_3_.3, f32[1,2,64,64]{3,2,1,0:T(8,128)} %refs_4_.3, ...), custom_call_target="tpu_custom_call" | custom-call | tf_op jit(solution)/shard_map/pallas_call | solution.py:660
  14.2 0.0 copy-start.10
  14.2 0.0 copy-start.11
  14.2 0.0 copy-start.12
  14.2 46.1 %shard_map.297.payload_ref = f32[2,768,128]{2,1,0:T(8,128)} custom-call(s32[16,128]{1,0:T(8,128)} %get-tuple-element.38.len_src, bf16[2,16,16,128]{3,2,1,0:T(8,128)(2,1)} %get-tuple-element.39.wave_src, s32[2,16,8,128]{3,2,1,0:T(8,128)} %get-tuple-element.40.ids_src, bf16[2,528,256]{2,1,0:T(8,128)(2,1)} %get-tuple-element.41.weight_src), custom_call_target="tpu_custom_call" | custom-call | tf_op jit(solution)/shard_map/pallas_call | solution.py:505
  60.3 0.0 copy-start
  60.3 1.1 %copy-done = f32[2,768,128]{2,1,0:T(8,128)S(1)} copy-done((f32[2,768,128]{2,1,0:T(8,128)S(1)}, f32[2,768,128]{2,1,0:T(8,128)}, u32[]{:S(2)}) %copy-start) | copy-done | bytes 786456
  61.4 0.0 copy-start.1
  61.4 0.0 copy-start.2
  61.4 0.0 copy-start.3
  61.4 0.0 copy-start.4
  61.4 0.0 copy-start.5
  61.5 0.0 copy-start.6
  61.5 0.0 copy-start.7
  61.5 0.0 copy-start.8
  61.5 0.0 copy-start.9
  61.5 19.1 %shard_map.298.refs_2_ = f32[768,128]{1,0:T(8,128)S(1)} custom-call(f32[2,768,128]{2,1,0:T(8,128)S(1)} %copy-done), custom_call_target="tpu_custom_call" | custom-call | tf_op jit(solution)/shard_map/pallas_call | solution.py:811
  80.6 0.0 copy-done.10
  80.6 0.0 copy-done.11
  80.6 0.0 copy-done.12
  80.6 0.0 copy-done.1
  80.6 0.0 copy-done.2
  80.6 0.0 copy-done.3
  80.7 0.0 copy-done.4
  80.7 0.0 copy-done.5
  80.7 0.0 copy-done.6
  80.7 0.0 copy-done.7
  80.7 0.0 copy-done.8
  80.7 0.0 copy-done.9
  80.7 1.4 %shard_map.299 = (f32[1]{0:T(128)}, f32[1,64,192]{2,1,0:T(8,128)}, f32[1,64,192]{2,1,0:T(8,128)}, f32[1,64,192]{2,1,0:T(8,128)}, bf16[1,64,192]{2,1,0:T(8,128)(2...) custom-call(f32[1]{0:T(128)S(6)} %copy.34.refs_0_, ...), custom_call_target="tpu_custom_call" | custom-call | tf_op jit(solution)/shard_map/pallas_call | solution.py:883
Async XLA Ops:
  14.2 66.4 %copy-start.10 = (f32[1,64,4]{1,2,0:T(4,128)S(1)}, f32[1,64,4]{1,2,0:T(4,128)}, u32[]{:S(2)}) copy-start(f32[1,64,4]{1,2,0:T(4,128)} %param.22) | copy-start | bytes 3076
  14.2 66.4 %copy-start.11 = (f32[1,64,4]{1,2,0:T(4,128)S(1)}, f32[1,64,4]{1,2,0:T(4,128)}, u32[]{:S(2)}) copy-start(f32[1,64,4]{1,2,0:T(4,128)} %param.26) | copy-start | bytes 3076
  14.2 66.4 %copy-start.12 = (f32[1,64,4]{1,2,0:T(4,128)S(1)}, f32[1,64,4]{1,2,0:T(4,128)}, u32[]{:S(2)}) copy-start(f32[1,64,4]{1,2,0:T(4,128)} %param.30) | copy-start | bytes 3076
  60.3 1.1 %copy-start = (f32[2,768,128]{2,1,0:T(8,128)S(1)}, f32[2,768,128]{2,1,0:T(8,128)}, u32[]{:S(2)}) copy-start(f32[2,768,128]{2,1,0:T(8,128)} %shard_map.297.payload_ref) | copy-start | bytes 2359300
  61.4 19.2 %copy-start.1 = (f32[1024,64]{0,1:T(8,128)S(1)}, f32[1024,64]{0,1:T(8,128)}, u32[]{:S(2)}) copy-start(f32[1024,64]{0,1:T(8,128)} %param.23) | copy-start | bytes 786436
  61.4 19.2 %copy-start.2 = (f32[1,64,192]{2,1,0:T(8,128)S(1)}, f32[1,64,192]{2,1,0:T(8,128)}, u32[]{:S(2)}) copy-start(f32[1,64,192]{2,1,0:T(8,128)} %refs_3_.3) | copy-start | bytes 147460
  61.4 19.2 %copy-start.3 = (f32[1,2,64,64]{3,2,1,0:T(8,128)S(1)}, f32[1,2,64,64]{3,2,1,0:T(8,128)}, u32[]{:S(2)}) copy-start(f32[1,2,64,64]{3,2,1,0:T(8,128)} %refs_4_.3) | copy-start | bytes 98308
  61.4 19.2 %copy-start.4 = (f32[1024,64]{0,1:T(8,128)S(1)}, f32[1024,64]{0,1:T(8,128)}, u32[]{:S(2)}) copy-start(f32[1024,64]{0,1:T(8,128)} %param.27) | copy-start | bytes 786436
  61.4 19.2 %copy-start.5 = (f32[1024,64]{0,1:T(8,128)S(1)}, f32[1024,64]{0,1:T(8,128)}, u32[]{:S(2)}) copy-start(f32[1024,64]{0,1:T(8,128)} %param.31) | copy-start | bytes 786436
  61.5 19.2 %copy-start.6 = (f32[1,64,192]{2,1,0:T(8,128)S(1)}, f32[1,64,192]{2,1,0:T(8,128)}, u32[]{:S(2)}) copy-start(f32[1,64,192]{2,1,0:T(8,128)} %refs_7_.1) | copy-start | bytes 147460
  61.5 19.2 %copy-start.7 = (f32[1,2,64,64]{3,2,1,0:T(8,128)S(1)}, f32[1,2,64,64]{3,2,1,0:T(8,128)}, u32[]{:S(2)}) copy-start(f32[1,2,64,64]{3,2,1,0:T(8,128)} %refs_8_.1) | copy-start | bytes 98308
  61.5 19.2 %copy-start.8 = (f32[1,64,192]{2,1,0:T(8,128)S(1)}, f32[1,64,192]{2,1,0:T(8,128)}, u32[]{:S(2)}) copy-start(f32[1,64,192]{2,1,0:T(8,128)} %refs_11_.1) | copy-start | bytes 147460
  61.5 19.2 %copy-start.9 = (f32[1,2,64,64]{3,2,1,0:T(8,128)S(1)}, f32[1,2,64,64]{3,2,1,0:T(8,128)}, u32[]{:S(2)}) copy-start(f32[1,2,64,64]{3,2,1,0:T(8,128)} %refs_12_.1) | copy-start | bytes 98308

commit v7 on v6

--- a/solution.py
+++ b/solution.py
@@ -161,23 +161,22 @@
             parted = wave_ref[k, block].astype(F32)
             even_scr[block, rows] = parted[:8]
             odd_scr[block, rows] = parted[8:]
-            code_scr[block, rows] = ids_ref[k, block]
+            code_scr[block, rows] = ids_ref[k, block].astype(F32)
 
     clips = 8 * sets
 
-    def blocks_of(length):
-        valid = lax.shift_right_arithmetic(length + 1, 1)
-        return lax.shift_right_arithmetic(valid + (SPARE + LANES - 1), 7)
+    def columns_of(length):
+        return lax.shift_right_arithmetic(length + 1, 1) + SPARE
 
     def length_of(clip):
         return len_ref[jnp.bitwise_and(clip, 8), jnp.bitwise_and(clip, 7)]
 
     def add_clip(c, carry):
         length = length_of(c)
-        return carry[0] + blocks_of(length), carry[1] + length
-
-    blocks, count = lax.fori_loop(0, clips, add_clip, (jnp.int32(0), jnp.int32(0)))
-    tiles = lax.div(blocks + per_tile - 1, jnp.int32(per_tile)) + DEPTH
+        return carry[0] + columns_of(length), carry[1] + length
+
+    columns, count = lax.fori_loop(0, clips, add_clip, (jnp.int32(0), jnp.int32(0)))
+    tiles = lax.div(columns + TILE - 1, jnp.int32(TILE)) + DEPTH
 
     sub = lax.broadcasted_iota(jnp.int32, (8, LANES), 0)
     lane = lax.broadcasted_iota(jnp.int32, (8, LANES), 1)
@@ -193,33 +192,45 @@
         other = jnp.where(sub_tile == 0, later, jnp.where(sub_tile == 1, earlier, 0.0))
         return jnp.concatenate([moved(ext, 0), other], axis=0)
 
+    def rows_at(clip, place):
+        here = (jnp.minimum(place, per_clip - 1), pl.ds(jnp.minimum(clip, clips - 1), 1), slice(None))
+        even, odd, code = (
+            jnp.broadcast_to(ref[here], (8, LANES)) for ref in (even_scr, odd_scr, code_scr)
+        )
+        return jnp.where(sub == 0, even, jnp.where(sub == 1, odd, code))
+
+    def known_length(clip):
+        return jnp.where(clip < clips, length_of(clip), -frames)
+
     def fetch(state, slot):
-        clip, place = state
-        real = clip < clips
-        length = jnp.where(real, length_of(clip), -frames)
-        row = pl.ds(jnp.minimum(clip, clips - 1), 1)
-        here = (jnp.minimum(place, per_clip - 1), row, slice(None))
-        t = place * LANES + lane
+        clip, start = state
+        own, following = known_length(clip), known_length(clip + 1)
+        cut = jnp.where(clip < clips, columns_of(own), 1 << 20) - start
+        inside = lane < cut
+        t = jnp.where(inside, start + lane, lane - cut)
+        length = jnp.where(inside, own, following)
+        turn = jnp.bitwise_and(start, LANES - 1)
+        place = lax.shift_right_logical(start, 7)
+        ahead = jnp.where(lane >= turn, rows_at(clip, place), rows_at(clip, place + 1))
+        ahead = pltpu.roll(ahead, jnp.bitwise_and(LANES - turn, LANES - 1), 1)
+        after = pltpu.roll(rows_at(clip + 1, 0), jnp.bitwise_and(cut, LANES - 1), 1)
+        values = jnp.where(inside, ahead, after)
+        code = jnp.broadcast_to(values[2:3], (8, LANES)).astype(jnp.int32)
         even_ok = 2 * t < length
         odd_ok = 2 * t + 1 < length
-        even = jnp.broadcast_to(even_scr[here], (8, LANES))
-        odd = jnp.broadcast_to(odd_scr[here], (8, LANES))
-        code = jnp.broadcast_to(code_scr[here], (8, LANES))
         live = t < jnp.minimum(lax.shift_right_arithmetic(length + 1, 1) + REAL, half)
         low = jnp.where(live, jnp.bitwise_and(code, LOW - 1), -1).astype(F32)
         high = lax.shift_right_logical(code, 8).astype(F32)
-        sig_r[slot] = jnp.where(
-            (sub == 0) & even_ok, even, jnp.where((sub == 1) & odd_ok, odd, 0.0)
-        )
-        msk_r[slot] = jnp.where(((sub == 0) & even_ok) | ((sub == 1) & odd_ok), 1.0, 0.0)
+        known = ((sub == 0) & even_ok) | ((sub == 1) & odd_ok)
+        sig_r[slot] = jnp.where(known, values, 0.0)
+        msk_r[slot] = jnp.where(known, 1.0, 0.0)
         live_r[slot] = jnp.where(live, 1.0, 0.0)
         me_r[slot] = jnp.where(even_ok, 1.0, 0.0)
         low_r[slot] = stack(low, 2).astype(BF16)
         high_r[slot] = high
         hi_r[slot] = stack(high, 2).astype(BF16)
-        done = place + 1 >= blocks_of(length)
-        clip = jnp.where(done, jnp.minimum(clip + 1, clips), clip)
-        return clip, jnp.where(done, 0, place + 1)
+        done = cut <= LANES
+        return jnp.where(done, clip + 1, clip), jnp.where(done, LANES - cut, start + LANES)
 
     state = (jnp.int32(0), jnp.int32(0))
     for b in range(per_tile + 1):
@@ -520,7 +531,7 @@
             pltpu.VMEM((8, LANES), F32),
             pltpu.VMEM((per_clip, clips, LANES), F32),
             pltpu.VMEM((per_clip, clips, LANES), F32),
-            pltpu.VMEM((per_clip, clips, LANES), jnp.int32),
+            pltpu.VMEM((per_clip, clips, LANES), F32),
             *(ring(8, F32) for _ in range(4)),
             ring(16, BF16),
             ring(8, F32),
@@ -734,10 +745,11 @@
             cross_send.at[k], cross_recv.at[k], partner,
         )
 
-    @pl.loop(1, items + 1)
+    @pl.loop(1, items)
     def _(d):
         cross_copy(peer(d)).start()
 
+    cross_copy(item).start()
     load.wait()
 
     def out_copy(to, place):
@@ -763,7 +775,7 @@
     whole[item, piece:] = jnp.concatenate([message, jnp.zeros_like(message)], axis=0).astype(BF16)
 
     def take(d, total):
-        source = peer(items - d)
+        source = peer(d)
         out_copy(source, source).wait_recv()
         return total + landed[source].astype(F32)
 
@@ -790,7 +802,7 @@
     cross_copy(item).wait_send()
 
     def gather(d, stats):
-        source = peer(items - d)
+        source = peer(d)
         back_copy(source, source).wait_recv()
         sum_ref[rows_of(source)] = whole[source, :piece].astype(F32)
         return stats + whole[source, piece:].astype(F32)[:8]

time: 81.4 us -> 78.7 us (0.967); the launches traced: 82.2 us -> 78 us
  Pallas kernels: 78.8 us -> 74.7 us
    pallas_call x1, Pallas kernels: 46.1 us -> 43.9 us  [net(): pl.pallas_call(net_kernel, out_shape=jax.ShapeDtypeStruct((2, rows, LANES...]
    pallas_call x1, Pallas kernels: 19.1 us -> 17.1 us  [summed(): pl.pallas_call(functools.partial(sum_kernel, items, stats_row), out_shape...]
where the time goes in v7:
time: 78.7 us; the launch traced here: 78 us
  Pallas kernels  74.7 us (95%)
  between operations  2.14 us (3%)
  local copies, waits for them, and re-layouts  1.19 us (2%)
    pallas_call x1, Pallas kernels, net(): pl.pallas_call(net_kernel, out_shape=jax.ShapeDtypeStruct((2, rows, LANES...  43.9 us
    pallas_call x1, Pallas kernels, summed(): pl.pallas_call(functools.partial(sum_kernel, items, stats_row), out_shape...  17.1 us
    pallas_call x1, Pallas kernels, shared(): pl.pallas_call(functools.partial(share_kernel, items), out_shape=(jax.Sha...  12.2 us

profile of v7, /device:TPU:0, one launch (start us, length us, event | category | flops | bytes accessed | tf_op | source)
XLA Modules:
  0.0 78.0 jit_solution(17892138018160707750)
XLA Ops:
  1.9 12.2 %shard_map.296 = (s32[16,128]{1,0:T(8,128)}, bf16[2,16,16,128]{3,2,1,0:T(8,128)(2,1)}, s32[2,16,8,128]{3,2,1,0:T(8,128)}, bf16[2,528,256]{2,1,0:T(8,128)(2,1)}) custom-call(s32[32]{0:T(128)} %refs_0_.2, bf16[32,4096]{1,0:T(8,128)(2,1)} %refs_1_.2, s32[32,2048]{1,0:T(8,128)} %refs_2_.1, f32[1,64,192]{2,1,0:T(8,128)} %refs_3_.3, f32[1,2,64,64]{3,2,1,0:T(8,128)} %refs_4_.3, ...), custom_call_target="tpu_custom_call" | custom-call | tf_op jit(solution)/shard_map/pallas_call | solution.py:671
  14.2 0.0 copy-start.10
  14.2 0.0 copy-start.11
  14.2 0.0 copy-start.12
  14.2 43.9 %shard_map.297.payload_ref = f32[2,768,128]{2,1,0:T(8,128)} custom-call(s32[16,128]{1,0:T(8,128)} %get-tuple-element.38.len_src, bf16[2,16,16,128]{3,2,1,0:T(8,128)(2,1)} %get-tuple-element.39.wave_src, s32[2,16,8,128]{3,2,1,0:T(8,128)} %get-tuple-element.40.ids_src, bf16[2,528,256]{2,1,0:T(8,128)(2,1)} %get-tuple-element.41.weight_src), custom_call_target="tpu_custom_call" | custom-call | tf_op jit(solution)/shard_map/pallas_call | solution.py:516
  58.1 0.0 copy-start
  58.1 1.1 %copy-done = f32[2,768,128]{2,1,0:T(8,128)S(1)} copy-done((f32[2,768,128]{2,1,0:T(8,128)S(1)}, f32[2,768,128]{2,1,0:T(8,128)}, u32[]{:S(2)}) %copy-start) | copy-done | bytes 786456
  59.2 0.0 copy-start.1
  59.2 0.0 copy-start.2
  59.2 0.0 copy-start.3
  59.2 0.0 copy-start.4
  59.2 0.0 copy-start.5
  59.3 0.0 copy-start.6
  59.3 0.0 copy-start.7
  59.3 0.0 copy-start.8
  59.3 0.0 copy-start.9
  59.3 17.1 %shard_map.298.refs_2_ = f32[768,128]{1,0:T(8,128)S(1)} custom-call(f32[2,768,128]{2,1,0:T(8,128)S(1)} %copy-done), custom_call_target="tpu_custom_call" | custom-call | tf_op jit(solution)/shard_map/pallas_call | solution.py:823
  76.4 0.0 copy-done.10
  76.4 0.0 copy-done.11
  76.5 0.0 copy-done.12
  76.5 0.0 copy-done.1
  76.5 0.0 copy-done.2
  76.5 0.0 copy-done.3
  76.5 0.0 copy-done.4
  76.5 0.0 copy-done.5
  76.5 0.0 copy-done.6
  76.5 0.0 copy-done.7
  76.5 0.0 copy-done.8
  76.5 0.0 copy-done.9
  76.6 1.4 %shard_map.299 = (f32[1]{0:T(128)}, f32[1,64,192]{2,1,0:T(8,128)}, f32[1,64,192]{2,1,0:T(8,128)}, f32[1,64,192]{2,1,0:T(8,128)}, bf16[1,64,192]{2,1,0:T(8,128)(2...) custom-call(f32[1]{0:T(128)S(6)} %copy.34.refs_0_, ...), custom_call_target="tpu_custom_call" | custom-call | tf_op jit(solution)/shard_map/pallas_call | solution.py:895
Async XLA Ops:
  14.2 62.3 %copy-start.10 = (f32[1,64,4]{1,2,0:T(4,128)S(1)}, f32[1,64,4]{1,2,0:T(4,128)}, u32[]{:S(2)}) copy-start(f32[1,64,4]{1,2,0:T(4,128)} %param.22) | copy-start | bytes 3076
  14.2 62.2 %copy-start.11 = (f32[1,64,4]{1,2,0:T(4,128)S(1)}, f32[1,64,4]{1,2,0:T(4,128)}, u32[]{:S(2)}) copy-start(f32[1,64,4]{1,2,0:T(4,128)} %param.26) | copy-start | bytes 3076
  14.2 62.2 %copy-start.12 = (f32[1,64,4]{1,2,0:T(4,128)S(1)}, f32[1,64,4]{1,2,0:T(4,128)}, u32[]{:S(2)}) copy-start(f32[1,64,4]{1,2,0:T(4,128)} %param.30) | copy-start | bytes 3076
  58.1 1.1 %copy-start = (f32[2,768,128]{2,1,0:T(8,128)S(1)}, f32[2,768,128]{2,1,0:T(8,128)}, u32[]{:S(2)}) copy-start(f32[2,768,128]{2,1,0:T(8,128)} %shard_map.297.payload_ref) | copy-start | bytes 2359300
  59.2 17.2 %copy-start.1 = (f32[1024,64]{0,1:T(8,128)S(1)}, f32[1024,64]{0,1:T(8,128)}, u32[]{:S(2)}) copy-start(f32[1024,64]{0,1:T(8,128)} %param.23) | copy-start | bytes 786436
  59.2 17.2 %copy-start.2 = (f32[1,64,192]{2,1,0:T(8,128)S(1)}, f32[1,64,192]{2,1,0:T(8,128)}, u32[]{:S(2)}) copy-start(f32[1,64,192]{2,1,0:T(8,128)} %refs_3_.3) | copy-start | bytes 147460
  59.2 17.2 %copy-start.3 = (f32[1,2,64,64]{3,2,1,0:T(8,128)S(1)}, f32[1,2,64,64]{3,2,1,0:T(8,128)}, u32[]{:S(2)}) copy-start(f32[1,2,64,64]{3,2,1,0:T(8,128)} %refs_4_.3) | copy-start | bytes 98308
  59.2 17.3 %copy-start.4 = (f32[1024,64]{0,1:T(8,128)S(1)}, f32[1024,64]{0,1:T(8,128)}, u32[]{:S(2)}) copy-start(f32[1024,64]{0,1:T(8,128)} %param.27) | copy-start | bytes 786436
  59.2 17.3 %copy-start.5 = (f32[1024,64]{0,1:T(8,128)S(1)}, f32[1024,64]{0,1:T(8,128)}, u32[]{:S(2)}) copy-start(f32[1024,64]{0,1:T(8,128)} %param.31) | copy-start | bytes 786436
  59.3 17.3 %copy-start.6 = (f32[1,64,192]{2,1,0:T(8,128)S(1)}, f32[1,64,192]{2,1,0:T(8,128)}, u32[]{:S(2)}) copy-start(f32[1,64,192]{2,1,0:T(8,128)} %refs_7_.1) | copy-start | bytes 147460
  59.3 17.3 %copy-start.7 = (f32[1,2,64,64]{3,2,1,0:T(8,128)S(1)}, f32[1,2,64,64]{3,2,1,0:T(8,128)}, u32[]{:S(2)}) copy-start(f32[1,2,64,64]{3,2,1,0:T(8,128)} %refs_8_.1) | copy-start | bytes 98308
  59.3 17.2 %copy-start.8 = (f32[1,64,192]{2,1,0:T(8,128)S(1)}, f32[1,64,192]{2,1,0:T(8,128)}, u32[]{:S(2)}) copy-start(f32[1,64,192]{2,1,0:T(8,128)} %refs_11_.1) | copy-start | bytes 147460
  59.3 17.2 %copy-start.9 = (f32[1,2,64,64]{3,2,1,0:T(8,128)S(1)}, f32[1,2,64,64]{3,2,1,0:T(8,128)}, u32[]{:S(2)}) copy-start(f32[1,2,64,64]{3,2,1,0:T(8,128)} %refs_12_.1) | copy-start | bytes 98308

commit v8 on v7

--- a/solution.py
+++ b/solution.py
@@ -448,8 +448,11 @@
         return state
 
     ranges = (
-        ((0, 1, 2, 3), 0, HEAD),
-        (range(8), HEAD, tiles - 2),
+        ((0, 1), 0, 1),
+        ((0, 1, 2, 3), 1, HEAD),
+        (range(8), HEAD, tiles - 4),
+        (range(2, 8), tiles - 4, tiles - 3),
+        (range(4, 8), tiles - 3, tiles - 2),
         ((6, 7), tiles - 2, tiles - 1),
         ((7,), tiles - 1, tiles),
     )

time: 78.7 us -> 78.4 us (level)
  no operation moved by 1% of the time
where the time goes in v8:
time: 78.4 us; the launch traced here: 78.2 us
  Pallas kernels  74.9 us (96%)
  between operations  2.14 us (3%)
  local copies, waits for them, and re-layouts  1.19 us (2%)
    pallas_call x1, Pallas kernels, net(): pl.pallas_call(net_kernel, out_shape=jax.ShapeDtypeStruct((2, rows, LANES...  44.1 us
    pallas_call x1, Pallas kernels, summed(): pl.pallas_call(functools.partial(sum_kernel, items, stats_row), out_shape...  17.2 us
    pallas_call x1, Pallas kernels, shared(): pl.pallas_call(functools.partial(share_kernel, items), out_shape=(jax.Sha...  12.2 us

profile of v8, /device:TPU:0, one launch (start us, length us, event | category | flops | bytes accessed | tf_op | source)
XLA Modules:
  0.0 78.2 jit_solution(11805242109974208171)
XLA Ops:
  1.9 12.2 %shard_map.296 = (s32[16,128]{1,0:T(8,128)}, bf16[2,16,16,128]{3,2,1,0:T(8,128)(2,1)}, s32[2,16,8,128]{3,2,1,0:T(8,128)}, bf16[2,528,256]{2,1,0:T(8,128)(2,1)}) custom-call(s32[32]{0:T(128)} %refs_0_.2, bf16[32,4096]{1,0:T(8,128)(2,1)} %refs_1_.2, s32[32,2048]{1,0:T(8,128)} %refs_2_.1, f32[1,64,192]{2,1,0:T(8,128)} %refs_3_.3, f32[1,2,64,64]{3,2,1,0:T(8,128)} %refs_4_.3, ...), custom_call_target="tpu_custom_call" | custom-call | tf_op jit(solution)/shard_map/pallas_call | solution.py:674
  14.2 0.0 copy-start.10
  14.2 0.0 copy-start.11
  14.2 0.0 copy-start.12
  14.2 44.1 %shard_map.297.payload_ref = f32[2,768,128]{2,1,0:T(8,128)} custom-call(s32[16,128]{1,0:T(8,128)} %get-tuple-element.38.len_src, bf16[2,16,16,128]{3,2,1,0:T(8,128)(2,1)} %get-tuple-element.39.wave_src, s32[2,16,8,128]{3,2,1,0:T(8,128)} %get-tuple-element.40.ids_src, bf16[2,528,256]{2,1,0:T(8,128)(2,1)} %get-tuple-element.41.weight_src), custom_call_target="tpu_custom_call" | custom-call | tf_op jit(solution)/shard_map/pallas_call | solution.py:519
  58.3 0.0 copy-start
  58.3 1.1 %copy-done = f32[2,768,128]{2,1,0:T(8,128)S(1)} copy-done((f32[2,768,128]{2,1,0:T(8,128)S(1)}, f32[2,768,128]{2,1,0:T(8,128)}, u32[]{:S(2)}) %copy-start) | copy-done | bytes 786456
  59.4 0.0 copy-start.1
  59.4 0.0 copy-start.2
  59.4 0.0 copy-start.3
  59.4 0.0 copy-start.4
  59.4 0.0 copy-start.5
  59.4 0.0 copy-start.6
  59.5 0.0 copy-start.7
  59.5 0.0 copy-start.8
  59.5 0.0 copy-start.9
  59.5 17.2 %shard_map.298.refs_2_ = f32[768,128]{1,0:T(8,128)S(1)} custom-call(f32[2,768,128]{2,1,0:T(8,128)S(1)} %copy-done), custom_call_target="tpu_custom_call" | custom-call | tf_op jit(solution)/shard_map/pallas_call | solution.py:826
  76.7 0.0 copy-done.10
  76.7 0.0 copy-done.11
  76.7 0.0 copy-done.12
  76.7 0.0 copy-done.1
  76.7 0.0 copy-done.2
  76.7 0.0 copy-done.3
  76.7 0.0 copy-done.4
  76.8 0.0 copy-done.5
  76.8 0.0 copy-done.6
  76.8 0.0 copy-done.7
  76.8 0.0 copy-done.8
  76.8 0.0 copy-done.9
  76.8 1.4 %shard_map.299 = (f32[1]{0:T(128)}, f32[1,64,192]{2,1,0:T(8,128)}, f32[1,64,192]{2,1,0:T(8,128)}, f32[1,64,192]{2,1,0:T(8,128)}, bf16[1,64,192]{2,1,0:T(8,128)(2...) custom-call(f32[1]{0:T(128)S(6)} %copy.34.refs_0_, ...), custom_call_target="tpu_custom_call" | custom-call | tf_op jit(solution)/shard_map/pallas_call | solution.py:898
Async XLA Ops:
  14.2 62.5 %copy-start.10 = (f32[1,64,4]{1,2,0:T(4,128)S(1)}, f32[1,64,4]{1,2,0:T(4,128)}, u32[]{:S(2)}) copy-start(f32[1,64,4]{1,2,0:T(4,128)} %param.22) | copy-start | bytes 3076
  14.2 62.5 %copy-start.11 = (f32[1,64,4]{1,2,0:T(4,128)S(1)}, f32[1,64,4]{1,2,0:T(4,128)}, u32[]{:S(2)}) copy-start(f32[1,64,4]{1,2,0:T(4,128)} %param.26) | copy-start | bytes 3076
  14.2 62.5 %copy-start.12 = (f32[1,64,4]{1,2,0:T(4,128)S(1)}, f32[1,64,4]{1,2,0:T(4,128)}, u32[]{:S(2)}) copy-start(f32[1,64,4]{1,2,0:T(4,128)} %param.30) | copy-start | bytes 3076
  58.3 1.1 %copy-start = (f32[2,768,128]{2,1,0:T(8,128)S(1)}, f32[2,768,128]{2,1,0:T(8,128)}, u32[]{:S(2)}) copy-start(f32[2,768,128]{2,1,0:T(8,128)} %shard_map.297.payload_ref) | copy-start | bytes 2359300
  59.4 17.3 %copy-start.1 = (f32[1024,64]{0,1:T(8,128)S(1)}, f32[1024,64]{0,1:T(8,128)}, u32[]{:S(2)}) copy-start(f32[1024,64]{0,1:T(8,128)} %param.23) | copy-start | bytes 786436
  59.4 17.3 %copy-start.2 = (f32[1,64,192]{2,1,0:T(8,128)S(1)}, f32[1,64,192]{2,1,0:T(8,128)}, u32[]{:S(2)}) copy-start(f32[1,64,192]{2,1,0:T(8,128)} %refs_3_.3) | copy-start | bytes 147460
  59.4 17.3 %copy-start.3 = (f32[1,2,64,64]{3,2,1,0:T(8,128)S(1)}, f32[1,2,64,64]{3,2,1,0:T(8,128)}, u32[]{:S(2)}) copy-start(f32[1,2,64,64]{3,2,1,0:T(8,128)} %refs_4_.3) | copy-start | bytes 98308
  59.4 17.3 %copy-start.4 = (f32[1024,64]{0,1:T(8,128)S(1)}, f32[1024,64]{0,1:T(8,128)}, u32[]{:S(2)}) copy-start(f32[1024,64]{0,1:T(8,128)} %param.27) | copy-start | bytes 786436
  59.4 17.3 %copy-start.5 = (f32[1024,64]{0,1:T(8,128)S(1)}, f32[1024,64]{0,1:T(8,128)}, u32[]{:S(2)}) copy-start(f32[1024,64]{0,1:T(8,128)} %param.31) | copy-start | bytes 786436
  59.4 17.3 %copy-start.6 = (f32[1,64,192]{2,1,0:T(8,128)S(1)}, f32[1,64,192]{2,1,0:T(8,128)}, u32[]{:S(2)}) copy-start(f32[1,64,192]{2,1,0:T(8,128)} %refs_7_.1) | copy-start | bytes 147460
  59.5 17.3 %copy-start.7 = (f32[1,2,64,64]{3,2,1,0:T(8,128)S(1)}, f32[1,2,64,64]{3,2,1,0:T(8,128)}, u32[]{:S(2)}) copy-start(f32[1,2,64,64]{3,2,1,0:T(8,128)} %refs_8_.1) | copy-start | bytes 98308
  59.5 17.3 %copy-start.8 = (f32[1,64,192]{2,1,0:T(8,128)S(1)}, f32[1,64,192]{2,1,0:T(8,128)}, u32[]{:S(2)}) copy-start(f32[1,64,192]{2,1,0:T(8,128)} %refs_11_.1) | copy-start | bytes 147460
  59.5 17.3 %copy-start.9 = (f32[1,2,64,64]{3,2,1,0:T(8,128)S(1)}, f32[1,2,64,64]{3,2,1,0:T(8,128)}, u32[]{:S(2)}) copy-start(f32[1,2,64,64]{3,2,1,0:T(8,128)} %refs_12_.1) | copy-start | bytes 98308

commit v9 on v8

--- a/solution.py
+++ b/solution.py
@@ -726,7 +726,10 @@
     def peer(d):
         if items & (items - 1):
             return lax.rem(item + d, items)
-        return jnp.bitwise_and(item + d, items - 1)
+        return jnp.bitwise_xor(item, items - d)
+
+    def peer_back(d):
+        return lax.rem(item + d, items)
 
     def rows_of(k):
         return pl.ds(pl.multiple_of(k * piece, piece), piece)
@@ -792,7 +795,7 @@
 
     @pl.loop(1, items)
     def _(d):
-        back_copy(item, peer(d)).start()
+        back_copy(item, peer_back(d)).start()
 
     sum_ref[rows_of(item)] = whole[item, :piece].astype(F32)
 
@@ -805,7 +808,7 @@
     cross_copy(item).wait_send()
 
     def gather(d, stats):
-        source = peer(d)
+        source = peer_back(d)
         back_copy(source, source).wait_recv()
         sum_ref[rows_of(source)] = whole[source, :piece].astype(F32)
         return stats + whole[source, piece:].astype(F32)[:8]

time: 78.4 us -> 77.3 us (0.986)
  Pallas kernels: 74.9 us -> 73.9 us
    pallas_call x1, Pallas kernels: 44.1 us -> 41.2 us  [net(): pl.pallas_call(net_kernel, out_shape=jax.ShapeDtypeStruct((2, rows, LANES...]
    pallas_call x1, Pallas kernels: 17.2 us -> 19.1 us  [summed(): pl.pallas_call(functools.partial(sum_kernel, items, stats_row), out_shape...]
where the time goes in v9:
time: 77.3 us; the launch traced here: 77.2 us
  Pallas kernels  73.9 us (96%)
  between operations  2.14 us (3%)
  local copies, waits for them, and re-layouts  1.19 us (2%)
    pallas_call x1, Pallas kernels, net(): pl.pallas_call(net_kernel, out_shape=jax.ShapeDtypeStruct((2, rows, LANES...  41.2 us
    pallas_call x1, Pallas kernels, summed(): pl.pallas_call(functools.partial(sum_kernel, items, stats_row), out_shape...  19.1 us
    pallas_call x1, Pallas kernels, shared(): pl.pallas_call(functools.partial(share_kernel, items), out_shape=(jax.Sha...  12.2 us

profile of v9, /device:TPU:0, one launch (start us, length us, event | category | flops | bytes accessed | tf_op | source)
XLA Modules:
  0.0 77.2 jit_solution(3902300866012874649)
XLA Ops:
  1.9 12.2 %shard_map.296 = (s32[16,128]{1,0:T(8,128)}, bf16[2,16,16,128]{3,2,1,0:T(8,128)(2,1)}, s32[2,16,8,128]{3,2,1,0:T(8,128)}, bf16[2,528,256]{2,1,0:T(8,128)(2,1)}) custom-call(s32[32]{0:T(128)} %refs_0_.2, bf16[32,4096]{1,0:T(8,128)(2,1)} %refs_1_.2, s32[32,2048]{1,0:T(8,128)} %refs_2_.1, f32[1,64,192]{2,1,0:T(8,128)} %refs_3_.3, f32[1,2,64,64]{3,2,1,0:T(8,128)} %refs_4_.3, ...), custom_call_target="tpu_custom_call" | custom-call | tf_op jit(solution)/shard_map/pallas_call | solution.py:674
  14.2 0.0 copy-start.10
  14.2 0.0 copy-start.11
  14.2 0.0 copy-start.12
  14.2 41.2 %shard_map.297.payload_ref = f32[2,768,128]{2,1,0:T(8,128)} custom-call(s32[16,128]{1,0:T(8,128)} %get-tuple-element.38.len_src, bf16[2,16,16,128]{3,2,1,0:T(8,128)(2,1)} %get-tuple-element.39.wave_src, s32[2,16,8,128]{3,2,1,0:T(8,128)} %get-tuple-element.40.ids_src, bf16[2,528,256]{2,1,0:T(8,128)(2,1)} %get-tuple-element.41.weight_src), custom_call_target="tpu_custom_call" | custom-call | tf_op jit(solution)/shard_map/pallas_call | solution.py:519
  55.4 0.0 copy-start
  55.4 1.1 %copy-done = f32[2,768,128]{2,1,0:T(8,128)S(1)} copy-done((f32[2,768,128]{2,1,0:T(8,128)S(1)}, f32[2,768,128]{2,1,0:T(8,128)}, u32[]{:S(2)}) %copy-start) | copy-done | bytes 786456
  56.5 0.0 copy-start.1
  56.5 0.0 copy-start.2
  56.5 0.0 copy-start.3
  56.5 0.0 copy-start.4
  56.5 0.0 copy-start.5
  56.5 0.0 copy-start.6
  56.6 0.0 copy-start.7
  56.6 0.0 copy-start.8
  56.6 0.0 copy-start.9
  56.6 19.1 %shard_map.298.refs_2_ = f32[768,128]{1,0:T(8,128)S(1)} custom-call(f32[2,768,128]{2,1,0:T(8,128)S(1)} %copy-done), custom_call_target="tpu_custom_call" | custom-call | tf_op jit(solution)/shard_map/pallas_call | solution.py:829
  75.7 0.0 copy-done.10
  75.7 0.0 copy-done.11
  75.7 0.0 copy-done.12
  75.7 0.0 copy-done.1
  75.7 0.0 copy-done.2
  75.7 0.0 copy-done.3
  75.7 0.0 copy-done.4
  75.7 0.0 copy-done.5
  75.7 0.0 copy-done.6
  75.8 0.0 copy-done.7
  75.8 0.0 copy-done.8
  75.8 0.0 copy-done.9
  75.8 1.4 %shard_map.299 = (f32[1]{0:T(128)}, f32[1,64,192]{2,1,0:T(8,128)}, f32[1,64,192]{2,1,0:T(8,128)}, f32[1,64,192]{2,1,0:T(8,128)}, bf16[1,64,192]{2,1,0:T(8,128)(2...) custom-call(f32[1]{0:T(128)S(6)} %copy.34.refs_0_, ...), custom_call_target="tpu_custom_call" | custom-call | tf_op jit(solution)/shard_map/pallas_call | solution.py:901
Async XLA Ops:
  14.2 61.5 %copy-start.10 = (f32[1,64,4]{1,2,0:T(4,128)S(1)}, f32[1,64,4]{1,2,0:T(4,128)}, u32[]{:S(2)}) copy-start(f32[1,64,4]{1,2,0:T(4,128)} %param.22) | copy-start | bytes 3076
  14.2 61.5 %copy-start.11 = (f32[1,64,4]{1,2,0:T(4,128)S(1)}, f32[1,64,4]{1,2,0:T(4,128)}, u32[]{:S(2)}) copy-start(f32[1,64,4]{1,2,0:T(4,128)} %param.26) | copy-start | bytes 3076
  14.2 61.5 %copy-start.12 = (f32[1,64,4]{1,2,0:T(4,128)S(1)}, f32[1,64,4]{1,2,0:T(4,128)}, u32[]{:S(2)}) copy-start(f32[1,64,4]{1,2,0:T(4,128)} %param.30) | copy-start | bytes 3076
  55.4 1.1 %copy-start = (f32[2,768,128]{2,1,0:T(8,128)S(1)}, f32[2,768,128]{2,1,0:T(8,128)}, u32[]{:S(2)}) copy-start(f32[2,768,128]{2,1,0:T(8,128)} %shard_map.297.payload_ref) | copy-start | bytes 2359300
  56.5 19.2 %copy-start.1 = (f32[1024,64]{0,1:T(8,128)S(1)}, f32[1024,64]{0,1:T(8,128)}, u32[]{:S(2)}) copy-start(f32[1024,64]{0,1:T(8,128)} %param.23) | copy-start | bytes 786436
  56.5 19.2 %copy-start.2 = (f32[1,64,192]{2,1,0:T(8,128)S(1)}, f32[1,64,192]{2,1,0:T(8,128)}, u32[]{:S(2)}) copy-start(f32[1,64,192]{2,1,0:T(8,128)} %refs_3_.3) | copy-start | bytes 147460
  56.5 19.2 %copy-start.3 = (f32[1,2,64,64]{3,2,1,0:T(8,128)S(1)}, f32[1,2,64,64]{3,2,1,0:T(8,128)}, u32[]{:S(2)}) copy-start(f32[1,2,64,64]{3,2,1,0:T(8,128)} %refs_4_.3) | copy-start | bytes 98308
  56.5 19.2 %copy-start.4 = (f32[1024,64]{0,1:T(8,128)S(1)}, f32[1024,64]{0,1:T(8,128)}, u32[]{:S(2)}) copy-start(f32[1024,64]{0,1:T(8,128)} %param.27) | copy-start | bytes 786436
  56.5 19.2 %copy-start.5 = (f32[1024,64]{0,1:T(8,128)S(1)}, f32[1024,64]{0,1:T(8,128)}, u32[]{:S(2)}) copy-start(f32[1024,64]{0,1:T(8,128)} %param.31) | copy-start | bytes 786436
  56.5 19.2 %copy-start.6 = (f32[1,64,192]{2,1,0:T(8,128)S(1)}, f32[1,64,192]{2,1,0:T(8,128)}, u32[]{:S(2)}) copy-start(f32[1,64,192]{2,1,0:T(8,128)} %refs_7_.1) | copy-start | bytes 147460
  56.6 19.2 %copy-start.7 = (f32[1,2,64,64]{3,2,1,0:T(8,128)S(1)}, f32[1,2,64,64]{3,2,1,0:T(8,128)}, u32[]{:S(2)}) copy-start(f32[1,2,64,64]{3,2,1,0:T(8,128)} %refs_8_.1) | copy-start | bytes 98308
  56.6 19.2 %copy-start.8 = (f32[1,64,192]{2,1,0:T(8,128)S(1)}, f32[1,64,192]{2,1,0:T(8,128)}, u32[]{:S(2)}) copy-start(f32[1,64,192]{2,1,0:T(8,128)} %refs_11_.1) | copy-start | bytes 147460
  56.6 19.2 %copy-start.9 = (f32[1,2,64,64]{3,2,1,0:T(8,128)S(1)}, f32[1,2,64,64]{3,2,1,0:T(8,128)}, u32[]{:S(2)}) copy-start(f32[1,2,64,64]{3,2,1,0:T(8,128)} %refs_12_.1) | copy-start | bytes 98308
